TPU v7x, 256 devices: a whole 4x4x8 slice. The times are simulated.
256 devices in a mesh: rep: 16 (over y_hi, x, core), node: 8 (over z), tp: 2 (over y_lo).
Axes of the slice: x: 4, y: 4 (y_hi: 2, y_lo: 2; y = y_hi * 2 + y_lo), z: 8, core: 2. Of those that a mesh axis runs over, the one named last changes fastest.
Arguments:
- hidden_states: bfloat16 [32768, 8192], P(('rep', 'node'), 'tp'), may hold values from -134 to 134
- norm_gain: bfloat16 [8192], P('tp'), may hold values from 0.5 to 1.5
- value_weight: bfloat16 [8192, 512], P(('rep', 'node'), 'tp'), may hold values from -0.0625 to 0.0625
- queries: bfloat16 [32768, 4096], P(('rep', 'node'), 'tp'), may hold values from -88 to 88
- keys: bfloat16 [32768, 512], P(('rep', 'node'), 'tp'), may hold values from -4.4 to 4.4
- readout: float32 [4096], P('tp'), may hold values from -1.5 to 1.5
- targets: float32 [32768], P(('rep', 'node')), may hold values from -4 to 4
- scored: int32 [32768], P(('rep', 'node')), may hold values 0 or 1
Outputs:
- values: float32 [32768], P(('rep', 'node'))
- grad_input: bfloat16 [32768, 8192], P(('rep', 'node'), 'tp')
- grad_weight: float32 [8192, 512], P(('rep', 'node'), 'tp')
- grad_gain: float32 [8192], P('tp')
- grad_readout: float32 [4096], P('tp')
- grad_log_scale: float32 [32768], P(('rep', 'node'))
All inputs are finite; a program needn't handle non-finite values. No bound on the sum of `scored` on one device may be relied on, other than what follows from the above.
Results may differ from a plain program's by a relative error of at most 0.015.
Values may be sent and summed in bfloat16 or wider, within the bound.
No kernel may reach another device: no remote copies, remote signals or barrier semaphores. Data moves between devices by JAX's collectives and lax.ppermute only.
A program may use at most 128 MiB of HBM per device.

v0:
```python
import math

import jax
import jax.numpy as jnp
from jax import lax
from jax.sharding import PartitionSpec as P

HD = 128
GROUP = 8


EPS = 1e-06


def reduce_weight(term_fn, rows):
    return lax.psum_scatter(
        term_fn(jnp.int32(0), rows * lax.axis_size(("rep", "node"))),
        ("rep", "node"),
        scatter_dimension=0,
        tiled=True,
    )


def shards(hidden_states, norm_gain, value_weight, queries, keys, readout, targets, scored):
    f32 = jnp.float32
    length = hidden_states.shape[0]
    width = hidden_states.shape[1] * lax.axis_size("tp")
    x_share = hidden_states.astype(f32)
    gain_share = norm_gain.astype(f32)
    columns = value_weight.shape[1]
    rows_local = value_weight.shape[0]
    full, gain_full = (
        lax.all_gather(hidden_states, "tp", axis=1, tiled=True),
        lax.all_gather(norm_gain, "tp", axis=0, tiled=True),
    )
    xf = full.astype(f32)
    rms_inv = lax.rsqrt(jnp.mean(xf * xf, axis=1, keepdims=True) + EPS)
    normed = (xf * rms_inv * gain_full.astype(f32)).astype(jnp.bfloat16)
    projected = jnp.dot(
        normed,
        lax.all_gather(value_weight, ("rep", "node"), axis=0, tiled=True),
        preferred_element_type=f32,
    )
    head_values = projected.astype(jnp.bfloat16)
    kv_local = keys.shape[1] // HD
    q4 = queries.reshape(length, kv_local, GROUP, HD)
    k3 = keys.reshape(length, kv_local, HD)
    v3 = head_values.reshape(length, kv_local, HD)
    read4 = readout.reshape(kv_local, GROUP, HD)
    positions = jnp.arange(length)
    allowed = positions[None, :] <= positions[:, None]
    scores = jnp.einsum("tkgd,skd->kgts", q4, k3, preferred_element_type=f32) / math.sqrt(HD)
    scores = jnp.where(allowed, scores, -1e30)
    top = jnp.max(scores, axis=-1, keepdims=True)
    weights = jnp.exp(scores - top)
    probs = (weights / jnp.sum(weights, axis=-1, keepdims=True)).astype(jnp.bfloat16)
    attended = jnp.einsum("kgts,skd->tkgd", probs, v3, preferred_element_type=f32)
    partial_value = jnp.sum(attended * read4[None], axis=(1, 2, 3))
    values = lax.psum(partial_value, "tp")
    error = (values - targets) * scored.astype(f32)
    grad_att = (error[:, None, None, None] * read4[None]).astype(jnp.bfloat16)
    grad_hv = jnp.einsum("kgts,tkgd->skd", probs, grad_att, preferred_element_type=f32)
    grad_hv = grad_hv.astype(jnp.bfloat16).reshape(length, columns)
    readout_part = jnp.sum(error[:, None, None, None] * attended, axis=0).reshape(-1)

    def weight_term(start, count):
        return lax.dot_general(
            normed, grad_hv, (((0,), (0,)), ((), ())), preferred_element_type=f32
        )

    grad_weight = reduce_weight(weight_term, rows_local)
    grad_normed = lax.dot_general(
        grad_hv,
        lax.all_gather(value_weight, ("rep", "node"), axis=0, tiled=True),
        (((1,), (1,)), ((), ())),
        preferred_element_type=f32,
    )
    grad_share = lax.psum_scatter(
        grad_normed.astype(jnp.bfloat16), "tp", scatter_dimension=1, tiled=True
    ).astype(jnp.float32)
    scaled = grad_share * gain_share
    dot_part = jnp.sum(scaled * x_share, axis=1)
    total_dot = lax.psum(dot_part, "tp")
    log_scale = rms_inv[:, 0] * total_dot
    grad_input = (
        rms_inv * scaled - x_share * rms_inv * rms_inv * rms_inv * total_dot[:, None] / width
    ).astype(jnp.bfloat16)
    gain_part = jnp.sum(grad_share * x_share * rms_inv, axis=0)
    grad_gain, grad_readout = lax.psum((gain_part, readout_part), ("rep", "node"))
    return (values, grad_input, grad_weight, grad_gain, grad_readout, log_scale)


def solution(mesh):
    return jax.shard_map(
        shards,
        mesh=mesh,
        in_specs=(
            P(("rep", "node"), "tp"),
            P("tp"),
            P(("rep", "node"), "tp"),
            P(("rep", "node"), "tp"),
            P(("rep", "node"), "tp"),
            P("tp"),
            P(("rep", "node")),
            P(("rep", "node")),
        ),
        out_specs=(
            P(("rep", "node")),
            P(("rep", "node"), "tp"),
            P(("rep", "node"), "tp"),
            P("tp"),
            P("tp"),
            P(("rep", "node")),
        ),
        check_vma=False,
    )
```

profile of v0, /device:TPU:32, one launch (start us, length us, event | category | flops | bytes accessed | tf_op | source)
XLA Modules:
  0.0 953.5 jit_solution(2692618285149122347)
XLA Ops:
  7.2 0.0 copy-start.1
  7.2 0.0 all-gather.3.cloned.1.call-start
  7.2 0.7 all-gather.3.cloned.1.call-update
  7.9 0.0 all-gather.5.cloned.1.call-start
  8.0 0.7 all-gather.5.cloned.1.call-update
  8.7 0.0 reduce-scatter.3.cloned.1.call-start
  8.7 4.6 all_gather.11
  13.3 1.4 copy.29
  14.7 0.0 copy-done.1
  14.8 0.7 fusion.28
  15.6 1.2 fusion.36
  16.8 0.4 divide_convert_fusion
  17.2 57.1 %all-gather.3.cloned.1.call-done = bf16[256,8192]{1,0:T(8,128)(2,1)} async-done(((bf16[256,4096]{1,0:T(8,128)(2,1)}), bf16[256,8192]{1,0:T(8,128)(2,1)}) %all-gather.3.cloned.1.call-update) | async-done | bytes 4194320 | tf_op jit(solution)/shard_map/all_gather | solution.py:33
  74.3 3.1 fusion.1
  77.4 0.0 copy-start.3
  77.4 119.9 %all-gather.5.cloned.1.call-done = bf16[8192,256]{1,0:T(8,128)(2,1)} async-done(((bf16[64,256]{1,0:T(8,128)(2,1)}), bf16[8192,256]{1,0:T(8,128)(2,1)}) %all-gather.5.cloned.1.call-update) | async-done | bytes 4194320 | tf_op jit(solution)/shard_map/all_gather | solution.py:41
  197.3 5.6 fusion.25
  202.9 0.0 copy-start.5
  202.9 0.0 copy-start.6
  203.0 0.0 copy-done.3
  203.0 1.8 fusion.15
  204.8 4.9 psum.28
  209.7 0.0 copy-done.5
  209.7 0.0 copy-done.6
  209.7 0.0 copy-start.4
  209.7 0.8 fusion.24
  210.5 5.5 convolution_convert_fusion
  216.0 0.0 copy-done.4
  216.0 0.0 reduce-scatter.3.cloned.1.call-update
  216.0 0.2 reduce-scatter.5.cloned.1.call-start
  216.3 7.1 fusion.20
  223.3 0.0 copy-start.2
  223.3 0.0 copy-start
  223.3 0.0 reduce-scatter.5.cloned.1.call-update
  223.4 0.7 copy-done.2
  224.0 2.5 fusion.16
  226.5 46.5 %reduce-scatter.3.cloned.1.call-done = bf16[256,4096]{1,0:T(8,128)(2,1)} async-done(((bf16[256,8192]{1,0:T(8,128)(2,1)}), bf16[256,4096]{1,0:T(8,128)(2,1)}) %reduce-scatter.3.cloned.1.call-update) | async-done | bytes 2097168 | tf_op jit(solution)/shard_map/reduce_scatter | solution.py:78
  273.0 0.0 copy-done
  273.0 4.1 fusion.13
  277.1 4.9 psum.29
  282.0 644.4 %all-reduce = (f32[4096]{0:T(1024)}, f32[2048]{0:T(1024)}) all-reduce(f32[4096]{0:T(1024)S(1)} %get-tuple-element.6, f32[2048]{0:T(1024)S(1)} %bitcast.50), channel_id=1, replica_groups=mesh['rep'=16,'node'=8,'tp'=2] {'rep','node'}, use_global_device_ids=true, to_apply=%region_10.11 | all-reduce | flops 6144 | bytes 49152 | tf_op jit(solution)/shard_map/psum | solution.py:89
  926.4 0.6 fusion.35
  927.0 4.5 fusion.6
  931.5 15.4 %reduce-scatter.5.cloned.1.call-done = f32[64,256]{1,0:T(8,128)} async-done(((f32[8192,256]{1,0:T(8,128)}), f32[64,256]{1,0:T(8,128)}) %reduce-scatter.5.cloned.1.call-update) | async-done | bytes 65552 | tf_op jit(solution)/shard_map/reduce_scatter | solution.py:16
  (6 shorter events, 0.1 us)
Async XLA Ops:
  7.2 7.6 copy-start.1
  7.2 67.1 %all-gather.3.cloned.1.call-start = ((), (), s32[]{:S(2)}) async-start(), calls=%async_computation.2 | async-start | bytes 6291456 | tf_op jit(solution)/shard_map/all_gather | solution.py:33
  7.9 189.4 %all-gather.5.cloned.1.call-start = ((), (), s32[]{:S(2)}) async-start(), calls=%async_computation.3 | async-start | bytes 4227072 | tf_op jit(solution)/shard_map/all_gather | solution.py:41
  8.7 264.3 %reduce-scatter.3.cloned.1.call-start = ((), (), s32[]{:S(2)}) async-start(), calls=%async_computation.4 | async-start | bytes 6291456 | tf_op jit(solution)/shard_map/reduce_scatter | solution.py:78
  77.4 125.6 %copy-start.3 = (f32[2048]{0:T(1024)S(1)}, f32[2048]{0:T(1024)}, u32[]{:S(2)}) copy-start(f32[2048]{0:T(1024)} %param.13) | copy-start | bytes 24580
  202.9 6.8 copy-start.5
  202.9 6.7 copy-start.6
  209.7 6.3 copy-start.4
  216.0 730.9 %reduce-scatter.5.cloned.1.call-start = ((), (), s32[]{:S(2)}) async-start(), calls=%async_computation.5 | async-start | bytes 8454144 | tf_op jit(solution)/shard_map/reduce_scatter | solution.py:16
  223.3 0.7 copy-start.2
  223.3 49.6 %copy-start = (bf16[256,4096]{1,0:T(8,128)(2,1)S(1)}, bf16[256,4096]{1,0:T(8,128)(2,1)}, u32[]{:S(2)}) copy-start(bf16[256,4096]{1,0:T(8,128)(2,1)} %param.8) | copy-start | bytes 6291460
Sparse Core Ops, SparseCore 0:
  9.8 64.4 all-gather.2
  78.2 119.1 all-gather.4
  216.1 56.7 reduce-scatter.2
  276.1 670.8 reduce-scatter.4
where the time goes:
time: 958 us; the launch traced here: 953 us
  blocking collectives  659 us (69%)
  waiting for transfers between devices  240 us (25%)
  matrix products  21.5 us (2%)
  other arithmetic  16.5 us (2%)
  between operations  13.9 us (1%)
    psum x1, blocking collectives, shards(): lax.psum((gain_part, readout_part), ('rep', 'node'))  644 us
    all_gather x1, waiting for transfers between devices, shards(): lax.all_gather(value_weight, ('rep', 'node'), axis=0, tiled=True)  120 us
    all_gather x1, waiting for transfers between devices, shards(): lax.all_gather(hidden_states, 'tp', axis=1, tiled=True)  57.1 us
    reduce_scatter x1, waiting for transfers between devices, shards(): lax.psum_scatter(grad_normed.astype(jnp.bfloat16), 'tp', scatter_dimensio...  46.5 us
  transfers between devices with their start and end apart: 4, of which 4 were waited for; matrix products, arithmetic and copies ran while one was open for 3% of the time, Pallas kernels for 0%

commit v1 on v0

v1 whole, which is shorter than its diff:
```python
import jax
import jax.numpy as jnp
from jax import lax
from jax.experimental import pallas as pl
from jax.experimental.pallas import tpu as pltpu
from jax.sharding import Mesh
from jax.sharding import PartitionSpec as P

HD = 128
GROUP = 8
EPS = 1e-06
F32 = jnp.float32
BF16 = jnp.bfloat16
HIGHEST = lax.Precision.HIGHEST
VMEM = pl.BlockSpec(memory_space=pltpu.VMEM)
PARAMS = pltpu.CompilerParams(vmem_limit_bytes=48 * 1024 * 1024)


def swap(v, axis, to):
    return lax.ppermute(v, axis, [(i, to(i)) for i in range(lax.axis_size(axis))])


def next_door(i):
    return i ^ 1


def two_off(i):
    return i ^ 2


def mirror_four(i):
    return 3 - i


def mirror_eight(i):
    return 7 - i


def cross(v):
    return lax.ppermute(v, ("yh", "yl"), [(0, 0), (1, 2), (2, 1), (3, 3)])


def split(bit, v, axis):
    n = v.shape[axis] // 2
    low = lax.slice_in_dim(v, 0, n, axis=axis)
    high = lax.slice_in_dim(v, n, 2 * n, axis=axis)
    return jnp.where(bit, high, low), jnp.where(bit, low, high)


def row_sum_of_transpose(a):
    return jnp.sum(a.T, axis=0, keepdims=True)


def probs_kernel(q_ref, k_ref, x_ref, p_ref, ss_ref, acc):
    step = pl.program_id(0)
    length = q_ref.shape[0]
    rows = lax.broadcasted_iota(jnp.int32, (length, length), 0)
    cols = lax.broadcasted_iota(jnp.int32, (length, length), 1)
    allowed = cols <= rows
    k = k_ref[...]
    for h in range(q_ref.shape[1] // HD):
        s = lax.dot_general(
            q_ref[:, h * HD : (h + 1) * HD], k, (((1,), (1,)), ((), ())), preferred_element_type=F32
        )
        s = jnp.where(allowed, s * (HD**-0.5), -1e30)
        e = jnp.exp(s - jnp.max(s, axis=1, keepdims=True))
        p_ref[h] = (e / jnp.sum(e, axis=1, keepdims=True)).astype(BF16)

    @pl.when(step == 0)
    def _():
        acc[...] = jnp.zeros_like(acc)

    total = acc[...]
    for b in range(x_ref.shape[1] // 128):
        xb = x_ref[:, b * 128 : (b + 1) * 128].astype(F32)
        total += xb * xb
    acc[...] = total

    @pl.when(step == pl.num_programs(0) - 1)
    def _():
        ss_ref[...] = row_sum_of_transpose(total)


def make_probs(queries, keys, x):
    length = queries.shape[0]
    heads = queries.shape[1] // HD
    steps = 4
    return pl.pallas_call(
        probs_kernel,
        grid=(steps,),
        in_specs=[
            pl.BlockSpec((length, heads // steps * HD), lambda i: (0, i)),
            pl.BlockSpec((length, HD), lambda i: (0, i // 2)),
            pl.BlockSpec((length, x.shape[1] // steps), lambda i: (0, i)),
        ],
        out_specs=[
            pl.BlockSpec((heads // steps, length, length), lambda i: (i, 0, 0)),
            pl.BlockSpec((1, length), lambda i: (0, 0)),
        ],
        out_shape=[
            jax.ShapeDtypeStruct((heads, length, length), BF16),
            jax.ShapeDtypeStruct((1, length), F32),
        ],
        scratch_shapes=[pltpu.VMEM((length, 128), F32)],
        compiler_params=PARAMS,
    )(queries, keys, x)


def project_kernel(blocks_ref, gain_ref, x_ref, vt_ref, gvt_ref, u_ref):
    low = lax.broadcasted_iota(jnp.int32, (16, 128), 1) < 64
    for b in range(blocks_ref.shape[0] // 2):
        one = blocks_ref[2 * b].astype(F32)
        two = blocks_ref[2 * b + 1].astype(F32)
        first = jnp.where(low, one, pltpu.roll(two, 64, 1))
        second = jnp.where(low, pltpu.roll(one, 64, 1), two)
        at = slice(b * 128, (b + 1) * 128)
        vt = jnp.concatenate([first, second], axis=0)
        vt_ref[:, at] = vt.astype(BF16)
        gvt_ref[:, at] = (vt * gain_ref[:, at].astype(F32)).astype(BF16)
    u_ref[...] = lax.dot_general(
        gvt_ref[...], x_ref[...], (((1,), (1,)), ((), ())), preferred_element_type=F32
    )


def project(blocks, gain, x):
    wide = x.shape[1]
    return pl.pallas_call(
        project_kernel,
        in_specs=[VMEM] * 3,
        out_specs=[VMEM] * 3,
        out_shape=[
            jax.ShapeDtypeStruct((32, wide), BF16),
            jax.ShapeDtypeStruct((32, wide), BF16),
            jax.ShapeDtypeStruct((32, x.shape[0]), F32),
        ],
        compiler_params=PARAMS,
    )(blocks, gain, x)


def values_kernel(width, p_ref, own_ref, got_ref, ss_ref, v_ref, u_ref, rms_ref):
    heads = p_ref.shape[0]
    got = got_ref[...]
    rms = lax.rsqrt((ss_ref[...] + got[heads : heads + 1]) / width + EPS)
    rms_ref[...] = rms
    u = own_ref[...] + got[:heads]
    u_ref[...] = u
    u = u * rms
    total = jnp.zeros(p_ref.shape[1:], F32)
    for j in range(heads):
        total += p_ref[j].astype(F32) * u[j : j + 1]
    v_ref[...] = row_sum_of_transpose(total)


def make_values(width, probs, own, got, ss):
    length = probs.shape[1]
    return pl.pallas_call(
        lambda *refs: values_kernel(width, *refs),
        in_specs=[VMEM] * 4,
        out_specs=[VMEM] * 3,
        out_shape=[
            jax.ShapeDtypeStruct((1, length), F32),
            jax.ShapeDtypeStruct(own.shape, F32),
            jax.ShapeDtypeStruct((1, length), F32),
        ],
        compiler_params=PARAMS,
    )(probs, own, got, ss)


def error_kernel(p_ref, u_ref, own_ref, got_ref, targets_ref, scored_ref, values_ref, c_ref):
    heads, length = u_ref.shape
    values = own_ref[...] + got_ref[...]
    values_ref[...] = values
    error = (values - targets_ref[...]) * scored_ref[...].astype(F32)
    spread = jnp.broadcast_to(error, (length, length)).T
    dot = jnp.zeros((1, length), F32)
    for j in range(heads):
        c = jnp.sum(p_ref[j].astype(F32) * spread, axis=0, keepdims=True)
        c_ref[j : j + 1] = c
        dot += c * u_ref[j : j + 1]
    c_ref[heads:] = jnp.broadcast_to(dot, (c_ref.shape[0] - heads, length))


def make_error(probs, u, own, got, targets, scored):
    length = probs.shape[1]
    return pl.pallas_call(
        error_kernel,
        in_specs=[VMEM] * 6,
        out_specs=[VMEM] * 2,
        out_shape=[
            jax.ShapeDtypeStruct((1, length), F32),
            jax.ShapeDtypeStruct((u.shape[0] + 8, length), F32),
        ],
        compiler_params=PARAMS,
    )(probs, u, own, got, targets, scored)


def weight_kernel(c_ref, rms_ref, gain_ref, vt_ref, x_ref, z_ref, part_ref):
    c = c_ref[...] * rms_ref[...]
    high = c.astype(BF16)
    low = (c - high.astype(F32)).astype(BF16)
    both = jnp.concatenate([high, low], axis=0)
    z = jnp.dot(both, x_ref[...], preferred_element_type=F32)
    z = z[:32] + z[32:]
    gain = gain_ref[...].astype(F32)
    part = jnp.sum(z * vt_ref[...].astype(F32), axis=0, keepdims=True)
    z = z * gain
    for b in range(z_ref.shape[0]):
        at = slice(b * 128, (b + 1) * 128)
        z_ref[b] = z[:, at]
        part_ref[b : b + 1] = part[:, at]


def weight_parts(c, rms, gain, vt, x):
    blocks = x.shape[1] // 128
    return pl.pallas_call(
        weight_kernel,
        in_specs=[VMEM] * 5,
        out_specs=[VMEM] * 2,
        out_shape=[
            jax.ShapeDtypeStruct((blocks, 32, 128), F32),
            jax.ShapeDtypeStruct((blocks, 128), F32),
        ],
        compiler_params=PARAMS,
    )(c, rms, gain, vt, x)


def input_kernel(width, c_ref, dot_ref, rms_ref, gvt_ref, x_ref, out_ref, log_ref):
    rms = rms_ref[...]
    length = rms.shape[1]
    c = c_ref[...] * rms
    high = c.astype(BF16)
    low = (c - high.astype(F32)).astype(BF16)
    log_scale = rms * dot_ref[...]
    log_ref[...] = log_scale
    back = jnp.broadcast_to(rms * rms * log_scale / width, (128, length)).T
    gvt = gvt_ref[...]
    grad = lax.dot_general(
        jnp.concatenate([high, low], axis=0),
        jnp.concatenate([gvt, gvt], axis=0),
        (((0,), (0,)), ((), ())),
        preferred_element_type=F32,
    )
    for b in range(grad.shape[1] // 128):
        at = slice(b * 128, (b + 1) * 128)
        out_ref[:, at] = (grad[:, at] - x_ref[:, at].astype(F32) * back).astype(BF16)


def input_grad(width, c, dot, rms, gvt, x):
    steps = 4
    length, wide = x.shape
    return pl.pallas_call(
        lambda *refs: input_kernel(width, *refs),
        grid=(steps,),
        in_specs=[
            pl.BlockSpec((32, length), lambda i: (0, 0)),
            pl.BlockSpec((1, length), lambda i: (0, 0)),
            pl.BlockSpec((1, length), lambda i: (0, 0)),
            pl.BlockSpec((32, wide // steps), lambda i: (0, i)),
            pl.BlockSpec((length, wide // steps), lambda i: (0, i)),
        ],
        out_specs=[
            pl.BlockSpec((length, wide // steps), lambda i: (0, i)),
            pl.BlockSpec((1, length), lambda i: (0, 0)),
        ],
        out_shape=[
            jax.ShapeDtypeStruct((length, wide), BF16),
            jax.ShapeDtypeStruct((1, length), F32),
        ],
        compiler_params=PARAMS,
    )(c, dot, rms, gvt, x)


def reduce_rows(z, part):
    zi = lax.axis_index("z")
    xi = lax.axis_index("x")
    core = lax.axis_index("core")

    def step(v, part, bit, axis, name, to):
        keep, send = split(bit, v, axis)
        n = send.size // 4096
        sent = jnp.concatenate([send.reshape(n, 32, 128), part[None]], axis=0)
        got = swap(sent, name, to)
        return keep + got[:n].reshape(keep.shape), part + got[n]

    z = z.reshape(4, 2, 4, 32, 128)
    z, part = step(z, part, core == 1, 1, "core", next_door)
    z, part = step(z, part, xi >= 2, 0, "x", mirror_four)
    z, part = step(z, part, xi % 2 == 1, 0, "x", next_door)
    z = z.reshape(4, 32, 128)
    z, part = step(z, part, zi >= 4, 0, "z", mirror_eight)
    z, part = step(z, part, zi % 4 >= 2, 0, "z", two_off)
    z = z[0]
    keep, send = split(zi % 2 == 1, z, 1)
    got = swap(jnp.concatenate([send, part.reshape(64, 64)], axis=0), "z", next_door)
    z = keep + got[:32]
    part = part.reshape(64, 64) + got[32:]
    keep, send = split(lax.axis_index("yh") == 1, z, 0)
    got = swap(jnp.concatenate([send, part], axis=0), "yh", next_door)
    z = cross(keep + got[:16])
    return z, (part + got[16:]).reshape(-1)


def all_reduce(v):
    v = v + swap(v, "core", next_door)
    v = v + swap(v, "x", next_door)
    v = v + swap(v, "x", mirror_four)
    v = v + swap(v, "z", next_door)
    v = v + swap(v, "z", two_off)
    v = v + swap(v, "z", mirror_eight)
    return v + swap(v, "yh", next_door)


def shards(hidden_states, norm_gain, value_weight, queries, keys, readout, targets, scored):
    x = hidden_states
    length = x.shape[0]
    width = x.shape[1] * 2
    yh = lax.axis_index("yh")
    yl = lax.axis_index("yl")
    gain = norm_gain[None]
    rows = value_weight.shape[0]
    w3 = value_weight.reshape(rows, 2, HD)
    r3 = readout.reshape(2, GROUP, HD)
    v = jnp.einsum("igd,gjd->gji", w3.astype(F32), r3, precision=HIGHEST)
    v = v.reshape(2 * GROUP, rows).astype(BF16)

    probs, ss = make_probs(queries, keys, x)

    v = cross(v)
    other = swap(v, "yh", next_door)
    v = jnp.concatenate([jnp.where(yh == 0, v, other), jnp.where(yh == 0, other, v)], axis=1)
    blocks = lax.all_to_all(
        jnp.broadcast_to(v, (64,) + v.shape), ("x", "core", "z"), 0, 0
    )
    vt, gvt, u = project(blocks, gain, x)
    own, send = split(yl == 1, u, 0)
    got = swap(jnp.concatenate([send, jnp.broadcast_to(ss, (8, length))], axis=0), "yl", next_door)
    part_values, u, rms = make_values(width, probs, own, got, ss)
    got = swap(part_values, "yl", next_door)
    values, c = make_error(probs, u, part_values, got, targets[None], scored[None])
    got = swap(c, "yl", next_door)
    dot = c[16:17] + got[16:17]
    c = jnp.concatenate([jnp.where(yl == 0, c[:16], got[:16]), jnp.where(yl == 0, got[:16], c[:16])], axis=0)
    z, part = weight_parts(c, rms, gain, vt, x)
    grad_input, log_scale = input_grad(width, c, dot, rms, gvt, x)
    z, grad_gain = reduce_rows(z, part)
    z3 = z.reshape(2, GROUP, rows)
    grad_weight = jnp.einsum("gji,gjd->igd", z3, r3, precision=HIGHEST).reshape(rows, 2 * HD)
    read_part = jnp.einsum("gji,igd->gjd", z3, w3.astype(F32), precision=HIGHEST)
    grad_readout = all_reduce(read_part.reshape(16, HD)).reshape(-1)
    return (values[0], grad_input, grad_weight, grad_gain, grad_readout, log_scale[0])


def solution(mesh):
    fine = Mesh(mesh.devices.reshape(2, 4, 2, 8, 2), ("yh", "x", "core", "z", "yl"))
    seq = ("yh", "x", "core", "z")
    return jax.shard_map(
        shards,
        mesh=fine,
        in_specs=(
            P(seq, "yl"),
            P("yl"),
            P(seq, "yl"),
            P(seq, "yl"),
            P(seq, "yl"),
            P("yl"),
            P(seq),
            P(seq),
        ),
        out_specs=(
            P(seq),
            P(seq, "yl"),
            P(seq, "yl"),
            P("yl"),
            P("yl"),
            P(seq),
        ),
        check_vma=False,
    )
```

time: 958 us -> 126 us (0.13)
  blocking collectives: 659 us -> 0 us
  waiting for transfers between devices: 240 us -> 56.7 us
  starting transfers between devices: 0.34 us -> 46.1 us
  matrix products: 21.5 us -> 1.26 us
  other arithmetic: 16.5 us -> 3.27 us
  between operations: 13.9 us -> 0.99 us
    psum x3 -> x0, blocking collectives: 654 us -> none  [the longest x1 644 us: shards(): lax.psum((gain_part, readout_part), ('rep', 'node'))]
    all_gather x2 -> x0, waiting for transfers between devices: 177 us -> none  [the longest x1 120 us: shards(): lax.all_gather(value_weight, ('rep', 'node'), axis=0, tiled=True)]
    reduce_scatter x2 -> x0, waiting for transfers between devices: 61.9 us -> none  [the longest x1 46.5 us: shards(): lax.psum_scatter(grad_normed.astype(jnp.bfloat16), 'tp', scatter_dimensio...]
    ppermute x0 -> x20, waiting for transfers between devices: none -> 52.8 us  [the longest x18 52.8 us: swap(): lax.ppermute(v, axis, [(i, to(i)) for i in range(lax.axis_size(axis))])]
    ppermute x0 -> x20, starting transfers between devices: none -> 34.5 us  [the longest x18 33.1 us: swap(): lax.ppermute(v, axis, [(i, to(i)) for i in range(lax.axis_size(axis))])]
    dot_general x6 -> x3, matrix products: 21.5 us -> 1.26 us  [the longest x1 0.83 us: shards(): v = jnp.einsum('igd,gjd->gji', w3.astype(F32), r3, precision=HIGHEST)]
    all_to_all x0 -> x1, starting transfers between devices: none -> 11.6 us  [shards(): lax.all_to_all(jnp.broadcast_to(v, (64,) + v.shape), ('x', 'core', 'z'),...]
    reduce_sum x3 -> x0, other arithmetic: 9.66 us -> none  [the longest x1 4.1 us: shards(): gain_part = jnp.sum(grad_share * x_share * rms_inv, axis=0)]
  transfers between devices with their start and end apart: 4 -> 21, of which waited for: 4 -> 19; matrix products, arithmetic and copies ran while one was open for 3% -> 2% of each run, Pallas kernels for 0% -> 5%
where the time goes in v1:
time: 126 us
  waiting for transfers between devices  56.7 us (45%)
  starting transfers between devices  46.1 us (37%)
  local copies, waits for them, and re-layouts  9.26 us (7%)
  Pallas kernels  8.1 us (6%)
  other arithmetic  3.27 us (3%)
  matrix products  1.26 us (1%)
    ppermute x18, waiting for transfers between devices, swap(): lax.ppermute(v, axis, [(i, to(i)) for i in range(lax.axis_size(axis))])  52.8 us
    ppermute x18, starting transfers between devices, swap(): lax.ppermute(v, axis, [(i, to(i)) for i in range(lax.axis_size(axis))])  33.1 us
    all_to_all x1, starting transfers between devices, shards(): lax.all_to_all(jnp.broadcast_to(v, (64,) + v.shape), ('x', 'core', 'z'),...  11.6 us
    unnamed x22, local copies, waits for them, and re-layouts  6.39 us
    all_to_all x1, waiting for transfers between devices, shards(): lax.all_to_all(jnp.broadcast_to(v, (64,) + v.shape), ('x', 'core', 'z'),...  3.86 us
    pallas_call x1, Pallas kernels, make_probs(): pl.pallas_call(probs_kernel, grid=(steps,), in_specs=[pl.BlockSpec((lengt...  3.02 us
    pallas_call x1, Pallas kernels, input_grad(): pl.pallas_call(lambda *refs: input_kernel(width, *refs), grid=(steps,), i...  2.72 us
  transfers between devices with their start and end apart: 21, of which 19 were waited for; matrix products, arithmetic and copies ran while one was open for 2% of the time, Pallas kernels for 5%

profile of v1, /device:TPU:32, one launch (start us, length us, event | category | flops | bytes accessed | tf_op | source)
XLA Modules:
  0.0 125.6 jit_solution(16242840798789971680)
XLA Ops:
  0.6 0.7 copy-done
  1.4 0.8 fusion
  2.2 0.7 collective-permute-start
  2.9 8.0 %collective-permute-start.1 = (bf16[16,64]{1,0:T(8,128)(2,1)S(1)}, bf16[16,64]{1,0:T(8,128)(2,1)S(1)}, u32[]{:S(2)}, u32[]{:S(2)}) collective-permute-start(bf16[16,64]{1,0:T(8,128)(2,1)S(1)} %collective-permute-done), channel_id=1, source_target_pairs={{0,128},{128,0},{1,129},{129,1},{2,130},{130,2},{3,131},{131,3},{4... | collective-permute-start | bytes 6152 | tf_op jit(solution)/shard_map/ppermute | solution.py:20
  10.9 1.6 %collective-permute-done.1 = bf16[16,64]{1,0:T(8,128)(2,1)S(1)} collective-permute-done((bf16[16,64]{1,0:T(8,128)(2,1)S(1)}, bf16[16,64]{1,0:T(8,128)(2,1)S(1)}, u32[]{:S(2)}, u32[]{:S(2)}) %collective-permute-start.1) | collective-permute-done | bytes 2080 | tf_op jit(solution)/shard_map/ppermute | solution.py:20
  12.5 0.1 pad_maximum_fusion.9
  12.6 0.7 broadcast_in_dim.34
  13.4 11.6 %all-to-all-start = ((bf16[64,16,128]{2,1,0:T(8,128)(2,1)}), bf16[64,16,128]{2,1,0:T(8,128)(2,1)S(1)}, u32[]{:S(2)}, u32[]{:S(2)}) async-start(bf16[64,16,128]{2,1,0:T(8,128)(2,1)} %broadcast_in_dim.34), calls=%async_computation | async-start | bytes 524288 | tf_op jit(solution)/shard_map/all_to_all | solution.py:331
  25.0 0.7 broadcast_in_dim.35.gain_ref
  25.7 1.6 %copy-done.1 = bf16[256,4096]{1,0:T(8,128)(2,1)S(1)} copy-done((bf16[256,4096]{1,0:T(8,128)(2,1)S(1)}, bf16[256,4096]{1,0:T(8,128)(2,1)}, u32[]{:S(2)}) %copy-start.1) | copy-done | bytes 2097176
  27.3 1.2 copy-done.5
  28.5 0.9 copy-done.6
  29.4 3.0 %shard_map.127 = (bf16[16,256,256]{2,1,0:T(8,128)(2,1)S(1)}, f32[1,256]{1,0:T(1,128)S(1)}) custom-call(bf16[256,2048]{1,0:T(8,128)(2,1)S(1)} %copy-done.5, bf16[256,256]{1,0:T(8,128)(2,1)S(1)} %copy-done.6, bf16[256,4096]{1,0:T(8,128)(2,1)S(1)} %copy-done.1), custom_call_target="tpu_custom_call" | custom-call | tf_op jit(solution)/shard_map/pallas_call | solution.py:88
  32.4 1.3 %copy-done.3 = bf16[16,256,256]{2,1,0:T(8,128)(2,1)} copy-done((bf16[16,256,256]{2,1,0:T(8,128)(2,1)}, bf16[16,256,256]{2,1,0:T(8,128)(2,1)S(1)}, u32[]{:S(2)}) %copy-start.3) | copy-done | bytes 2097176
  33.7 3.9 %all-to-all-done.blocks_ref = bf16[64,16,128]{2,1,0:T(8,128)(2,1)S(1)} async-done(((bf16[64,16,128]{2,1,0:T(8,128)(2,1)}), bf16[64,16,128]{2,1,0:T(8,128)(2,1)S(1)}, u32[]{:S(2)}, u32[]{:S(2)}) %all-to-all-start) | async-done | bytes 262176 | tf_op jit(solution)/shard_map/all_to_all | solution.py:331
  37.6 0.8 shard_map.128
  38.4 2.0 %collective-permute-start.2 = (f32[24,256]{1,0:T(8,128)S(1)}, f32[24,256]{1,0:T(8,128)S(1)}, u32[]{:S(2)}, u32[]{:S(2)}) collective-permute-start(f32[24,256]{1,0:T(8,128)S(1)} %pad_maximum_fusion.8), channel_id=1, source_target_pairs={{0,1},{1,0},{2,3},{3,2},{4,5},{5,4},{6,7},{7,6},{8,9},{9,8},{10,11... | collective-permute-start | bytes 73736 | tf_op jit(solution)/shard_map/ppermute | solution.py:20
  40.4 1.9 %collective-permute-done.2.refs_2_ = f32[24,256]{1,0:T(8,128)S(1)} collective-permute-done((f32[24,256]{1,0:T(8,128)S(1)}, f32[24,256]{1,0:T(8,128)S(1)}, u32[]{:S(2)}, u32[]{:S(2)}) %collective-permute-start.2) | collective-permute-done | bytes 24608 | tf_op jit(solution)/shard_map/ppermute | solution.py:20
  42.3 0.6 shard_map.129
  42.9 2.0 %collective-permute-start.3 = (f32[1,256]{1,0:T(1,128)S(1)}, f32[1,256]{1,0:T(1,128)S(1)}, u32[]{:S(2)}, u32[]{:S(2)}) collective-permute-start(f32[1,256]{1,0:T(1,128)S(1)} %get-tuple-element.24.own_ref), channel_id=1, source_target_pairs={{0,1},{1,0},{2,3},{3,2},{4,5},{5,4},{6,7},{7,6},{8,9},{9,8},{10,11... | collective-permute-start | bytes 3080 | tf_op jit(solution)/shard_map/ppermute | solution.py:20
  44.9 1.7 %collective-permute-done.3.got_ref = f32[1,256]{1,0:T(1,128)S(1)} collective-permute-done((f32[1,256]{1,0:T(1,128)S(1)}, f32[1,256]{1,0:T(1,128)S(1)}, u32[]{:S(2)}, u32[]{:S(2)}) %collective-permute-start.3) | collective-permute-done | bytes 1056 | tf_op jit(solution)/shard_map/ppermute | solution.py:20
  46.6 0.6 shard_map.130
  47.1 2.0 %collective-permute-start.4 = (f32[24,256]{1,0:T(8,128)S(1)}, f32[24,256]{1,0:T(8,128)S(1)}, u32[]{:S(2)}, u32[]{:S(2)}) collective-permute-start(f32[24,256]{1,0:T(8,128)S(1)} %get-tuple-element.26), channel_id=1, source_target_pairs={{0,1},{1,0},{2,3},{3,2},{4,5},{5,4},{6,7},{7,6},{8,9},{9,8},{10,11... | collective-permute-start | bytes 73736 | tf_op jit(solution)/shard_map/ppermute | solution.py:20
  49.1 1.9 %collective-permute-done.4 = f32[24,256]{1,0:T(8,128)S(1)} collective-permute-done((f32[24,256]{1,0:T(8,128)S(1)}, f32[24,256]{1,0:T(8,128)S(1)}, u32[]{:S(2)}, u32[]{:S(2)}) %collective-permute-start.4) | collective-permute-done | bytes 24608 | tf_op jit(solution)/shard_map/ppermute | solution.py:20
  51.0 0.6 copy-done.10
  51.6 0.5 shard_map.132
  52.1 0.7 pad_maximum_fusion
  52.9 1.8 %collective-permute-done.5 = f32[17,32,128]{2,1,0:T(8,128)S(1)} collective-permute-done((f32[17,32,128]{2,1,0:T(8,128)}, f32[17,32,128]{2,1,0:T(8,128)S(1)}, u32[]{:S(2)}, u32[]{:S(2)}) %collective-permute-start.5) | collective-permute-done | bytes 278560 | tf_op jit(solution)/shard_map/ppermute | solution.py:20
  54.8 0.7 pad_maximum_fusion.1
  55.4 1.1 collective-permute-start.6
  56.5 6.2 %collective-permute-done.6 = f32[9,32,128]{2,1,0:T(8,128)S(1)} collective-permute-done((f32[9,32,128]{2,1,0:T(8,128)}, f32[9,32,128]{2,1,0:T(8,128)S(1)}, u32[]{:S(2)}, u32[]{:S(2)}) %collective-permute-start.6) | collective-permute-done | bytes 147488 | tf_op jit(solution)/shard_map/ppermute | solution.py:20
  62.9 0.1 collective-permute-start.7
  63.0 4.4 %collective-permute-done.7 = f32[5,32,128]{2,1,0:T(8,128)S(1)} collective-permute-done((f32[5,32,128]{2,1,0:T(8,128)S(1)}, f32[5,32,128]{2,1,0:T(8,128)S(1)}, u32[]{:S(2)}, u32[]{:S(2)}) %collective-permute-start.7) | collective-permute-done | bytes 81952 | tf_op jit(solution)/shard_map/ppermute | solution.py:20
  67.4 2.0 %collective-permute-start.8 = (f32[3,32,128]{2,1,0:T(8,128)S(1)}, f32[3,32,128]{2,1,0:T(8,128)S(1)}, u32[]{:S(2)}, u32[]{:S(2)}) collective-permute-start(f32[3,32,128]{2,1,0:T(8,128)S(1)} %pad_maximum_fusion.3), channel_id=1, source_target_pairs={{0,14},{2,12},{4,10},{6,8},{8,6},{10,4},{12,2},{14,0},{1,15},{3,13... | collective-permute-start | bytes 147464 | tf_op jit(solution)/shard_map/ppermute | solution.py:20
  69.4 5.2 %collective-permute-done.8 = f32[3,32,128]{2,1,0:T(8,128)S(1)} collective-permute-done((f32[3,32,128]{2,1,0:T(8,128)S(1)}, f32[3,32,128]{2,1,0:T(8,128)S(1)}, u32[]{:S(2)}, u32[]{:S(2)}) %collective-permute-start.8) | collective-permute-done | bytes 49184 | tf_op jit(solution)/shard_map/ppermute | solution.py:20
  74.7 0.1 collective-permute-start.9
  74.8 4.8 %collective-permute-done.9 = f32[2,32,128]{2,1,0:T(8,128)S(1)} collective-permute-done((f32[2,32,128]{2,1,0:T(8,128)S(1)}, f32[2,32,128]{2,1,0:T(8,128)S(1)}, u32[]{:S(2)}, u32[]{:S(2)}) %collective-permute-start.9) | collective-permute-done | bytes 32800 | tf_op jit(solution)/shard_map/ppermute | solution.py:20
  79.6 0.1 reshape.76
  79.7 0.1 slice_select_fusion.2
  79.8 0.1 collective-permute-start.10
  79.9 4.1 %collective-permute-done.10 = f32[96,64]{1,0:T(8,128)S(1)} collective-permute-done((f32[96,64]{1,0:T(8,128)S(1)}, f32[96,64]{1,0:T(8,128)S(1)}, u32[]{:S(2)}, u32[]{:S(2)}) %collective-permute-start.10) | collective-permute-done | bytes 24608 | tf_op jit(solution)/shard_map/ppermute | solution.py:20
  83.9 0.1 slice_add_fusion.3
  84.0 3.6 %collective-permute-start.11 = (f32[80,64]{1,0:T(8,128)S(1)}, f32[80,64]{1,0:T(8,128)S(1)}, u32[]{:S(2)}, u32[]{:S(2)}) collective-permute-start(f32[80,64]{1,0:T(8,128)S(1)} %pad_maximum_fusion.5), channel_id=1, source_target_pairs={{0,128},{128,0},{1,129},{129,1},{2,130},{130,2},{3,131},{131,3},{4... | collective-permute-start | bytes 61448 | tf_op jit(solution)/shard_map/ppermute | solution.py:20
  87.7 2.0 %collective-permute-done.11 = f32[80,64]{1,0:T(8,128)S(1)} collective-permute-done((f32[80,64]{1,0:T(8,128)S(1)}, f32[80,64]{1,0:T(8,128)S(1)}, u32[]{:S(2)}, u32[]{:S(2)}) %collective-permute-start.11) | collective-permute-done | bytes 20512 | tf_op jit(solution)/shard_map/ppermute | solution.py:20
  89.6 0.7 collective-permute-start.12
  90.3 0.1 convolution_bitcast_fusion.1
  90.5 1.2 collective-permute-done.13
  91.6 0.3 collective-permute-start.14
  91.9 3.4 %collective-permute-done.14 = f32[16,128]{1,0:T(8,128)S(1)} collective-permute-done((f32[16,128]{1,0:T(8,128)S(1)}, f32[16,128]{1,0:T(8,128)S(1)}, u32[]{:S(2)}, u32[]{:S(2)}) %collective-permute-start.14) | collective-permute-done | bytes 8224 | tf_op jit(solution)/shard_map/ppermute | solution.py:20
  95.3 1.1 collective-permute-start.15
  96.4 3.8 %collective-permute-done.15 = f32[16,128]{1,0:T(8,128)S(1)} collective-permute-done((f32[16,128]{1,0:T(8,128)S(1)}, f32[16,128]{1,0:T(8,128)S(1)}, u32[]{:S(2)}, u32[]{:S(2)}) %collective-permute-start.15) | collective-permute-done | bytes 8224 | tf_op jit(solution)/shard_map/ppermute | solution.py:20
  100.2 3.6 %collective-permute-done.16 = f32[16,128]{1,0:T(8,128)S(1)} collective-permute-done((f32[16,128]{1,0:T(8,128)S(1)}, f32[16,128]{1,0:T(8,128)S(1)}, u32[]{:S(2)}, u32[]{:S(2)}) %collective-permute-start.16) | collective-permute-done | bytes 8224 | tf_op jit(solution)/shard_map/ppermute | solution.py:20
  103.8 0.5 collective-permute-start.17
  104.3 0.7 slice_add_fusion.6.refs_1_
  105.0 2.7 %shard_map.131 = (bf16[256,4096]{1,0:T(8,128)(2,1)}, f32[1,256]{1,0:T(1,128)}) custom-call(f32[32,256]{1,0:T(8,128)S(1)} %pad_maximum_fusion.6.refs_0_.c_ref, f32[1,256]{1,0:T(1,128)S(1)} %slice_add_fusion.6.refs_1_, f32[1,256]{1,0:T(1,128)S(1)} %get-tuple-element.27.refs_2_.rms_ref, bf16[32,4096]{1,0:T(8,128)(2,1)S(1)} %get-tuple-element.28.refs_3_, ...), custom_call_target="tpu_custom_call" | custom-call | tf_op jit(solution)/shard_map/pallas_call | solution.py:251
  107.7 0.6 collective-permute-done.17
  108.4 1.9 %collective-permute-start.18 = (f32[16,128]{1,0:T(8,128)S(1)}, f32[16,128]{1,0:T(8,128)S(1)}, u32[]{:S(2)}, u32[]{:S(2)}) collective-permute-start(f32[16,128]{1,0:T(8,128)S(1)} %add.98), channel_id=1, source_target_pairs={{0,14},{2,12},{4,10},{6,8},{8,6},{10,4},{12,2},{14,0},{1,15},{3,13... | collective-permute-start | bytes 24584 | tf_op jit(solution)/shard_map/ppermute | solution.py:20
  110.3 0.7 reshape.79
  111.0 4.1 %collective-permute-done.18 = f32[16,128]{1,0:T(8,128)S(1)} collective-permute-done((f32[16,128]{1,0:T(8,128)S(1)}, f32[16,128]{1,0:T(8,128)S(1)}, u32[]{:S(2)}, u32[]{:S(2)}) %collective-permute-start.18) | collective-permute-done | bytes 8224 | tf_op jit(solution)/shard_map/ppermute | solution.py:20
  115.0 8.4 %collective-permute-start.19 = (f32[16,128]{1,0:T(8,128)S(1)}, f32[16,128]{1,0:T(8,128)S(1)}, u32[]{:S(2)}, u32[]{:S(2)}) collective-permute-start(f32[16,128]{1,0:T(8,128)S(1)} %add.99), channel_id=1, source_target_pairs={{0,128},{128,0},{1,129},{129,1},{2,130},{130,2},{3,131},{131,3},{4... | collective-permute-start | bytes 24584 | tf_op jit(solution)/shard_map/ppermute | solution.py:20
  123.4 0.3 convolution_bitcast_fusion
  123.7 0.6 copy.30
  124.3 0.7 collective-permute-done.19
  125.0 0.6 add_bitcast_fusion
  (59 shorter events, 0.4 us)
Async XLA Ops:
  0.6 0.8 copy-start
  2.2 0.7 collective-permute-start
  2.9 9.6 %collective-permute-start.1 = (bf16[16,64]{1,0:T(8,128)(2,1)S(1)}, bf16[16,64]{1,0:T(8,128)(2,1)S(1)}, u32[]{:S(2)}, u32[]{:S(2)}) collective-permute-start(bf16[16,64]{1,0:T(8,128)(2,1)S(1)} %collective-permute-done), channel_id=1, source_target_pairs={{0,128},{128,0},{1,129},{129,1},{2,130},{130,2},{3,131},{131,3},{4... | collective-permute-start | bytes 6152 | tf_op jit(solution)/shard_map/ppermute | solution.py:20
  13.4 24.2 %all-to-all-start = ((bf16[64,16,128]{2,1,0:T(8,128)(2,1)}), bf16[64,16,128]{2,1,0:T(8,128)(2,1)S(1)}, u32[]{:S(2)}, u32[]{:S(2)}) async-start(bf16[64,16,128]{2,1,0:T(8,128)(2,1)} %broadcast_in_dim.34), calls=%async_computation | async-start | bytes 524288 | tf_op jit(solution)/shard_map/all_to_all | solution.py:331
  25.7 1.6 %copy-start.1 = (bf16[256,4096]{1,0:T(8,128)(2,1)S(1)}, bf16[256,4096]{1,0:T(8,128)(2,1)}, u32[]{:S(2)}) copy-start(bf16[256,4096]{1,0:T(8,128)(2,1)} %x_ref.5) | copy-start | bytes 6291460
  27.3 1.2 copy-start.5
  28.5 0.9 copy-start.6
  29.4 8.2 %copy-start.2 = (bf16[256,4096]{1,0:T(8,128)(2,1)S(1)}, bf16[256,4096]{1,0:T(8,128)(2,1)}, u32[]{:S(2)}) copy-start(bf16[256,4096]{1,0:T(8,128)(2,1)} %x_ref.5) | copy-start | bytes 6291460
  32.4 1.3 %copy-start.3 = (bf16[16,256,256]{2,1,0:T(8,128)(2,1)}, bf16[16,256,256]{2,1,0:T(8,128)(2,1)S(1)}, u32[]{:S(2)}) copy-start(bf16[16,256,256]{2,1,0:T(8,128)(2,1)S(1)} %get-tuple-element.20.refs_0_.p_ref) | copy-start | bytes 6291460
  33.7 12.8 %copy-start.7 = (f32[256]{0:T(256)S(1)}, f32[256]{0:T(256)}, u32[]{:S(2)}) copy-start(f32[256]{0:T(256)} %param.14) | copy-start | bytes 3076
  33.7 12.8 %copy-start.8 = (s32[256]{0:T(256)S(1)}, s32[256]{0:T(256)}, u32[]{:S(2)}) copy-start(s32[256]{0:T(256)} %param.15) | copy-start | bytes 3076
  37.6 4.7 %copy-start.4 = (bf16[16,256,256]{2,1,0:T(8,128)(2,1)S(1)}, bf16[16,256,256]{2,1,0:T(8,128)(2,1)}, u32[]{:S(2)}) copy-start(bf16[16,256,256]{2,1,0:T(8,128)(2,1)} %copy-done.3) | copy-start | bytes 6291460
  38.4 3.9 %collective-permute-start.2 = (f32[24,256]{1,0:T(8,128)S(1)}, f32[24,256]{1,0:T(8,128)S(1)}, u32[]{:S(2)}, u32[]{:S(2)}) collective-permute-start(f32[24,256]{1,0:T(8,128)S(1)} %pad_maximum_fusion.8), channel_id=1, source_target_pairs={{0,1},{1,0},{2,3},{3,2},{4,5},{5,4},{6,7},{7,6},{8,9},{9,8},{10,11... | collective-permute-start | bytes 73736 | tf_op jit(solution)/shard_map/ppermute | solution.py:20
  42.9 3.7 %collective-permute-start.3 = (f32[1,256]{1,0:T(1,128)S(1)}, f32[1,256]{1,0:T(1,128)S(1)}, u32[]{:S(2)}, u32[]{:S(2)}) collective-permute-start(f32[1,256]{1,0:T(1,128)S(1)} %get-tuple-element.24.own_ref), channel_id=1, source_target_pairs={{0,1},{1,0},{2,3},{3,2},{4,5},{5,4},{6,7},{7,6},{8,9},{9,8},{10,11... | collective-permute-start | bytes 3080 | tf_op jit(solution)/shard_map/ppermute | solution.py:20
  47.1 3.9 %collective-permute-start.4 = (f32[24,256]{1,0:T(8,128)S(1)}, f32[24,256]{1,0:T(8,128)S(1)}, u32[]{:S(2)}, u32[]{:S(2)}) collective-permute-start(f32[24,256]{1,0:T(8,128)S(1)} %get-tuple-element.26), channel_id=1, source_target_pairs={{0,1},{1,0},{2,3},{3,2},{4,5},{5,4},{6,7},{7,6},{8,9},{9,8},{10,11... | collective-permute-start | bytes 73736 | tf_op jit(solution)/shard_map/ppermute | solution.py:20
  51.0 0.6 copy-start.10
  52.9 1.8 %collective-permute-start.5 = (f32[17,32,128]{2,1,0:T(8,128)}, f32[17,32,128]{2,1,0:T(8,128)S(1)}, u32[]{:S(2)}, u32[]{:S(2)}) collective-permute-start(f32[17,32,128]{2,1,0:T(8,128)} %pad_maximum_fusion), channel_id=1, source_target_pairs={{0,16},{16,0},{1,17},{17,1},{2,18},{18,2},{3,19},{19,3},{4,20},{20... | collective-permute-start | bytes 835592 | tf_op jit(solution)/shard_map/ppermute | solution.py:20
  55.4 7.3 %collective-permute-start.6 = (f32[9,32,128]{2,1,0:T(8,128)}, f32[9,32,128]{2,1,0:T(8,128)S(1)}, u32[]{:S(2)}, u32[]{:S(2)}) collective-permute-start(f32[9,32,128]{2,1,0:T(8,128)} %pad_maximum_fusion.1), channel_id=1, source_target_pairs={{0,96},{32,64},{64,32},{96,0},{1,97},{33,65},{65,33},{97,1},{2,98}... | collective-permute-start | bytes 442376 | tf_op jit(solution)/shard_map/ppermute | solution.py:20
  62.9 4.5 %collective-permute-start.7 = (f32[5,32,128]{2,1,0:T(8,128)S(1)}, f32[5,32,128]{2,1,0:T(8,128)S(1)}, u32[]{:S(2)}, u32[]{:S(2)}) collective-permute-start(f32[5,32,128]{2,1,0:T(8,128)S(1)} %pad_maximum_fusion.2), channel_id=1, source_target_pairs={{0,32},{32,0},{64,96},{96,64},{1,33},{33,1},{65,97},{97,65},{2,34}... | collective-permute-start | bytes 245768 | tf_op jit(solution)/shard_map/ppermute | solution.py:20
  63.0 60.5 %copy-start.9 = (f32[2048]{0:T(1024)S(1)}, f32[2048]{0:T(1024)}, u32[]{:S(2)}) copy-start(f32[2048]{0:T(1024)} %param.13) | copy-start | bytes 24580
  67.4 7.2 %collective-permute-start.8 = (f32[3,32,128]{2,1,0:T(8,128)S(1)}, f32[3,32,128]{2,1,0:T(8,128)S(1)}, u32[]{:S(2)}, u32[]{:S(2)}) collective-permute-start(f32[3,32,128]{2,1,0:T(8,128)S(1)} %pad_maximum_fusion.3), channel_id=1, source_target_pairs={{0,14},{2,12},{4,10},{6,8},{8,6},{10,4},{12,2},{14,0},{1,15},{3,13... | collective-permute-start | bytes 147464 | tf_op jit(solution)/shard_map/ppermute | solution.py:20
  74.7 4.9 %collective-permute-start.9 = (f32[2,32,128]{2,1,0:T(8,128)S(1)}, f32[2,32,128]{2,1,0:T(8,128)S(1)}, u32[]{:S(2)}, u32[]{:S(2)}) collective-permute-start(f32[2,32,128]{2,1,0:T(8,128)S(1)} %pad_maximum_fusion.7), channel_id=1, source_target_pairs={{0,4},{2,6},{4,0},{6,2},{8,12},{10,14},{12,8},{14,10},{1,5},{3,7},... | collective-permute-start | bytes 98312 | tf_op jit(solution)/shard_map/ppermute | solution.py:20
  79.8 4.2 %collective-permute-start.10 = (f32[96,64]{1,0:T(8,128)S(1)}, f32[96,64]{1,0:T(8,128)S(1)}, u32[]{:S(2)}, u32[]{:S(2)}) collective-permute-start(f32[96,64]{1,0:T(8,128)S(1)} %pad_maximum_fusion.4), channel_id=1, source_target_pairs={{0,2},{2,0},{4,6},{6,4},{8,10},{10,8},{12,14},{14,12},{1,3},{3,1},... | collective-permute-start | bytes 73736 | tf_op jit(solution)/shard_map/ppermute | solution.py:20
  84.0 5.6 %collective-permute-start.11 = (f32[80,64]{1,0:T(8,128)S(1)}, f32[80,64]{1,0:T(8,128)S(1)}, u32[]{:S(2)}, u32[]{:S(2)}) collective-permute-start(f32[80,64]{1,0:T(8,128)S(1)} %pad_maximum_fusion.5), channel_id=1, source_target_pairs={{0,128},{128,0},{1,129},{129,1},{2,130},{130,2},{3,131},{131,3},{4... | collective-permute-start | bytes 61448 | tf_op jit(solution)/shard_map/ppermute | solution.py:20
  89.6 0.7 collective-permute-start.12
  90.5 1.2 collective-permute-start.13
  91.6 3.7 %collective-permute-start.14 = (f32[16,128]{1,0:T(8,128)S(1)}, f32[16,128]{1,0:T(8,128)S(1)}, u32[]{:S(2)}, u32[]{:S(2)}) collective-permute-start(f32[16,128]{1,0:T(8,128)S(1)} %add.94), channel_id=1, source_target_pairs={{0,32},{32,0},{64,96},{96,64},{1,33},{33,1},{65,97},{97,65},{2,34}... | collective-permute-start | bytes 24584 | tf_op jit(solution)/shard_map/ppermute | solution.py:20
  95.3 4.9 %collective-permute-start.15 = (f32[16,128]{1,0:T(8,128)S(1)}, f32[16,128]{1,0:T(8,128)S(1)}, u32[]{:S(2)}, u32[]{:S(2)}) collective-permute-start(f32[16,128]{1,0:T(8,128)S(1)} %add.95), channel_id=1, source_target_pairs={{0,96},{32,64},{64,32},{96,0},{1,97},{33,65},{65,33},{97,1},{2,98}... | collective-permute-start | bytes 24584 | tf_op jit(solution)/shard_map/ppermute | solution.py:20
  100.2 3.7 %collective-permute-start.16 = (f32[16,128]{1,0:T(8,128)S(1)}, f32[16,128]{1,0:T(8,128)S(1)}, u32[]{:S(2)}, u32[]{:S(2)}) collective-permute-start(f32[16,128]{1,0:T(8,128)S(1)} %add.96), channel_id=1, source_target_pairs={{0,2},{2,0},{4,6},{6,4},{8,10},{10,8},{12,14},{14,12},{1,3},{3,1},... | collective-permute-start | bytes 24584 | tf_op jit(solution)/shard_map/ppermute | solution.py:20
  103.8 4.5 %collective-permute-start.17 = (f32[16,128]{1,0:T(8,128)S(1)}, f32[16,128]{1,0:T(8,128)S(1)}, u32[]{:S(2)}, u32[]{:S(2)}) collective-permute-start(f32[16,128]{1,0:T(8,128)S(1)} %add.97), channel_id=1, source_target_pairs={{0,4},{2,6},{4,0},{6,2},{8,12},{10,14},{12,8},{14,10},{1,5},{3,7},... | collective-permute-start | bytes 24584 | tf_op jit(solution)/shard_map/ppermute | solution.py:20
  108.4 6.7 %collective-permute-start.18 = (f32[16,128]{1,0:T(8,128)S(1)}, f32[16,128]{1,0:T(8,128)S(1)}, u32[]{:S(2)}, u32[]{:S(2)}) collective-permute-start(f32[16,128]{1,0:T(8,128)S(1)} %add.98), channel_id=1, source_target_pairs={{0,14},{2,12},{4,10},{6,8},{8,6},{10,4},{12,2},{14,0},{1,15},{3,13... | collective-permute-start | bytes 24584 | tf_op jit(solution)/shard_map/ppermute | solution.py:20
  115.0 10.0 %collective-permute-start.19 = (f32[16,128]{1,0:T(8,128)S(1)}, f32[16,128]{1,0:T(8,128)S(1)}, u32[]{:S(2)}, u32[]{:S(2)}) collective-permute-start(f32[16,128]{1,0:T(8,128)S(1)} %add.99), channel_id=1, source_target_pairs={{0,128},{128,0},{1,129},{129,1},{2,130},{130,2},{3,131},{131,3},{4... | collective-permute-start | bytes 24584 | tf_op jit(solution)/shard_map/ppermute | solution.py:20

commit v2 on v1

--- a/solution.py
+++ b/solution.py
@@ -16,24 +16,14 @@
 PARAMS = pltpu.CompilerParams(vmem_limit_bytes=48 * 1024 * 1024)
 
 
-def swap(v, axis, to):
-    return lax.ppermute(v, axis, [(i, to(i)) for i in range(lax.axis_size(axis))])
-
-
-def next_door(i):
-    return i ^ 1
-
-
-def two_off(i):
-    return i ^ 2
-
-
-def mirror_four(i):
-    return 3 - i
-
-
-def mirror_eight(i):
-    return 7 - i
+SEQ = ("yh", "x", "core", "z")
+ROWS = 64
+BLOCKS = 64
+HALF = 16
+
+
+def swap(v, axis):
+    return lax.ppermute(v, axis, [(0, 1), (1, 0)])
 
 
 def cross(v):
@@ -45,6 +35,37 @@
     low = lax.slice_in_dim(v, 0, n, axis=axis)
     high = lax.slice_in_dim(v, n, 2 * n, axis=axis)
     return jnp.where(bit, high, low), jnp.where(bit, low, high)
+
+
+def whole(body, out_shape, *args):
+    many = isinstance(out_shape, list)
+    return pl.pallas_call(
+        body,
+        in_specs=[VMEM] * len(args),
+        out_specs=[VMEM] * len(out_shape) if many else VMEM,
+        out_shape=out_shape,
+        compiler_params=PARAMS,
+    )(*args)
+
+
+def shape(*dims, dtype=F32):
+    return jax.ShapeDtypeStruct(dims, dtype)
+
+
+def exact_dot(a, b, dims):
+    return lax.dot_general(a, b, (dims, ((), ())), precision=HIGHEST, preferred_element_type=F32)
+
+
+def left_lanes(rows):
+    return lax.broadcasted_iota(jnp.int32, (rows, 128), 1) < 64
+
+
+def read_kernel(w_ref, r_ref, v_ref):
+    parts = []
+    for g in range(2):
+        w = w_ref[:, g * HD : (g + 1) * HD].astype(F32)
+        parts.append(exact_dot(r_ref[g * GROUP : (g + 1) * GROUP], w, ((1,), (1,))))
+    v_ref[...] = jnp.concatenate(parts, axis=1).astype(BF16)
 
 
 def row_sum_of_transpose(a):
@@ -106,16 +127,18 @@
     )(queries, keys, x)
 
 
-def project_kernel(blocks_ref, gain_ref, x_ref, vt_ref, gvt_ref, u_ref):
-    low = lax.broadcasted_iota(jnp.int32, (16, 128), 1) < 64
-    for b in range(blocks_ref.shape[0] // 2):
-        one = blocks_ref[2 * b].astype(F32)
-        two = blocks_ref[2 * b + 1].astype(F32)
-        first = jnp.where(low, one, pltpu.roll(two, 64, 1))
-        second = jnp.where(low, pltpu.roll(one, 64, 1), two)
+def project_kernel(blocks_ref, gain_ref, x_ref, gvt_ref, u_ref):
+    low = left_lanes(8)
+    for b in range(BLOCKS // 2):
         at = slice(b * 128, (b + 1) * 128)
-        vt = jnp.concatenate([first, second], axis=0)
-        vt_ref[:, at] = vt.astype(BF16)
+        heads = []
+        for h in range(2):
+            row = (h * BLOCKS + 2 * b) * 8
+            pair = blocks_ref[row : row + 16].astype(F32)
+            one, two = pair[:8], pair[8:]
+            heads.append(jnp.where(low, one, pltpu.roll(two, 64, 1)))
+            heads.append(jnp.where(low, pltpu.roll(one, 64, 1), two))
+        vt = jnp.concatenate(heads, axis=0)
         gvt_ref[:, at] = (vt * gain_ref[:, at].astype(F32)).astype(BF16)
     u_ref[...] = lax.dot_general(
         gvt_ref[...], x_ref[...], (((1,), (1,)), ((), ())), preferred_element_type=F32
@@ -123,18 +146,8 @@
 
 
 def project(blocks, gain, x):
-    wide = x.shape[1]
-    return pl.pallas_call(
-        project_kernel,
-        in_specs=[VMEM] * 3,
-        out_specs=[VMEM] * 3,
-        out_shape=[
-            jax.ShapeDtypeStruct((32, wide), BF16),
-            jax.ShapeDtypeStruct((32, wide), BF16),
-            jax.ShapeDtypeStruct((32, x.shape[0]), F32),
-        ],
-        compiler_params=PARAMS,
-    )(blocks, gain, x)
+    length, wide = x.shape
+    return whole(project_kernel, [shape(32, wide, dtype=BF16), shape(32, length)], blocks, gain, x)
 
 
 def values_kernel(width, p_ref, own_ref, got_ref, ss_ref, v_ref, u_ref, rms_ref):
@@ -194,34 +207,59 @@
     )(probs, u, own, got, targets, scored)
 
 
-def weight_kernel(c_ref, rms_ref, gain_ref, vt_ref, x_ref, z_ref, part_ref):
+def weight_kernel(c_ref, rms_ref, x_ref, z_ref):
     c = c_ref[...] * rms_ref[...]
     high = c.astype(BF16)
     low = (c - high.astype(F32)).astype(BF16)
     both = jnp.concatenate([high, low], axis=0)
     z = jnp.dot(both, x_ref[...], preferred_element_type=F32)
     z = z[:32] + z[32:]
-    gain = gain_ref[...].astype(F32)
-    part = jnp.sum(z * vt_ref[...].astype(F32), axis=0, keepdims=True)
-    z = z * gain
-    for b in range(z_ref.shape[0]):
-        at = slice(b * 128, (b + 1) * 128)
-        z_ref[b] = z[:, at]
-        part_ref[b : b + 1] = part[:, at]
-
-
-def weight_parts(c, rms, gain, vt, x):
-    blocks = x.shape[1] // 128
-    return pl.pallas_call(
-        weight_kernel,
-        in_specs=[VMEM] * 5,
-        out_specs=[VMEM] * 2,
-        out_shape=[
-            jax.ShapeDtypeStruct((blocks, 32, 128), F32),
-            jax.ShapeDtypeStruct((blocks, 128), F32),
-        ],
-        compiler_params=PARAMS,
-    )(c, rms, gain, vt, x)
+    left = left_lanes(8)
+    for b in range(BLOCKS // 2):
+        for h in range(2):
+            one = z[h * HALF : h * HALF + 8, b * 128 : (b + 1) * 128]
+            two = z[h * HALF + 8 : h * HALF + 16, b * 128 : (b + 1) * 128]
+            first = jnp.where(left, one, pltpu.roll(two, 64, 1))
+            second = jnp.where(left, pltpu.roll(one, 64, 1), two)
+            row = (h * BLOCKS + 2 * b) * 8
+            z_ref[row : row + 16] = jnp.concatenate([first, second], axis=0).astype(BF16)
+
+
+def sum_kernel(parts_ref, gain_ref, v_ref, z_ref, part_ref):
+    total = jnp.zeros((8, 128), F32)
+    for b in range(parts_ref.shape[0] // 16):
+        pair = parts_ref[b * 16 : (b + 1) * 16].astype(F32)
+        total += pair[:8] + pair[8:]
+    z_ref[...] = total * gain_ref[...].astype(F32)
+    part = jnp.sum(total * v_ref[...].astype(F32), axis=0, keepdims=True)
+    part_ref[...] = jnp.broadcast_to(part + pltpu.roll(part, 64, 1), (8, 128))
+
+
+def outputs_kernel(z_ref, w_ref, r_ref, part_ref, grad_ref, read_ref):
+    for g in range(2):
+        z = z_ref[:, g * ROWS : (g + 1) * ROWS]
+        at = slice(g * HD, (g + 1) * HD)
+        heads = slice(g * GROUP, (g + 1) * GROUP)
+        grad_ref[:, at] = exact_dot(z, r_ref[heads], ((0,), (0,)))
+        read_ref[heads] = exact_dot(z, w_ref[:, at].astype(F32), ((1,), (0,)))
+    read_ref[HALF:] = part_ref[...]
+
+
+def last_kernel(all_ref, read_ref, gain_ref):
+    left = left_lanes(1)
+    total = all_ref[0].astype(F32)
+    for i in range(1, 64):
+        total += all_ref[i].astype(F32)
+    read_ref[...] = total[:HALF]
+    for xi in range(4):
+        for zp in range(4):
+            i = xi * 8 + 2 * zp
+            one = all_ref[i].astype(F32) + all_ref[32 + i].astype(F32)
+            two = all_ref[i + 1].astype(F32) + all_ref[33 + i].astype(F32)
+            one, two = one[HALF : HALF + 1], two[HALF : HALF + 1]
+            row = xi * 8 + zp
+            gain_ref[row : row + 1] = jnp.where(left, one, pltpu.roll(two, 64, 1))
+            gain_ref[row + 4 : row + 5] = jnp.where(left, pltpu.roll(one, 64, 1), two)
 
 
 def input_kernel(width, c_ref, dot_ref, rms_ref, gvt_ref, x_ref, out_ref, log_ref):
@@ -270,84 +308,43 @@
     )(c, dot, rms, gvt, x)
 
 
-def reduce_rows(z, part):
-    zi = lax.axis_index("z")
-    xi = lax.axis_index("x")
-    core = lax.axis_index("core")
-
-    def step(v, part, bit, axis, name, to):
-        keep, send = split(bit, v, axis)
-        n = send.size // 4096
-        sent = jnp.concatenate([send.reshape(n, 32, 128), part[None]], axis=0)
-        got = swap(sent, name, to)
-        return keep + got[:n].reshape(keep.shape), part + got[n]
-
-    z = z.reshape(4, 2, 4, 32, 128)
-    z, part = step(z, part, core == 1, 1, "core", next_door)
-    z, part = step(z, part, xi >= 2, 0, "x", mirror_four)
-    z, part = step(z, part, xi % 2 == 1, 0, "x", next_door)
-    z = z.reshape(4, 32, 128)
-    z, part = step(z, part, zi >= 4, 0, "z", mirror_eight)
-    z, part = step(z, part, zi % 4 >= 2, 0, "z", two_off)
-    z = z[0]
-    keep, send = split(zi % 2 == 1, z, 1)
-    got = swap(jnp.concatenate([send, part.reshape(64, 64)], axis=0), "z", next_door)
-    z = keep + got[:32]
-    part = part.reshape(64, 64) + got[32:]
-    keep, send = split(lax.axis_index("yh") == 1, z, 0)
-    got = swap(jnp.concatenate([send, part], axis=0), "yh", next_door)
-    z = cross(keep + got[:16])
-    return z, (part + got[16:]).reshape(-1)
-
-
-def all_reduce(v):
-    v = v + swap(v, "core", next_door)
-    v = v + swap(v, "x", next_door)
-    v = v + swap(v, "x", mirror_four)
-    v = v + swap(v, "z", next_door)
-    v = v + swap(v, "z", two_off)
-    v = v + swap(v, "z", mirror_eight)
-    return v + swap(v, "yh", next_door)
-
-
 def shards(hidden_states, norm_gain, value_weight, queries, keys, readout, targets, scored):
     x = hidden_states
     length = x.shape[0]
     width = x.shape[1] * 2
-    yh = lax.axis_index("yh")
     yl = lax.axis_index("yl")
+    core = lax.axis_index("core")
     gain = norm_gain[None]
     rows = value_weight.shape[0]
-    w3 = value_weight.reshape(rows, 2, HD)
-    r3 = readout.reshape(2, GROUP, HD)
-    v = jnp.einsum("igd,gjd->gji", w3.astype(F32), r3, precision=HIGHEST)
-    v = v.reshape(2 * GROUP, rows).astype(BF16)
-
+    read = readout.reshape(HALF, HD)
+    v = cross(whole(read_kernel, shape(8, 128, dtype=BF16), value_weight, read))
+    blocks = lax.all_to_all(jnp.broadcast_to(v, (128, 8, 128)), SEQ, 0, 0)
     probs, ss = make_probs(queries, keys, x)
-
-    v = cross(v)
-    other = swap(v, "yh", next_door)
-    v = jnp.concatenate([jnp.where(yh == 0, v, other), jnp.where(yh == 0, other, v)], axis=1)
-    blocks = lax.all_to_all(
-        jnp.broadcast_to(v, (64,) + v.shape), ("x", "core", "z"), 0, 0
-    )
-    vt, gvt, u = project(blocks, gain, x)
+    gvt, u = project(blocks.reshape(1024, 128), gain, x)
     own, send = split(yl == 1, u, 0)
-    got = swap(jnp.concatenate([send, jnp.broadcast_to(ss, (8, length))], axis=0), "yl", next_door)
+    got = swap(jnp.concatenate([send, jnp.broadcast_to(ss, (8, length))], axis=0), "yl")
     part_values, u, rms = make_values(width, probs, own, got, ss)
-    got = swap(part_values, "yl", next_door)
+    got = swap(part_values, "yl")
     values, c = make_error(probs, u, part_values, got, targets[None], scored[None])
-    got = swap(c, "yl", next_door)
+    got = swap(c, "yl")
     dot = c[16:17] + got[16:17]
     c = jnp.concatenate([jnp.where(yl == 0, c[:16], got[:16]), jnp.where(yl == 0, got[:16], c[:16])], axis=0)
-    z, part = weight_parts(c, rms, gain, vt, x)
+    z = whole(weight_kernel, shape(1024, 128, dtype=BF16), c, rms, x)
+    z = lax.all_to_all(z.reshape(128, 8, 128), SEQ, 0, 0).reshape(1024, 128)
     grad_input, log_scale = input_grad(width, c, dot, rms, gvt, x)
-    z, grad_gain = reduce_rows(z, part)
-    z3 = z.reshape(2, GROUP, rows)
-    grad_weight = jnp.einsum("gji,gjd->igd", z3, r3, precision=HIGHEST).reshape(rows, 2 * HD)
-    read_part = jnp.einsum("gji,igd->gjd", z3, w3.astype(F32), precision=HIGHEST)
-    grad_readout = all_reduce(read_part.reshape(16, HD)).reshape(-1)
-    return (values[0], grad_input, grad_weight, grad_gain, grad_readout, log_scale[0])
+    at = (lax.axis_index("x") * 2 + core) * 8 + lax.axis_index("z")
+    own_gain = lax.dynamic_slice(norm_gain, (at * rows,), (rows,))
+    own_gain = jnp.concatenate([own_gain, own_gain])[None]
+    z, part = whole(sum_kernel, [shape(8, 128), shape(8, 128)], z, own_gain, v)
+    grad_weight, tail = whole(
+        outputs_kernel, [shape(rows, 2 * HD), shape(HALF + 8, 128)], cross(z), value_weight, read, part
+    )
+    got = swap(tail, "core")
+    pair = jnp.where((jnp.arange(128) < 64) == (core == 0), tail[HALF:], got[HALF:])
+    tail = jnp.concatenate([tail[:HALF] + got[:HALF], pair], axis=0).astype(BF16)
+    tails = lax.all_to_all(jnp.broadcast_to(tail, (64,) + tail.shape), ("yh", "x", "z"), 0, 0)
+    grad_readout, grad_gain = whole(last_kernel, [shape(HALF, HD), shape(32, 128)], tails)
+    return (values[0], grad_input, grad_weight, grad_gain.reshape(-1), grad_readout.reshape(-1), log_scale[0])
 
 
 def solution(mesh):

time: 126 us -> 109 us (0.87)
  starting transfers between devices: 46.1 us -> 37.8 us
  waiting for transfers between devices: 56.7 us -> 48.8 us
  other arithmetic: 3.27 us -> 0.14 us
  Pallas kernels: 8.1 us -> 10.9 us
  matrix products: 1.26 us -> 0 us
    ppermute x18 -> x4, waiting for transfers between devices: 52.8 us -> 12.3 us  [swap(): return lax.ppermute(v, axis, [(0, 1), (1, 0)])]
    ppermute x18 -> x4, starting transfers between devices: 33.1 us -> 0.26 us  [swap(): return lax.ppermute(v, axis, [(0, 1), (1, 0)])]
    all_to_all x1 -> x3, waiting for transfers between devices: 3.86 us -> 36.4 us  [the longest x1 14.8 us: shards(): z = lax.all_to_all(z.reshape(128, 8, 128), SEQ, 0, 0).reshape(1024, 128)]
    all_to_all x1 -> x3, starting transfers between devices: 11.6 us -> 36.1 us  [the longest x1 19.8 us: shards(): blocks = lax.all_to_all(jnp.broadcast_to(v, (128, 8, 128)), SEQ, 0, 0)]
    pallas_call x2 -> x6, Pallas kernels: 1.24 us -> 4.05 us  [whole(): pl.pallas_call(body, in_specs=[VMEM] * len(args), out_specs=[VMEM] * len(...]
    concatenate x8 -> x1, other arithmetic: 1.52 us -> 0.01 us  [shards(): jnp.concatenate([tail[:HALF] + got[:HALF], pair], axis=0).astype(BF16)]
    reshape x3 -> x0, local copies, waits for them, and re-layouts: 1.39 us -> none  [the longest x1 0.68 us: reduce_rows(): return (z, (part + got[16:]).reshape(-1))]
    unnamed x22 -> x24, local copies, waits for them, and re-layouts: 6.39 us -> 6.5 us
  transfers between devices with their start and end apart: 21 -> 9, of which waited for: 19 -> 7; matrix products, arithmetic and copies ran while one was open for 2% -> 1% of each run, Pallas kernels for 5% -> 5%
where the time goes in v2:
time: 109 us; the launch traced here: 108 us
  waiting for transfers between devices  48.8 us (45%)
  starting transfers between devices  37.8 us (35%)
  Pallas kernels  10.9 us (10%)
  local copies, waits for them, and re-layouts  9.49 us (9%)
    all_to_all x1, starting transfers between devices, shards(): blocks = lax.all_to_all(jnp.broadcast_to(v, (128, 8, 128)), SEQ, 0, 0)  19.8 us
    all_to_all x1, waiting for transfers between devices, shards(): z = lax.all_to_all(z.reshape(128, 8, 128), SEQ, 0, 0).reshape(1024, 128)  14.8 us
    all_to_all x1, waiting for transfers between devices, shards(): lax.all_to_all(jnp.broadcast_to(tail, (64,) + tail.shape), ('yh', 'x', 'z...  14.7 us
    ppermute x4, waiting for transfers between devices, swap(): return lax.ppermute(v, axis, [(0, 1), (1, 0)])  12.3 us
    all_to_all x1, starting transfers between devices, shards(): lax.all_to_all(jnp.broadcast_to(tail, (64,) + tail.shape), ('yh', 'x', 'z...  9.26 us
    all_to_all x1, starting transfers between devices, shards(): z = lax.all_to_all(z.reshape(128, 8, 128), SEQ, 0, 0).reshape(1024, 128)  7.05 us
    all_to_all x1, waiting for transfers between devices, shards(): blocks = lax.all_to_all(jnp.broadcast_to(v, (128, 8, 128)), SEQ, 0, 0)  6.87 us
    unnamed x24, local copies, waits for them, and re-layouts  6.5 us
  transfers between devices with their start and end apart: 9, of which 7 were waited for; matrix products, arithmetic and copies ran while one was open for 1% of the time, Pallas kernels for 5%

profile of v2, /device:TPU:32, one launch (start us, length us, event | category | flops | bytes accessed | tf_op | source)
XLA Modules:
  0.0 108.0 jit_solution(10221140070634339817)
XLA Ops:
  0.6 0.0 copy-start.6
  0.6 0.7 copy-done.6
  1.4 0.0 copy-start.8
  1.4 0.7 copy-done.8
  2.1 0.2 shard_map.128
  2.3 0.7 collective-permute-start
  3.0 0.0 collective-permute-done.v_ref
  3.0 0.7 broadcast_in_dim.29
  3.8 19.8 %all-to-all-start = ((bf16[128,8,128]{2,1,0:T(8,128)(2,1)}), bf16[128,8,128]{2,1,0:T(8,128)(2,1)S(1)}, u32[]{:S(2)}, u32[]{:S(2)}) async-start(bf16[128,8,128]{2,1,0:T(8,128)(2,1)} %broadcast_in_dim.29), calls=%async_computation | async-start | bytes 524288 | tf_op jit(solution)/shard_map/all_to_all | solution.py:321
  23.6 0.7 broadcast_in_dim.30.gain_ref
  24.3 0.0 copy-start
  24.3 1.6 %copy-done = bf16[256,4096]{1,0:T(8,128)(2,1)S(1)} copy-done((bf16[256,4096]{1,0:T(8,128)(2,1)S(1)}, bf16[256,4096]{1,0:T(8,128)(2,1)}, u32[]{:S(2)}) %copy-start) | copy-done | bytes 2097176
  25.9 0.0 copy-start.4
  25.9 1.2 %copy-done.4 = bf16[256,2048]{1,0:T(8,128)(2,1)S(1)} copy-done((bf16[256,2048]{1,0:T(8,128)(2,1)S(1)}, bf16[256,2048]{1,0:T(8,128)(2,1)}, u32[]{:S(2)}) %copy-start.4) | copy-done | bytes 1048600
  27.1 0.0 copy-start.5
  27.1 0.9 copy-done.5
  28.0 0.0 copy-start.1
  28.0 3.0 %shard_map.127 = (bf16[16,256,256]{2,1,0:T(8,128)(2,1)S(1)}, f32[1,256]{1,0:T(1,128)S(1)}) custom-call(bf16[256,2048]{1,0:T(8,128)(2,1)S(1)} %copy-done.4, bf16[256,256]{1,0:T(8,128)(2,1)S(1)} %copy-done.5, bf16[256,4096]{1,0:T(8,128)(2,1)S(1)} %copy-done), custom_call_target="tpu_custom_call" | custom-call | tf_op jit(solution)/shard_map/pallas_call | solution.py:109
  31.1 0.0 copy-start.2
  31.1 1.3 %copy-done.2 = bf16[16,256,256]{2,1,0:T(8,128)(2,1)} copy-done((bf16[16,256,256]{2,1,0:T(8,128)(2,1)}, bf16[16,256,256]{2,1,0:T(8,128)(2,1)S(1)}, u32[]{:S(2)}) %copy-start.2) | copy-done | bytes 2097176
  32.4 6.9 %all-to-all-done = bf16[128,8,128]{2,1,0:T(8,128)(2,1)S(1)} async-done(((bf16[128,8,128]{2,1,0:T(8,128)(2,1)}), bf16[128,8,128]{2,1,0:T(8,128)(2,1)S(1)}, u32[]{:S(2)}, u32[]{:S(2)}) %all-to-all-start) | async-done | bytes 262176 | tf_op jit(solution)/shard_map/all_to_all | solution.py:321
  39.2 0.0 copy-start.3
  39.3 0.0 copy-done.1
  39.3 0.0 copy-start.10
  39.3 0.0 copy-start.11
  39.3 0.8 shard_map.129
  40.1 0.1 collective-permute-start.1
  40.2 3.8 %collective-permute-done.1.refs_2_ = f32[24,256]{1,0:T(8,128)S(1)} collective-permute-done((f32[24,256]{1,0:T(8,128)S(1)}, f32[24,256]{1,0:T(8,128)S(1)}, u32[]{:S(2)}, u32[]{:S(2)}) %collective-permute-start.1) | collective-permute-done | bytes 24608 | tf_op jit(solution)/shard_map/ppermute | solution.py:26
  44.0 0.0 copy-done.3
  44.0 0.6 shard_map.130
  44.5 0.1 collective-permute-start.2
  44.6 3.6 %collective-permute-done.2.got_ref = f32[1,256]{1,0:T(1,128)S(1)} collective-permute-done((f32[1,256]{1,0:T(1,128)S(1)}, f32[1,256]{1,0:T(1,128)S(1)}, u32[]{:S(2)}, u32[]{:S(2)}) %collective-permute-start.2) | collective-permute-done | bytes 1056 | tf_op jit(solution)/shard_map/ppermute | solution.py:26
  48.2 0.0 copy-done.10
  48.2 0.0 copy-done.11
  48.2 0.6 shard_map.131
  48.8 0.0 copy-start.7
  48.8 0.0 copy-start.9
  48.8 0.1 collective-permute-start.3
  48.9 3.8 %collective-permute-done.3 = f32[24,256]{1,0:T(8,128)S(1)} collective-permute-done((f32[24,256]{1,0:T(8,128)S(1)}, f32[24,256]{1,0:T(8,128)S(1)}, u32[]{:S(2)}, u32[]{:S(2)}) %collective-permute-start.3) | collective-permute-done | bytes 24608 | tf_op jit(solution)/shard_map/ppermute | solution.py:26
  52.7 1.3 %shard_map.133 = bf16[1024,128]{1,0:T(8,128)(2,1)} custom-call(f32[32,256]{1,0:T(8,128)S(1)} %pad_maximum_fusion.refs_0_.c_ref, f32[1,256]{1,0:T(1,128)S(1)} %get-tuple-element.30.refs_2_.rms_ref, bf16[256,4096]{1,0:T(8,128)(2,1)S(1)} %copy-done.1), custom_call_target="tpu_custom_call" | custom-call | tf_op jit(solution)/shard_map/pallas_call | solution.py:42
  53.9 7.1 %all-to-all-start.1 = ((bf16[128,8,128]{2,1,0:T(8,128)(2,1)}), bf16[128,8,128]{2,1,0:T(8,128)(2,1)S(1)}, u32[]{:S(2)}, u32[]{:S(2)}) async-start(bf16[128,8,128]{2,1,0:T(8,128)(2,1)} %bitcast.6), calls=%async_computation.1 | async-start | bytes 524288 | tf_op jit(solution)/shard_map/all_to_all | solution.py:333
  61.0 0.8 dynamic_slice.3
  61.8 0.1 maximum_bitcast_fusion.gain_ref
  61.9 14.8 %all-to-all-done.1 = bf16[128,8,128]{2,1,0:T(8,128)(2,1)S(1)} async-done(((bf16[128,8,128]{2,1,0:T(8,128)(2,1)}), bf16[128,8,128]{2,1,0:T(8,128)(2,1)S(1)}, u32[]{:S(2)}, u32[]{:S(2)}) %all-to-all-start.1) | async-done | bytes 262176 | tf_op jit(solution)/shard_map/all_to_all | solution.py:333
  76.7 0.1 shard_map.134
  76.8 0.7 collective-permute-start.4
  77.5 0.0 collective-permute-done.4.z_ref
  77.5 0.0 copy-done.7
  77.5 0.0 copy-done.9
  77.5 1.0 shard_map.135
  78.5 0.0 collective-permute-start.5
  78.5 1.2 %collective-permute-done.5 = f32[24,128]{1,0:T(8,128)S(1)} collective-permute-done((f32[24,128]{1,0:T(8,128)S(1)}, f32[24,128]{1,0:T(8,128)S(1)}, u32[]{:S(2)}, u32[]{:S(2)}) %collective-permute-start.5) | collective-permute-done | bytes 12320 | tf_op jit(solution)/shard_map/ppermute | solution.py:26
  79.7 0.8 broadcast_in_dim.37
  80.5 9.3 %all-to-all-start.2 = ((bf16[64,24,128]{2,1,0:T(8,128)(2,1)}), bf16[64,24,128]{2,1,0:T(8,128)(2,1)S(1)}, u32[]{:S(2)}, u32[]{:S(2)}) async-start(bf16[64,24,128]{2,1,0:T(8,128)(2,1)} %broadcast_in_dim.37), calls=%async_computation.2 | async-start | bytes 786432 | tf_op jit(solution)/shard_map/all_to_all | solution.py:345
  89.8 2.7 %shard_map.132 = (bf16[256,4096]{1,0:T(8,128)(2,1)}, f32[1,256]{1,0:T(1,128)}) custom-call(f32[32,256]{1,0:T(8,128)S(1)} %pad_maximum_fusion.refs_0_.c_ref, f32[1,256]{1,0:T(1,128)S(1)} %slice_add_fusion.1.refs_1_, f32[1,256]{1,0:T(1,128)S(1)} %get-tuple-element.30.refs_2_.rms_ref, bf16[32,4096]{1,0:T(8,128)(2,1)S(1)} %get-tuple-element.31.refs_3_, ...), custom_call_target="tpu_custom_call" | custom-call | tf_op jit(solution)/shard_map/pallas_call | solution.py:289
  92.5 14.7 %all-to-all-done.2.all_ref = bf16[64,24,128]{2,1,0:T(8,128)(2,1)S(1)} async-done(((bf16[64,24,128]{2,1,0:T(8,128)(2,1)}), bf16[64,24,128]{2,1,0:T(8,128)(2,1)S(1)}, u32[]{:S(2)}, u32[]{:S(2)}) %all-to-all-start.2) | async-done | bytes 393248 | tf_op jit(solution)/shard_map/all_to_all | solution.py:345
  107.2 0.7 shard_map.136
  (10 shorter events, 0.1 us)
Async XLA Ops:
  0.6 0.8 copy-start.6
  1.4 0.7 copy-start.8
  2.3 0.7 collective-permute-start
  3.8 35.5 %all-to-all-start = ((bf16[128,8,128]{2,1,0:T(8,128)(2,1)}), bf16[128,8,128]{2,1,0:T(8,128)(2,1)S(1)}, u32[]{:S(2)}, u32[]{:S(2)}) async-start(bf16[128,8,128]{2,1,0:T(8,128)(2,1)} %broadcast_in_dim.29), calls=%async_computation | async-start | bytes 524288 | tf_op jit(solution)/shard_map/all_to_all | solution.py:321
  24.3 1.6 %copy-start = (bf16[256,4096]{1,0:T(8,128)(2,1)S(1)}, bf16[256,4096]{1,0:T(8,128)(2,1)}, u32[]{:S(2)}) copy-start(bf16[256,4096]{1,0:T(8,128)(2,1)} %x_ref.5) | copy-start | bytes 6291460
  25.9 1.2 %copy-start.4 = (bf16[256,2048]{1,0:T(8,128)(2,1)S(1)}, bf16[256,2048]{1,0:T(8,128)(2,1)}, u32[]{:S(2)}) copy-start(bf16[256,2048]{1,0:T(8,128)(2,1)} %q_ref.1) | copy-start | bytes 3145732
  27.1 0.9 copy-start.5
  28.0 11.2 %copy-start.1 = (bf16[256,4096]{1,0:T(8,128)(2,1)S(1)}, bf16[256,4096]{1,0:T(8,128)(2,1)}, u32[]{:S(2)}) copy-start(bf16[256,4096]{1,0:T(8,128)(2,1)} %x_ref.5) | copy-start | bytes 6291460
  31.1 1.3 %copy-start.2 = (bf16[16,256,256]{2,1,0:T(8,128)(2,1)}, bf16[16,256,256]{2,1,0:T(8,128)(2,1)S(1)}, u32[]{:S(2)}) copy-start(bf16[16,256,256]{2,1,0:T(8,128)(2,1)S(1)} %get-tuple-element.23.refs_0_.p_ref) | copy-start | bytes 6291460
  39.2 4.7 %copy-start.3 = (bf16[16,256,256]{2,1,0:T(8,128)(2,1)S(1)}, bf16[16,256,256]{2,1,0:T(8,128)(2,1)}, u32[]{:S(2)}) copy-start(bf16[16,256,256]{2,1,0:T(8,128)(2,1)} %copy-done.2) | copy-start | bytes 6291460
  39.3 8.9 %copy-start.10 = (f32[256]{0:T(256)S(1)}, f32[256]{0:T(256)}, u32[]{:S(2)}) copy-start(f32[256]{0:T(256)} %param.14) | copy-start | bytes 3076
  39.3 8.9 %copy-start.11 = (s32[256]{0:T(256)S(1)}, s32[256]{0:T(256)}, u32[]{:S(2)}) copy-start(s32[256]{0:T(256)} %param.15) | copy-start | bytes 3076
  40.1 3.9 %collective-permute-start.1 = (f32[24,256]{1,0:T(8,128)S(1)}, f32[24,256]{1,0:T(8,128)S(1)}, u32[]{:S(2)}, u32[]{:S(2)}) collective-permute-start(f32[24,256]{1,0:T(8,128)S(1)} %pad_maximum_fusion.1), channel_id=1, source_target_pairs={{0,1},{1,0},{2,3},{3,2},{4,5},{5,4},{6,7},{7,6},{8,9},{9,8},{10,11... | collective-permute-start | bytes 73736 | tf_op jit(solution)/shard_map/ppermute | solution.py:26
  44.5 3.7 %collective-permute-start.2 = (f32[1,256]{1,0:T(1,128)S(1)}, f32[1,256]{1,0:T(1,128)S(1)}, u32[]{:S(2)}, u32[]{:S(2)}) collective-permute-start(f32[1,256]{1,0:T(1,128)S(1)} %get-tuple-element.27.own_ref), channel_id=1, source_target_pairs={{0,1},{1,0},{2,3},{3,2},{4,5},{5,4},{6,7},{7,6},{8,9},{9,8},{10,11... | collective-permute-start | bytes 3080 | tf_op jit(solution)/shard_map/ppermute | solution.py:26
  48.8 28.7 %copy-start.7 = (bf16[64,256]{1,0:T(8,128)(2,1)S(1)}, bf16[64,256]{1,0:T(8,128)(2,1)}, u32[]{:S(2)}) copy-start(bf16[64,256]{1,0:T(8,128)(2,1)} %w_ref.3) | copy-start | bytes 98308
  48.8 28.7 %copy-start.9 = (f32[2048]{0:T(1024)S(1)}, f32[2048]{0:T(1024)}, u32[]{:S(2)}) copy-start(f32[2048]{0:T(1024)} %param.13) | copy-start | bytes 24580
  48.8 3.9 %collective-permute-start.3 = (f32[24,256]{1,0:T(8,128)S(1)}, f32[24,256]{1,0:T(8,128)S(1)}, u32[]{:S(2)}, u32[]{:S(2)}) collective-permute-start(f32[24,256]{1,0:T(8,128)S(1)} %get-tuple-element.29), channel_id=1, source_target_pairs={{0,1},{1,0},{2,3},{3,2},{4,5},{5,4},{6,7},{7,6},{8,9},{9,8},{10,11... | collective-permute-start | bytes 73736 | tf_op jit(solution)/shard_map/ppermute | solution.py:26
  53.9 22.7 %all-to-all-start.1 = ((bf16[128,8,128]{2,1,0:T(8,128)(2,1)}), bf16[128,8,128]{2,1,0:T(8,128)(2,1)S(1)}, u32[]{:S(2)}, u32[]{:S(2)}) async-start(bf16[128,8,128]{2,1,0:T(8,128)(2,1)} %bitcast.6), calls=%async_computation.1 | async-start | bytes 524288 | tf_op jit(solution)/shard_map/all_to_all | solution.py:333
  76.8 0.7 collective-permute-start.4
  78.5 1.2 %collective-permute-start.5 = (f32[24,128]{1,0:T(8,128)S(1)}, f32[24,128]{1,0:T(8,128)S(1)}, u32[]{:S(2)}, u32[]{:S(2)}) collective-permute-start(f32[24,128]{1,0:T(8,128)S(1)} %get-tuple-element.36), channel_id=1, source_target_pairs={{0,16},{16,0},{1,17},{17,1},{2,18},{18,2},{3,19},{19,3},{4,20},{20... | collective-permute-start | bytes 36872 | tf_op jit(solution)/shard_map/ppermute | solution.py:26
  80.5 26.7 %all-to-all-start.2 = ((bf16[64,24,128]{2,1,0:T(8,128)(2,1)}), bf16[64,24,128]{2,1,0:T(8,128)(2,1)S(1)}, u32[]{:S(2)}, u32[]{:S(2)}) async-start(bf16[64,24,128]{2,1,0:T(8,128)(2,1)} %broadcast_in_dim.37), calls=%async_computation.2 | async-start | bytes 786432 | tf_op jit(solution)/shard_map/all_to_all | solution.py:345

commit v3 on v2

v3 whole, which is shorter than its diff:
```python
import jax
import jax.numpy as jnp
from jax import lax
from jax.experimental import pallas as pl
from jax.experimental.pallas import tpu as pltpu
from jax.sharding import Mesh
from jax.sharding import PartitionSpec as P

HD = 128
GROUP = 8
EPS = 1e-06
F32 = jnp.float32
BF16 = jnp.bfloat16
HIGHEST = lax.Precision.HIGHEST
VMEM = pl.BlockSpec(memory_space=pltpu.VMEM)
HBM = pl.BlockSpec(memory_space=pltpu.HBM)
ANY = pl.BlockSpec(memory_space=pl.ANY)
PARAMS = pltpu.CompilerParams(vmem_limit_bytes=16 * 1024 * 1024)


FAR = ("yh", "x", "z")
PLANE = ("x", "z")
NEAR = ("yh", "core", "yl")
ROWS = 64
BLOCKS = 64
HALF = 16


def swap(v, axis):
    return lax.ppermute(v, axis, [(0, 1), (1, 0)])


def cross(v):
    return lax.ppermute(v, ("yh", "yl"), [(0, 0), (1, 2), (2, 1), (3, 3)])


def split(bit, v, axis):
    n = v.shape[axis] // 2
    low = lax.slice_in_dim(v, 0, n, axis=axis)
    high = lax.slice_in_dim(v, n, 2 * n, axis=axis)
    return jnp.where(bit, high, low), jnp.where(bit, low, high)


def whole(body, out_shape, *args, scratch=()):
    many = isinstance(out_shape, list)
    return pl.pallas_call(
        body,
        in_specs=[VMEM] * len(args),
        out_specs=[VMEM] * len(out_shape) if many else VMEM,
        out_shape=out_shape,
        scratch_shapes=scratch,
        compiler_params=PARAMS,
    )(*args)


def shape(*dims, dtype=F32):
    return jax.ShapeDtypeStruct(dims, dtype)


def exact_dot(a, b, dims):
    return lax.dot_general(a, b, (dims, ((), ())), precision=HIGHEST, preferred_element_type=F32)


def left_lanes(rows):
    return lax.broadcasted_iota(jnp.int32, (rows, 128), 1) < 64


def read_kernel(w_ref, r_ref, v_ref, wv_ref, rv_ref, sems):
    copies = [
        pltpu.make_async_copy(w_ref, wv_ref, sems.at[0]),
        pltpu.make_async_copy(r_ref, rv_ref, sems.at[1]),
    ]
    for copy in copies:
        copy.start()
    for copy in copies:
        copy.wait()
    parts = []
    for g in range(2):
        w = wv_ref[:, g * HD : (g + 1) * HD].astype(F32)
        parts.append(exact_dot(rv_ref[g * GROUP : (g + 1) * GROUP], w, ((1,), (1,))))
    v = jnp.concatenate(parts, axis=1)
    v = jnp.concatenate([v, v], axis=0).astype(BF16)
    for i in range(32):
        v_ref[i * 16 : (i + 1) * 16] = v


def read_weight(w, read):
    return pl.pallas_call(
        read_kernel,
        in_specs=[HBM] * 2,
        out_specs=VMEM,
        out_shape=shape(512, 128, dtype=BF16),
        scratch_shapes=[
            pltpu.VMEM(w.shape, BF16), pltpu.VMEM(read.shape, F32), pltpu.SemaphoreType.DMA((2,))
        ],
        compiler_params=PARAMS,
    )(w, read)


def row_sum_of_transpose(a):
    return jnp.sum(a.T, axis=0, keepdims=True)


def attention(q_ref, k_ref, p_ref):
    length = q_ref.shape[0]
    rows = lax.broadcasted_iota(jnp.int32, (length, length), 0)
    cols = lax.broadcasted_iota(jnp.int32, (length, length), 1)
    allowed = cols <= rows
    for h in range(HALF):
        g = h // GROUP
        s = lax.dot_general(
            q_ref[:, h * HD : (h + 1) * HD],
            k_ref[:, g * HD : (g + 1) * HD],
            (((1,), (1,)), ((), ())),
            preferred_element_type=F32,
        )
        s = jnp.where(allowed, s * (HD**-0.5), -1e30)
        e = jnp.exp(s - jnp.max(s, axis=1, keepdims=True))
        p_ref[h] = (e / jnp.sum(e, axis=1, keepdims=True)).astype(BF16)


def early_kernel(x_ref, q_ref, k_ref, after_ref, xv_ref, p_ref, ss_ref, qv_ref, kv_ref, sems):
    copies = [
        pltpu.make_async_copy(q_ref, qv_ref, sems.at[0]),
        pltpu.make_async_copy(k_ref, kv_ref, sems.at[1]),
        pltpu.make_async_copy(x_ref, xv_ref, sems.at[2]),
    ]
    for copy in copies:
        copy.start()
    copies[0].wait()
    copies[1].wait()
    attention(qv_ref, kv_ref, p_ref)
    copies[2].wait()
    total = jnp.zeros((xv_ref.shape[0], 128), F32)
    for b in range(xv_ref.shape[1] // 128):
        xb = xv_ref[:, b * 128 : (b + 1) * 128].astype(F32)
        total += xb * xb
    ss_ref[...] = row_sum_of_transpose(total)


def early(x, queries, keys, after):
    length = x.shape[0]
    return pl.pallas_call(
        early_kernel,
        in_specs=[HBM] * 3 + [ANY],
        out_specs=[VMEM] * 3,
        out_shape=[shape(*x.shape, dtype=BF16), shape(HALF, length, length, dtype=BF16), shape(1, length)],
        scratch_shapes=[
            pltpu.VMEM(queries.shape, BF16), pltpu.VMEM(keys.shape, BF16), pltpu.SemaphoreType.DMA((3,))
        ],
        compiler_params=PARAMS,
    )(x, queries, keys, after)


def project_kernel(
    own_ref, own_y_ref, got_ref, got_y_ref, gain_ref, x_ref, ss_ref, gvt_ref, u_ref, send_ref
):
    core = lax.axis_index("core")
    low = left_lanes(8)
    for b in range(BLOCKS // 2):
        xi, c, zp = b // 8, b // 4 % 2, b % 4
        at = slice(b * 128, (b + 1) * 128)
        row = (xi * 8 + 2 * zp) * 8
        halves = []
        for here, there in ((own_ref, got_ref), (own_y_ref, got_y_ref)):
            pair = jnp.where(
                core == c, here[row : row + 16].astype(F32), there[row : row + 16].astype(F32)
            )
            one, two = pair[:8], pair[8:]
            halves.append(jnp.where(low, one, pltpu.roll(two, 64, 1)))
            halves.append(jnp.where(low, pltpu.roll(one, 64, 1), two))
        vt = jnp.concatenate(halves, axis=0)
        gvt_ref[:, at] = (vt * gain_ref[:, at].astype(F32)).astype(BF16)
    u = lax.dot_general(
        gvt_ref[...], x_ref[...], (((1,), (1,)), ((), ())), preferred_element_type=F32
    )
    u_ref[...] = u[:HALF]
    send_ref[:HALF] = u[HALF:]
    send_ref[HALF:] = jnp.broadcast_to(ss_ref[...], (8, u.shape[1]))


def project(vs, gain, x, ss):
    length, wide = x.shape
    return whole(
        project_kernel,
        [shape(32, wide, dtype=BF16), shape(HALF, length), shape(HALF + 8, length)],
        *vs, gain, x, ss,
    )


def values_kernel(width, p_ref, own_ref, got_ref, ss_ref, v_ref, u_ref, rms_ref):
    got = got_ref[...]
    rms = lax.rsqrt((ss_ref[...] + got[HALF : HALF + 1]) / width + EPS)
    rms_ref[...] = rms
    u = own_ref[...] + got[:HALF]
    u_ref[...] = u
    u = u * rms
    total = jnp.zeros(p_ref.shape[1:], F32)
    for j in range(HALF):
        total += p_ref[j].astype(F32) * u[j : j + 1]
    v_ref[...] = row_sum_of_transpose(total)


def make_values(width, probs, own, got, ss):
    length = probs.shape[1]
    return whole(
        lambda *refs: values_kernel(width, *refs),
        [shape(1, length), shape(HALF, length), shape(1, length)],
        probs, own, got, ss,
    )


def error_kernel(p_ref, u_ref, own_ref, got_ref, targets_ref, scored_ref, values_ref, c_ref):
    length = u_ref.shape[1]
    values = own_ref[...] + got_ref[...]
    values_ref[...] = values
    error = (values - targets_ref[...]) * scored_ref[...].astype(F32)
    spread = jnp.broadcast_to(error, (length, length)).T
    rows = [jnp.sum(p_ref[j].astype(F32) * spread, axis=0, keepdims=True) for j in range(HALF)]
    c = jnp.concatenate(rows, axis=0)
    c_ref[:HALF] = c
    c_ref[HALF:] = jnp.broadcast_to(jnp.sum(c * u_ref[...], axis=0, keepdims=True), (8, length))


def make_error(probs, u, own, got, targets, scored):
    length = probs.shape[1]
    return whole(
        error_kernel, [shape(1, length), shape(HALF + 8, length)], probs, u, own, got, targets, scored
    )


def rows_kernel(own_ref, got_ref, rms_ref, x_ref, c_ref, dot_ref, keep_ref, send_ref):
    core = lax.axis_index("core")
    c = jnp.concatenate([own_ref[:HALF], got_ref[:HALF]], axis=0) * rms_ref[...]
    c_ref[...] = c
    dot_ref[...] = own_ref[HALF : HALF + 1] + got_ref[HALF : HALF + 1]
    high = c.astype(BF16)
    low = (c - high.astype(F32)).astype(BF16)
    both = jnp.concatenate([high, low], axis=0)
    z = jnp.dot(both, x_ref[...], preferred_element_type=F32)
    z = z[:32] + z[32:]
    left = left_lanes(8)

    def chunks(b):
        at = slice(b * 128, (b + 1) * 128)
        parts = [z[i * 8 : (i + 1) * 8, at] for i in range(4)]
        even = [jnp.where(left, parts[i], pltpu.roll(parts[i + 1], 64, 1)) for i in (0, 2)]
        odd = [jnp.where(left, pltpu.roll(parts[i], 64, 1), parts[i + 1]) for i in (0, 2)]
        return jnp.concatenate([*even, *odd], axis=0)

    for xi in range(4):
        for zp in range(4):
            at = pl.ds((xi * 4 + zp) * 32, 32)
            zero, one = chunks(xi * 8 + zp), chunks(xi * 8 + 4 + zp)
            keep_ref[at] = jnp.where(core == 0, zero, one)
            send_ref[at] = jnp.where(core == 0, one, zero)


def make_rows(own, got, rms, x):
    length = x.shape[0]
    return whole(
        rows_kernel,
        [shape(32, length), shape(1, length), shape(512, 128), shape(512, 128)],
        own, got, rms, x,
    )


def pick_kernel(v_ref, own_ref, send_ref):
    side = lax.axis_index("yl")
    own_ref[...] = v_ref[pl.ds(pl.multiple_of(side * 256, 256), 256)]
    send_ref[...] = v_ref[pl.ds(pl.multiple_of((1 - side) * 256, 256), 256)]


def sum_kernel(parts_ref, gain_ref, own_ref, own_y_ref, w_ref, w_other_ref, tails_ref):
    side = lax.axis_index("yl")
    straight = lax.axis_index("yh") == side
    xi, zi = lax.axis_index("x"), lax.axis_index("z")
    even = zi % 2 == 0
    at = pl.ds(pl.multiple_of((xi * 4 + zi // 2) * 16, 16), 16)
    vs = []
    for ref in (own_ref, own_y_ref):
        pair = ref[at].astype(F32)
        vs.append(jnp.where(even, pair[:8], pair[8:]))
    v = jnp.concatenate(vs, axis=0)
    spot = (xi * 2 + lax.axis_index("core")) * 4 + zi // 2
    gain = jnp.zeros((1, 128), F32)
    for b in range(BLOCKS // 2):
        gain = jnp.where(spot == b, gain_ref[:, b * 128 : (b + 1) * 128].astype(F32), gain)
    gain = jnp.where(left_lanes(1) == even, gain, pltpu.roll(gain, 64, 1))
    total = jnp.zeros((HALF, 128), F32)
    for b in range(32):
        total += parts_ref[b].astype(F32)
    z = total * gain
    part = jnp.sum(total * v, axis=0, keepdims=True)
    part = jnp.broadcast_to(part + pltpu.roll(part, 64, 1), (8, 128))
    w, w_other = w_ref[...].astype(F32), w_other_ref[...].astype(F32)
    tails = []
    for h, weight in enumerate((jnp.where(straight, w, w_other), jnp.where(straight, w_other, w))):
        rows = z[h * 8 : (h + 1) * 8]
        reads = [
            exact_dot(rows[:, g * ROWS : (g + 1) * ROWS], weight[:, g * HD : (g + 1) * HD], ((1,), (0,)))
            for g in range(2)
        ]
        tails.append(jnp.concatenate([*reads, part, rows], axis=0))
    for i in range(8):
        tails_ref[i] = jnp.where(side == i % 2, tails[0], tails[1])


def weight_kernel(z_ref, r_ref, grad_ref):
    for g in range(2):
        z = z_ref[:, g * ROWS : (g + 1) * ROWS]
        grad_ref[:, g * HD : (g + 1) * HD] = exact_dot(z, r_ref[g * GROUP : (g + 1) * GROUP], ((0,), (0,)))


def near_kernel(tails_ref, out_ref, z_ref):
    core, side, far = lax.axis_index("core"), lax.axis_index("yl"), lax.axis_index("yh")
    read = tails_ref[0][:HALF]
    for i in range(1, 8):
        read += tails_ref[i][:HALF]
    gain = slice(HALF, HALF + 8)
    zero = tails_ref[side][gain] + tails_ref[4 + side][gain]
    one = tails_ref[2 + side][gain] + tails_ref[6 + side][gain]
    at = 2 * core + far
    z_ref[...] = tails_ref[at][HALF + 8 :] + tails_ref[4 + at][HALF + 8 :]
    tail = jnp.concatenate([read, jnp.where(left_lanes(8), zero, one)], axis=0).astype(BF16)
    for i in range(32):
        out_ref[i] = tail


def last_kernel(all_ref, read_ref, gain_ref):
    left = left_lanes(1)
    total = all_ref[0].astype(F32)
    for i in range(1, 32):
        total += all_ref[i].astype(F32)
    read_ref[...] = total[:HALF]
    for xi in range(4):
        for zp in range(4):
            i = xi * 8 + 2 * zp
            one = all_ref[i].astype(F32)[HALF : HALF + 1]
            two = all_ref[i + 1].astype(F32)[HALF : HALF + 1]
            row = xi * 8 + zp
            gain_ref[row : row + 1] = jnp.where(left, one, pltpu.roll(two, 64, 1))
            gain_ref[row + 4 : row + 5] = jnp.where(left, pltpu.roll(one, 64, 1), two)


def input_kernel(width, c_ref, dot_ref, rms_ref, gvt_ref, x_ref, after_ref, out_ref, log_ref):
    rms = rms_ref[...]
    length = rms.shape[1]
    c = c_ref[...]
    high = c.astype(BF16)
    low = (c - high.astype(F32)).astype(BF16)
    log_scale = rms * dot_ref[...]
    log_ref[...] = log_scale
    back = jnp.broadcast_to(rms * rms * log_scale / width, (128, length)).T
    gvt = gvt_ref[...]
    grad = lax.dot_general(
        jnp.concatenate([high, low], axis=0),
        jnp.concatenate([gvt, gvt], axis=0),
        (((0,), (0,)), ((), ())),
        preferred_element_type=F32,
    )
    for b in range(grad.shape[1] // 128):
        at = slice(b * 128, (b + 1) * 128)
        out_ref[:, at] = (grad[:, at] - x_ref[:, at].astype(F32) * back).astype(BF16)


def input_grad(width, c, dot, rms, gvt, x, after):
    steps = 4
    length, wide = x.shape
    return pl.pallas_call(
        lambda *refs: input_kernel(width, *refs),
        grid=(steps,),
        in_specs=[
            pl.BlockSpec((32, length), lambda i: (0, 0)),
            pl.BlockSpec((1, length), lambda i: (0, 0)),
            pl.BlockSpec((1, length), lambda i: (0, 0)),
            pl.BlockSpec((32, wide // steps), lambda i: (0, i)),
            pl.BlockSpec((length, wide // steps), lambda i: (0, i)),
            ANY,
        ],
        out_specs=[
            pl.BlockSpec((length, wide // steps), lambda i: (0, i)),
            pl.BlockSpec((1, length), lambda i: (0, 0)),
        ],
        out_shape=[shape(length, wide, dtype=BF16), shape(1, length)],
        compiler_params=PARAMS,
    )(c, dot, rms, gvt, x, after)


def together(*values):
    return lax.optimization_barrier(values)


def shards(hidden_states, norm_gain, value_weight, queries, keys, readout, targets, scored):
    width = hidden_states.shape[1] * 2
    read = readout.reshape(HALF, HD)
    v = read_weight(value_weight, read)
    v = lax.all_to_all(v.reshape(64, 8, 128), FAR, 0, 0).reshape(512, 128)
    v, norm_gain, targets, scored, value_weight = together(v, norm_gain, targets, scored, value_weight)
    gain = norm_gain[None]
    own, send = whole(pick_kernel, [shape(256, 128, dtype=BF16)] * 2, v)
    own_y = swap(send, "yl")
    got = swap(own, "core")
    x, probs, ss = early(hidden_states, queries, keys, v)
    own_y, got, ss = together(own_y, got, ss)
    got_y = swap(own_y, "core")
    gvt, u, send = project((own, own_y, got, got_y), gain, x, ss)
    send, weight = together(send, value_weight)
    got, weight = together(swap(send, "yl"), cross(weight))
    part, u, rms = make_values(width, probs, u, got, ss)
    part, weight = together(part, weight)
    got, other_weight = together(swap(part, "yl"), swap(weight, "yh"))
    values, c = make_error(probs, u, part, got, targets[None], scored[None])
    c, dot, keep, send = make_rows(c, swap(c, "yl"), rms, x)
    z = (keep + swap(send, "core")).astype(BF16).reshape(32, HALF, 128)
    z = lax.all_to_all(z, PLANE, 0, 0)
    grad_input, log_scale = input_grad(width, c, dot, rms, gvt, x, z)
    tails = whole(sum_kernel, shape(8, HALF + 16, 128), z, gain, own, own_y, weight, other_weight)
    tails = lax.all_to_all(tails, NEAR, 0, 0)
    tails, z = whole(near_kernel, [shape(32, HALF + 8, 128, dtype=BF16), shape(8, 128)], tails)
    grad_weight = whole(weight_kernel, shape(ROWS, 2 * HD), z, read)
    tails = lax.all_to_all(tails, PLANE, 0, 0)
    grad_readout, grad_gain = whole(last_kernel, [shape(HALF, HD), shape(32, 128)], tails)
    return (values[0], grad_input, grad_weight, grad_gain.reshape(-1), grad_readout.reshape(-1), log_scale[0])


def solution(mesh):
    fine = Mesh(mesh.devices.reshape(2, 4, 2, 8, 2), ("yh", "x", "core", "z", "yl"))
    seq = ("yh", "x", "core", "z")
    return jax.shard_map(
        shards,
        mesh=fine,
        in_specs=(
            P(seq, "yl"),
            P("yl"),
            P(seq, "yl"),
            P(seq, "yl"),
            P(seq, "yl"),
            P("yl"),
            P(seq),
            P(seq),
        ),
        out_specs=(
            P(seq),
            P(seq, "yl"),
            P(seq, "yl"),
            P("yl"),
            P("yl"),
            P(seq),
        ),
        check_vma=False,
    )
```

time: 109 us -> 99.5 us (0.913)
  blocking collectives: 0 us -> 49.2 us
  waiting for transfers between devices: 48.8 us -> 18.8 us
  starting transfers between devices: 37.8 us -> 13.4 us
  local copies, waits for them, and re-layouts: 9.49 us -> 5.22 us
    all_to_all x0 -> x3, blocking collectives: none -> 49.2 us  [the longest x1 25.9 us: shards(): v = lax.all_to_all(v.reshape(64, 8, 128), FAR, 0, 0).reshape(512, 128)]
    all_to_all x3 -> x1, starting transfers between devices: 36.1 us -> 4.35 us  [shards(): tails = lax.all_to_all(tails, PLANE, 0, 0)]
    all_to_all x3 -> x1, waiting for transfers between devices: 36.4 us -> 7.33 us  [shards(): tails = lax.all_to_all(tails, PLANE, 0, 0)]
    ppermute x4 -> x8, starting transfers between devices: 0.26 us -> 8.38 us  [swap(): return lax.ppermute(v, axis, [(0, 1), (1, 0)])]
    pallas_call x6 -> x9, Pallas kernels: 4.05 us -> 5.67 us  [whole(): pl.pallas_call(body, in_specs=[VMEM] * len(args), out_specs=[VMEM] * len(...]
    broadcast_in_dim x3 -> x0, local copies, waits for them, and re-layouts: 1.52 us -> none  [the longest x1 0.79 us: shards(): jnp.broadcast_to(tail, (64,) + tail.shape)]
    unnamed x24 -> x20, local copies, waits for them, and re-layouts: 6.5 us -> 5.21 us
    pallas_call x3 -> x2, Pallas kernels: 4.15 us -> 3.11 us  [the longest x1 2.77 us: early(): pl.pallas_call(early_kernel, in_specs=[HBM] * 3 + [ANY], out_specs=[VMEM]...]
  transfers between devices with their start and end apart: 9 -> 10, of which waited for: 7 -> 6; matrix products, arithmetic and copies ran while one was open for 1% -> 0% of each run, Pallas kernels for 5% -> 7%
where the time goes in v3:
time: 99.5 us; the launch traced here: 98.9 us
  blocking collectives  49.2 us (49%)
  waiting for transfers between devices  18.8 us (19%)
  starting transfers between devices  13.4 us (13%)
  Pallas kernels  11.5 us (12%)
  local copies, waits for them, and re-layouts  5.22 us (5%)
    all_to_all x1, blocking collectives, shards(): v = lax.all_to_all(v.reshape(64, 8, 128), FAR, 0, 0).reshape(512, 128)  25.9 us
    all_to_all x1, blocking collectives, shards(): z = lax.all_to_all(z, PLANE, 0, 0)  14.2 us
    ppermute x8, waiting for transfers between devices, swap(): return lax.ppermute(v, axis, [(0, 1), (1, 0)])  11.5 us
    all_to_all x1, blocking collectives, shards(): tails = lax.all_to_all(tails, NEAR, 0, 0)  9.06 us
    ppermute x8, starting transfers between devices, swap(): return lax.ppermute(v, axis, [(0, 1), (1, 0)])  8.38 us
    all_to_all x1, waiting for transfers between devices, shards(): tails = lax.all_to_all(tails, PLANE, 0, 0)  7.33 us
    pallas_call x9, Pallas kernels, whole(): pl.pallas_call(body, in_specs=[VMEM] * len(args), out_specs=[VMEM] * len(...  5.67 us
    unnamed x20, local copies, waits for them, and re-layouts  5.21 us
  transfers between devices with their start and end apart: 10, of which 6 were waited for; matrix products, arithmetic and copies ran while one was open for 0% of the time, Pallas kernels for 7%

profile of v3, /device:TPU:32, one launch (start us, length us, event | category | flops | bytes accessed | tf_op | source)
XLA Modules:
  0.0 98.9 jit_solution(1554298399829546854)
XLA Ops:
  0.6 0.0 copy-start.3
  0.6 0.7 copy-done.3
  1.4 0.0 copy-start.5
  1.4 0.7 copy-done.5
  2.1 0.0 copy-start.9
  2.1 0.3 shard_map.127
  2.4 25.9 %all_to_all.20 = bf16[64,8,128]{2,1,0:T(8,128)(2,1)S(1)} all-to-all(bf16[64,8,128]{2,1,0:T(8,128)(2,1)S(1)} %bitcast.12), channel_id=1, replica_groups=mesh['yh'=2,'x'=4,'core'=2,'z'=8,'yl'=2] {'yh','x','z'}, dimensions={0} | all-to-all | bytes 262144 | tf_op jit(solution)/shard_map/all_to_all | solution.py:398
  28.4 0.1 collective-permute-start.1
  28.5 0.8 collective-permute-start
  29.2 0.0 copy-start
  29.3 1.6 %copy-done = bf16[256,4096]{1,0:T(8,128)(2,1)S(1)} copy-done((bf16[256,4096]{1,0:T(8,128)(2,1)S(1)}, bf16[256,4096]{1,0:T(8,128)(2,1)}, u32[]{:S(2)}) %copy-start) | copy-done | bytes 2097176
  30.8 0.0 copy-start.1
  30.8 1.2 %copy-done.1 = bf16[256,2048]{1,0:T(8,128)(2,1)S(1)} copy-done((bf16[256,2048]{1,0:T(8,128)(2,1)S(1)}, bf16[256,2048]{1,0:T(8,128)(2,1)}, u32[]{:S(2)}) %copy-start.1) | copy-done | bytes 1048600
  32.1 0.0 copy-start.2
  32.1 0.9 copy-done.2
  33.0 0.0 copy-start.4
  33.0 2.8 %shard_map.128 = (bf16[256,4096]{1,0:T(8,128)(2,1)S(1)}, bf16[16,256,256]{2,1,0:T(8,128)(2,1)S(1)}, f32[1,256]{1,0:T(1,128)S(1)}) custom-call(bf16[256,4096]{1,0:T(8,128)(2,1)S(1)} %copy-done, bf16[256,2048]{1,0:T(8,128)(2,1)S(1)} %copy-done.1, bf16[256,256]{1,0:T(8,128)(2,1)S(1)} %copy-done.2, bf16[512,128]{1,0:T(8,128)(2,1)S(1)} %bitcast.11), custom_call_target="tpu_custom_call" | custom-call | tf_op jit(solution)/shard_map/pallas_call | solution.py:143
  35.7 0.0 collective-permute-done.1.got_ref
  35.8 0.0 collective-permute-done.own_y_ref
  35.8 0.2 collective-permute-start.2
  36.0 0.0 copy-done.9
  36.0 1.1 %collective-permute-done.2.got_y_ref = bf16[256,128]{1,0:T(8,128)(2,1)S(1)} collective-permute-done((bf16[256,128]{1,0:T(8,128)(2,1)S(1)}, bf16[256,128]{1,0:T(8,128)(2,1)S(1)}, u32[]{:S(2)}, u32[]{:S(2)}) %collective-permute-start.2) | collective-permute-done | bytes 65568 | tf_op jit(solution)/shard_map/ppermute | solution.py:30
  37.1 0.0 copy-start.7
  37.1 0.0 copy-start.8
  37.1 0.8 shard_map.130
  37.9 0.0 copy-done.4
  37.9 0.7 collective-permute-start.4
  38.6 2.9 %collective-permute-start.3 = (f32[24,256]{1,0:T(8,128)S(1)}, f32[24,256]{1,0:T(8,128)S(1)}, u32[]{:S(2)}, u32[]{:S(2)}) collective-permute-start(f32[24,256]{1,0:T(8,128)S(1)} %get-tuple-element.58), channel_id=1, source_target_pairs={{0,1},{1,0},{2,3},{3,2},{4,5},{5,4},{6,7},{7,6},{8,9},{9,8},{10,11... | collective-permute-start | bytes 73736 | tf_op jit(solution)/shard_map/ppermute | solution.py:30
  41.4 1.8 %collective-permute-done.3.refs_2_ = f32[24,256]{1,0:T(8,128)S(1)} collective-permute-done((f32[24,256]{1,0:T(8,128)S(1)}, f32[24,256]{1,0:T(8,128)S(1)}, u32[]{:S(2)}, u32[]{:S(2)}) %collective-permute-start.3) | collective-permute-done | bytes 24608 | tf_op jit(solution)/shard_map/ppermute | solution.py:30
  43.2 0.0 collective-permute-done.4.w_ref
  43.2 0.5 shard_map.131
  43.8 4.0 %collective-permute-start.6 = (bf16[64,256]{1,0:T(8,128)(2,1)S(1)}, bf16[64,256]{1,0:T(8,128)(2,1)S(1)}, u32[]{:S(2)}, u32[]{:S(2)}) collective-permute-start(bf16[64,256]{1,0:T(8,128)(2,1)S(1)} %collective-permute-done.4.w_ref), channel_id=1, source_target_pairs={{0,128},{128,0},{1,129},{129,1},{2,130},{130,2},{3,131},{131,3},{4... | collective-permute-start | bytes 98312 | tf_op jit(solution)/shard_map/ppermute | solution.py:30
  47.8 0.0 collective-permute-start.5
  47.8 3.6 %collective-permute-done.5.got_ref = f32[1,256]{1,0:T(1,128)S(1)} collective-permute-done((f32[1,256]{1,0:T(1,128)S(1)}, f32[1,256]{1,0:T(1,128)S(1)}, u32[]{:S(2)}, u32[]{:S(2)}) %collective-permute-start.5) | collective-permute-done | bytes 1056 | tf_op jit(solution)/shard_map/ppermute | solution.py:30
  51.4 0.0 collective-permute-done.6.w_other_ref
  51.4 0.0 copy-done.7
  51.4 0.0 copy-done.8
  51.4 1.1 %shard_map.132 = (f32[1,256]{1,0:T(1,128)}, f32[24,256]{1,0:T(8,128)S(1)}) custom-call(bf16[16,256,256]{2,1,0:T(8,128)(2,1)S(1)} %get-tuple-element.46.refs_0_.p_ref, f32[16,256]{1,0:T(8,128)S(1)} %get-tuple-element.61.u_ref, f32[1,256]{1,0:T(1,128)S(1)} %get-tuple-element.64.own_ref, f32[1,256]{1,0:T(1,128)S(1)} %collective-permute-done.5.got_ref, ...), custom_call_target="tpu_custom_call" | custom-call | tf_op jit(solution)/shard_map/pallas_call | solution.py:46
  52.5 0.4 collective-permute-start.7
  52.8 3.5 %collective-permute-done.7.got_ref = f32[24,256]{1,0:T(8,128)S(1)} collective-permute-done((f32[24,256]{1,0:T(8,128)S(1)}, f32[24,256]{1,0:T(8,128)S(1)}, u32[]{:S(2)}, u32[]{:S(2)}) %collective-permute-start.7) | collective-permute-done | bytes 24608 | tf_op jit(solution)/shard_map/ppermute | solution.py:30
  56.3 0.6 shard_map.133
  56.9 0.1 collective-permute-start.8
  57.0 1.5 %collective-permute-done.8 = f32[512,128]{1,0:T(8,128)S(1)} collective-permute-done((f32[512,128]{1,0:T(8,128)S(1)}, f32[512,128]{1,0:T(8,128)S(1)}, u32[]{:S(2)}, u32[]{:S(2)}) %collective-permute-start.8) | collective-permute-done | bytes 262176 | tf_op jit(solution)/shard_map/ppermute | solution.py:30
  58.5 0.0 copy-start.6
  58.5 14.2 %all_to_all.21.refs_5_.parts_ref = bf16[32,16,128]{2,1,0:T(8,128)(2,1)S(1)} all-to-all(bf16[32,16,128]{2,1,0:T(8,128)(2,1)S(1)} %bitcast.17), channel_id=1, replica_groups=mesh['yh'=2,'x'=4,'core'=2,'z'=8,'yl'=2] {'x','z'}, dimensions={0} | all-to-all | bytes 262144 | tf_op jit(solution)/shard_map/all_to_all | solution.py:416
  72.8 0.4 shard_map.135
  73.1 9.1 %all_to_all.22.tails_ref = f32[8,32,128]{2,1,0:T(8,128)S(1)} all-to-all(f32[8,32,128]{2,1,0:T(8,128)S(1)} %shard_map.135), channel_id=1, replica_groups=mesh['yh'=2,'x'=4,'core'=2,'z'=8,'yl'=2] {'yh','core','yl'}, dimensions={0} | all-to-all | bytes 262144 | tf_op jit(solution)/shard_map/all_to_all | solution.py:419
  82.2 0.7 shard_map.136
  82.9 4.4 %all-to-all-start.3 = ((bf16[32,24,128]{2,1,0:T(8,128)(2,1)}), bf16[32,24,128]{2,1,0:T(8,128)(2,1)S(1)}, u32[]{:S(2)}, u32[]{:S(2)}) async-start(bf16[32,24,128]{2,1,0:T(8,128)(2,1)} %get-tuple-element.80), calls=%async_computation.3 | async-start | bytes 393216 | tf_op jit(solution)/shard_map/all_to_all | solution.py:422
  87.3 2.7 %shard_map.134 = (bf16[256,4096]{1,0:T(8,128)(2,1)}, f32[1,256]{1,0:T(1,128)}) custom-call(f32[32,256]{1,0:T(8,128)S(1)} %get-tuple-element.72.refs_0_, f32[1,256]{1,0:T(1,128)S(1)} %get-tuple-element.73.refs_1_, f32[1,256]{1,0:T(1,128)S(1)} %get-tuple-element.71.rms_ref.refs_2_, bf16[32,4096]{1,0:T(8,128)(2,1)S(1)} %get-tuple-element.74.refs_3_, ...), custom_call_target="tpu_custom_call" | custom-call | tf_op jit(solution)/shard_map/pallas_call | solution.py:370
  90.0 0.0 copy-done.6
  90.0 0.9 shard_map.137
  90.9 7.3 %all-to-all-done.3.all_ref = bf16[32,24,128]{2,1,0:T(8,128)(2,1)S(1)} async-done(((bf16[32,24,128]{2,1,0:T(8,128)(2,1)}), bf16[32,24,128]{2,1,0:T(8,128)(2,1)S(1)}, u32[]{:S(2)}, u32[]{:S(2)}) %all-to-all-start.3) | async-done | bytes 196640 | tf_op jit(solution)/shard_map/all_to_all | solution.py:422
  98.3 0.7 shard_map.138
  (3 shorter events, 0.0 us)
Async XLA Ops:
  0.6 0.8 copy-start.3
  1.4 0.7 copy-start.5
  2.1 33.9 %copy-start.9 = (bf16[4096]{0:T(1024)(128)(2,1)S(1)}, bf16[4096]{0:T(1024)(128)(2,1)}, u32[]{:S(2)}) copy-start(bf16[4096]{0:T(1024)(128)(2,1)} %param.9) | copy-start | bytes 24580
  28.4 7.4 %collective-permute-start.1 = (bf16[256,128]{1,0:T(8,128)(2,1)S(1)}, bf16[256,128]{1,0:T(8,128)(2,1)S(1)}, u32[]{:S(2)}, u32[]{:S(2)}) collective-permute-start(bf16[256,128]{1,0:T(8,128)(2,1)S(1)} %get-tuple-element.47.own_ref), channel_id=1, source_target_pairs={{0,16},{16,0},{1,17},{17,1},{2,18},{18,2},{3,19},{19,3},{4,20},{20... | collective-permute-start | bytes 196616 | tf_op jit(solution)/shard_map/ppermute | solution.py:30
  28.5 7.3 %collective-permute-start = (bf16[256,128]{1,0:T(8,128)(2,1)S(1)}, bf16[256,128]{1,0:T(8,128)(2,1)S(1)}, u32[]{:S(2)}, u32[]{:S(2)}) collective-permute-start(bf16[256,128]{1,0:T(8,128)(2,1)S(1)} %get-tuple-element.48), channel_id=1, source_target_pairs={{0,1},{1,0},{2,3},{3,2},{4,5},{5,4},{6,7},{7,6},{8,9},{9,8},{10,11... | collective-permute-start | bytes 196616 | tf_op jit(solution)/shard_map/ppermute | solution.py:30
  29.2 1.6 %copy-start = (bf16[256,4096]{1,0:T(8,128)(2,1)S(1)}, bf16[256,4096]{1,0:T(8,128)(2,1)}, u32[]{:S(2)}) copy-start(bf16[256,4096]{1,0:T(8,128)(2,1)} %x_ref.1) | copy-start | bytes 6291460
  30.8 1.2 %copy-start.1 = (bf16[256,2048]{1,0:T(8,128)(2,1)S(1)}, bf16[256,2048]{1,0:T(8,128)(2,1)}, u32[]{:S(2)}) copy-start(bf16[256,2048]{1,0:T(8,128)(2,1)} %q_ref.1) | copy-start | bytes 3145732
  32.1 0.9 copy-start.2
  33.0 4.9 %copy-start.4 = (bf16[64,256]{1,0:T(8,128)(2,1)S(1)}, bf16[64,256]{1,0:T(8,128)(2,1)}, u32[]{:S(2)}) copy-start(bf16[64,256]{1,0:T(8,128)(2,1)} %w_ref.1) | copy-start | bytes 98308
  35.8 1.3 %collective-permute-start.2 = (bf16[256,128]{1,0:T(8,128)(2,1)S(1)}, bf16[256,128]{1,0:T(8,128)(2,1)S(1)}, u32[]{:S(2)}, u32[]{:S(2)}) collective-permute-start(bf16[256,128]{1,0:T(8,128)(2,1)S(1)} %collective-permute-done.own_y_ref), channel_id=1, source_target_pairs={{0,16},{16,0},{1,17},{17,1},{2,18},{18,2},{3,19},{19,3},{4,20},{20... | collective-permute-start | bytes 196616 | tf_op jit(solution)/shard_map/ppermute | solution.py:30
  37.1 14.3 %copy-start.7 = (f32[256]{0:T(256)S(1)}, f32[256]{0:T(256)}, u32[]{:S(2)}) copy-start(f32[256]{0:T(256)} %param.14) | copy-start | bytes 3076
  37.1 14.3 %copy-start.8 = (s32[256]{0:T(256)S(1)}, s32[256]{0:T(256)}, u32[]{:S(2)}) copy-start(s32[256]{0:T(256)} %param.15) | copy-start | bytes 3076
  37.9 5.3 %collective-permute-start.4 = (bf16[64,256]{1,0:T(8,128)(2,1)S(1)}, bf16[64,256]{1,0:T(8,128)(2,1)S(1)}, u32[]{:S(2)}, u32[]{:S(2)}) collective-permute-start(bf16[64,256]{1,0:T(8,128)(2,1)S(1)} %copy-done.4), channel_id=1, source_target_pairs={{0,0},{1,128},{128,1},{129,129},{2,2},{3,130},{130,3},{131,131},{4... | collective-permute-start | bytes 98312 | tf_op jit(solution)/shard_map/ppermute | solution.py:34
  38.6 4.7 %collective-permute-start.3 = (f32[24,256]{1,0:T(8,128)S(1)}, f32[24,256]{1,0:T(8,128)S(1)}, u32[]{:S(2)}, u32[]{:S(2)}) collective-permute-start(f32[24,256]{1,0:T(8,128)S(1)} %get-tuple-element.58), channel_id=1, source_target_pairs={{0,1},{1,0},{2,3},{3,2},{4,5},{5,4},{6,7},{7,6},{8,9},{9,8},{10,11... | collective-permute-start | bytes 73736 | tf_op jit(solution)/shard_map/ppermute | solution.py:30
  43.8 7.6 %collective-permute-start.6 = (bf16[64,256]{1,0:T(8,128)(2,1)S(1)}, bf16[64,256]{1,0:T(8,128)(2,1)S(1)}, u32[]{:S(2)}, u32[]{:S(2)}) collective-permute-start(bf16[64,256]{1,0:T(8,128)(2,1)S(1)} %collective-permute-done.4.w_ref), channel_id=1, source_target_pairs={{0,128},{128,0},{1,129},{129,1},{2,130},{130,2},{3,131},{131,3},{4... | collective-permute-start | bytes 98312 | tf_op jit(solution)/shard_map/ppermute | solution.py:30
  47.8 3.6 %collective-permute-start.5 = (f32[1,256]{1,0:T(1,128)S(1)}, f32[1,256]{1,0:T(1,128)S(1)}, u32[]{:S(2)}, u32[]{:S(2)}) collective-permute-start(f32[1,256]{1,0:T(1,128)S(1)} %get-tuple-element.64.own_ref), channel_id=1, source_target_pairs={{0,1},{1,0},{2,3},{3,2},{4,5},{5,4},{6,7},{7,6},{8,9},{9,8},{10,11... | collective-permute-start | bytes 3080 | tf_op jit(solution)/shard_map/ppermute | solution.py:30
  52.5 3.8 %collective-permute-start.7 = (f32[24,256]{1,0:T(8,128)S(1)}, f32[24,256]{1,0:T(8,128)S(1)}, u32[]{:S(2)}, u32[]{:S(2)}) collective-permute-start(f32[24,256]{1,0:T(8,128)S(1)} %get-tuple-element.70.own_ref), channel_id=1, source_target_pairs={{0,1},{1,0},{2,3},{3,2},{4,5},{5,4},{6,7},{7,6},{8,9},{9,8},{10,11... | collective-permute-start | bytes 73736 | tf_op jit(solution)/shard_map/ppermute | solution.py:30
  56.9 1.6 %collective-permute-start.8 = (f32[512,128]{1,0:T(8,128)S(1)}, f32[512,128]{1,0:T(8,128)S(1)}, u32[]{:S(2)}, u32[]{:S(2)}) collective-permute-start(f32[512,128]{1,0:T(8,128)S(1)} %get-tuple-element.76), channel_id=1, source_target_pairs={{0,16},{16,0},{1,17},{17,1},{2,18},{18,2},{3,19},{19,3},{4,20},{20... | collective-permute-start | bytes 786440 | tf_op jit(solution)/shard_map/ppermute | solution.py:30
  58.5 31.5 %copy-start.6 = (f32[2048]{0:T(1024)S(1)}, f32[2048]{0:T(1024)}, u32[]{:S(2)}) copy-start(f32[2048]{0:T(1024)} %param.13) | copy-start | bytes 24580
  82.9 15.4 %all-to-all-start.3 = ((bf16[32,24,128]{2,1,0:T(8,128)(2,1)}), bf16[32,24,128]{2,1,0:T(8,128)(2,1)S(1)}, u32[]{:S(2)}, u32[]{:S(2)}) async-start(bf16[32,24,128]{2,1,0:T(8,128)(2,1)} %get-tuple-element.80), calls=%async_computation.3 | async-start | bytes 393216 | tf_op jit(solution)/shard_map/all_to_all | solution.py:422

commit v4 on v3

--- a/solution.py
+++ b/solution.py
@@ -15,10 +15,10 @@
 VMEM = pl.BlockSpec(memory_space=pltpu.VMEM)
 HBM = pl.BlockSpec(memory_space=pltpu.HBM)
 ANY = pl.BlockSpec(memory_space=pl.ANY)
+LOADS = pltpu.CompilerParams(vmem_limit_bytes=51 * 1024 * 1024)
 PARAMS = pltpu.CompilerParams(vmem_limit_bytes=16 * 1024 * 1024)
 
 
-FAR = ("yh", "x", "z")
 PLANE = ("x", "z")
 NEAR = ("yh", "core", "yl")
 ROWS = 64
@@ -65,43 +65,61 @@
     return lax.broadcasted_iota(jnp.int32, (rows, 128), 1) < 64
 
 
-def read_kernel(w_ref, r_ref, v_ref, wv_ref, rv_ref, sems):
-    copies = [
-        pltpu.make_async_copy(w_ref, wv_ref, sems.at[0]),
-        pltpu.make_async_copy(r_ref, rv_ref, sems.at[1]),
-    ]
-    for copy in copies:
-        copy.start()
-    for copy in copies:
-        copy.wait()
+def read_kernel(w_ref, r_ref, v_ref, w2_ref):
     parts = []
     for g in range(2):
-        w = wv_ref[:, g * HD : (g + 1) * HD].astype(F32)
-        parts.append(exact_dot(rv_ref[g * GROUP : (g + 1) * GROUP], w, ((1,), (1,))))
+        w = w_ref[:, g * HD : (g + 1) * HD]
+        w2_ref[g * ROWS : (g + 1) * ROWS] = w
+        parts.append(exact_dot(r_ref[g * GROUP : (g + 1) * GROUP], w.astype(F32), ((1,), (1,))))
     v = jnp.concatenate(parts, axis=1)
     v = jnp.concatenate([v, v], axis=0).astype(BF16)
-    for i in range(32):
+    for i in range(16):
         v_ref[i * 16 : (i + 1) * 16] = v
 
 
-def read_weight(w, read):
-    return pl.pallas_call(
-        read_kernel,
-        in_specs=[HBM] * 2,
-        out_specs=VMEM,
-        out_shape=shape(512, 128, dtype=BF16),
-        scratch_shapes=[
-            pltpu.VMEM(w.shape, BF16), pltpu.VMEM(read.shape, F32), pltpu.SemaphoreType.DMA((2,))
-        ],
-        compiler_params=PARAMS,
-    )(w, read)
+def stack_kernel(v_ref, w_ref, out_ref):
+    out_ref[:256] = v_ref[...]
+    out_ref[256:] = w_ref[...]
+
+
+def merge_kernel(self_ref, ring_ref, swap_ref, v_ref, w_ref):
+    straight = lax.axis_index("yh") == lax.axis_index("yl")
+    ring = ring_ref[...]
+    own = jnp.where(straight, self_ref[...], ring)
+    other = jnp.where(straight, ring, swap_ref[...])
+    v_ref[:256] = own[:256]
+    v_ref[256:] = other[:256]
+    w_ref[:128] = own[256:]
+    w_ref[128:] = other[256:]
 
 
 def row_sum_of_transpose(a):
     return jnp.sum(a.T, axis=0, keepdims=True)
 
 
-def attention(q_ref, k_ref, p_ref):
+def load_kernel(x_ref, after_ref, xv_ref, ss_ref, sem):
+    copy = pltpu.make_async_copy(x_ref, xv_ref, sem)
+    copy.start()
+    copy.wait()
+    total = jnp.zeros((xv_ref.shape[0], 128), F32)
+    for b in range(xv_ref.shape[1] // 128):
+        xb = xv_ref[:, b * 128 : (b + 1) * 128].astype(F32)
+        total += xb * xb
+    ss_ref[...] = row_sum_of_transpose(total)
+
+
+def load(x, after):
+    return pl.pallas_call(
+        load_kernel,
+        in_specs=[HBM, ANY],
+        out_specs=[VMEM] * 2,
+        out_shape=[shape(*x.shape, dtype=BF16), shape(1, x.shape[0])],
+        scratch_shapes=[pltpu.SemaphoreType.DMA],
+        compiler_params=LOADS,
+    )(x, after)
+
+
+def attention_kernel(q_ref, k_ref, after_ref, p_ref):
     length = q_ref.shape[0]
     rows = lax.broadcasted_iota(jnp.int32, (length, length), 0)
     cols = lax.broadcasted_iota(jnp.int32, (length, length), 1)
@@ -119,52 +137,24 @@
         p_ref[h] = (e / jnp.sum(e, axis=1, keepdims=True)).astype(BF16)
 
 
-def early_kernel(x_ref, q_ref, k_ref, after_ref, xv_ref, p_ref, ss_ref, qv_ref, kv_ref, sems):
-    copies = [
-        pltpu.make_async_copy(q_ref, qv_ref, sems.at[0]),
-        pltpu.make_async_copy(k_ref, kv_ref, sems.at[1]),
-        pltpu.make_async_copy(x_ref, xv_ref, sems.at[2]),
-    ]
-    for copy in copies:
-        copy.start()
-    copies[0].wait()
-    copies[1].wait()
-    attention(qv_ref, kv_ref, p_ref)
-    copies[2].wait()
-    total = jnp.zeros((xv_ref.shape[0], 128), F32)
-    for b in range(xv_ref.shape[1] // 128):
-        xb = xv_ref[:, b * 128 : (b + 1) * 128].astype(F32)
-        total += xb * xb
-    ss_ref[...] = row_sum_of_transpose(total)
-
-
-def early(x, queries, keys, after):
-    length = x.shape[0]
-    return pl.pallas_call(
-        early_kernel,
-        in_specs=[HBM] * 3 + [ANY],
-        out_specs=[VMEM] * 3,
-        out_shape=[shape(*x.shape, dtype=BF16), shape(HALF, length, length, dtype=BF16), shape(1, length)],
-        scratch_shapes=[
-            pltpu.VMEM(queries.shape, BF16), pltpu.VMEM(keys.shape, BF16), pltpu.SemaphoreType.DMA((3,))
-        ],
-        compiler_params=PARAMS,
-    )(x, queries, keys, after)
+def attention(queries, keys, after):
+    length = queries.shape[0]
+    return whole(attention_kernel, shape(HALF, length, length, dtype=BF16), queries, keys, after)
 
 
 def project_kernel(
-    own_ref, own_y_ref, got_ref, got_y_ref, gain_ref, x_ref, ss_ref, gvt_ref, u_ref, send_ref
+    own_ref, got_ref, gain_ref, x_ref, ss_ref, gvt_ref, u_ref, send_ref
 ):
     core = lax.axis_index("core")
     low = left_lanes(8)
     for b in range(BLOCKS // 2):
         xi, c, zp = b // 8, b // 4 % 2, b % 4
         at = slice(b * 128, (b + 1) * 128)
-        row = (xi * 8 + 2 * zp) * 8
         halves = []
-        for here, there in ((own_ref, got_ref), (own_y_ref, got_y_ref)):
+        for h in range(2):
+            row = h * 256 + (xi * 8 + 2 * zp) * 8
             pair = jnp.where(
-                core == c, here[row : row + 16].astype(F32), there[row : row + 16].astype(F32)
+                core == c, own_ref[row : row + 16].astype(F32), got_ref[row : row + 16].astype(F32)
             )
             one, two = pair[:8], pair[8:]
             halves.append(jnp.where(low, one, pltpu.roll(two, 64, 1)))
@@ -179,12 +169,12 @@
     send_ref[HALF:] = jnp.broadcast_to(ss_ref[...], (8, u.shape[1]))
 
 
-def project(vs, gain, x, ss):
+def project(own, got, gain, x, ss):
     length, wide = x.shape
     return whole(
         project_kernel,
         [shape(32, wide, dtype=BF16), shape(HALF, length), shape(HALF + 8, length)],
-        *vs, gain, x, ss,
+        own, got, gain, x, ss,
     )
 
 
@@ -215,8 +205,13 @@
     values = own_ref[...] + got_ref[...]
     values_ref[...] = values
     error = (values - targets_ref[...]) * scored_ref[...].astype(F32)
-    spread = jnp.broadcast_to(error, (length, length)).T
-    rows = [jnp.sum(p_ref[j].astype(F32) * spread, axis=0, keepdims=True) for j in range(HALF)]
+    high = error.astype(BF16)
+    low = (error - high.astype(F32)).astype(BF16)
+    both = jnp.concatenate([jnp.broadcast_to(high, (8, length)), jnp.broadcast_to(low, (8, length))], axis=0)
+    rows = []
+    for j in range(HALF):
+        c = jnp.dot(both, p_ref[j], preferred_element_type=F32)
+        rows.append(c[:1] + c[8:9])
     c = jnp.concatenate(rows, axis=0)
     c_ref[:HALF] = c
     c_ref[HALF:] = jnp.broadcast_to(jnp.sum(c * u_ref[...], axis=0, keepdims=True), (8, length))
@@ -253,33 +248,26 @@
             at = pl.ds((xi * 4 + zp) * 32, 32)
             zero, one = chunks(xi * 8 + zp), chunks(xi * 8 + 4 + zp)
             keep_ref[at] = jnp.where(core == 0, zero, one)
-            send_ref[at] = jnp.where(core == 0, one, zero)
+            send_ref[at] = jnp.where(core == 0, one, zero).astype(BF16)
 
 
 def make_rows(own, got, rms, x):
     length = x.shape[0]
     return whole(
         rows_kernel,
-        [shape(32, length), shape(1, length), shape(512, 128), shape(512, 128)],
+        [shape(32, length), shape(1, length), shape(512, 128), shape(512, 128, dtype=BF16)],
         own, got, rms, x,
     )
 
 
-def pick_kernel(v_ref, own_ref, send_ref):
+def sum_kernel(parts_ref, gain_ref, v_ref, w_ref, tails_ref):
     side = lax.axis_index("yl")
-    own_ref[...] = v_ref[pl.ds(pl.multiple_of(side * 256, 256), 256)]
-    send_ref[...] = v_ref[pl.ds(pl.multiple_of((1 - side) * 256, 256), 256)]
-
-
-def sum_kernel(parts_ref, gain_ref, own_ref, own_y_ref, w_ref, w_other_ref, tails_ref):
-    side = lax.axis_index("yl")
-    straight = lax.axis_index("yh") == side
     xi, zi = lax.axis_index("x"), lax.axis_index("z")
     even = zi % 2 == 0
-    at = pl.ds(pl.multiple_of((xi * 4 + zi // 2) * 16, 16), 16)
     vs = []
-    for ref in (own_ref, own_y_ref):
-        pair = ref[at].astype(F32)
+    for h in range(2):
+        at = pl.ds(pl.multiple_of(h * 256 + (xi * 4 + zi // 2) * 16, 16), 16)
+        pair = v_ref[at].astype(F32)
         vs.append(jnp.where(even, pair[:8], pair[8:]))
     v = jnp.concatenate(vs, axis=0)
     spot = (xi * 2 + lax.axis_index("core")) * 4 + zi // 2
@@ -293,14 +281,13 @@
     z = total * gain
     part = jnp.sum(total * v, axis=0, keepdims=True)
     part = jnp.broadcast_to(part + pltpu.roll(part, 64, 1), (8, 128))
-    w, w_other = w_ref[...].astype(F32), w_other_ref[...].astype(F32)
+    ws = [w_ref[i * ROWS : (i + 1) * ROWS].astype(F32) for i in range(4)]
     tails = []
-    for h, weight in enumerate((jnp.where(straight, w, w_other), jnp.where(straight, w_other, w))):
+    for h in range(2):
         rows = z[h * 8 : (h + 1) * 8]
-        reads = [
-            exact_dot(rows[:, g * ROWS : (g + 1) * ROWS], weight[:, g * HD : (g + 1) * HD], ((1,), (0,)))
-            for g in range(2)
-        ]
+        reads = []
+        for g in range(2):
+            reads.append(exact_dot(rows[:, g * ROWS : (g + 1) * ROWS], ws[2 * h + g], ((1,), (0,))))
         tails.append(jnp.concatenate([*reads, part, rows], axis=0))
     for i in range(8):
         tails_ref[i] = jnp.where(side == i % 2, tails[0], tails[1])
@@ -394,28 +381,30 @@
 def shards(hidden_states, norm_gain, value_weight, queries, keys, readout, targets, scored):
     width = hidden_states.shape[1] * 2
     read = readout.reshape(HALF, HD)
-    v = read_weight(value_weight, read)
-    v = lax.all_to_all(v.reshape(64, 8, 128), FAR, 0, 0).reshape(512, 128)
-    v, norm_gain, targets, scored, value_weight = together(v, norm_gain, targets, scored, value_weight)
+    v, w = whole(
+        read_kernel, [shape(256, 128, dtype=BF16), shape(128, 128, dtype=BF16)], value_weight, read
+    )
+    v = lax.all_to_all(v.reshape(32, 8, 128), PLANE, 0, 0).reshape(256, 128)
+    v, norm_gain, targets, scored = together(v, norm_gain, targets, scored)
     gain = norm_gain[None]
-    own, send = whole(pick_kernel, [shape(256, 128, dtype=BF16)] * 2, v)
-    own_y = swap(send, "yl")
-    got = swap(own, "core")
-    x, probs, ss = early(hidden_states, queries, keys, v)
-    own_y, got, ss = together(own_y, got, ss)
-    got_y = swap(own_y, "core")
-    gvt, u, send = project((own, own_y, got, got_y), gain, x, ss)
-    send, weight = together(send, value_weight)
-    got, weight = together(swap(send, "yl"), cross(weight))
-    part, u, rms = make_values(width, probs, u, got, ss)
-    part, weight = together(part, weight)
-    got, other_weight = together(swap(part, "yl"), swap(weight, "yh"))
+    both = whole(stack_kernel, shape(384, 128, dtype=BF16), v, w)
+    first = lax.ppermute(both, ("yh", "yl"), [(1, 0), (0, 2), (2, 3), (3, 1)])
+    second = lax.ppermute(both, ("yh", "yl"), [(1, 2), (2, 1)])
+    x, ss = load(hidden_states, v)
+    first, second, ss = together(first, second, ss)
+    v, weight = whole(
+        merge_kernel, [shape(512, 128, dtype=BF16), shape(256, 128, dtype=BF16)], both, first, second
+    )
+    gvt, u, send = project(v, swap(v, "core"), gain, x, ss)
+    probs = attention(queries, keys, u)
+    part, u, rms = make_values(width, probs, u, swap(send, "yl"), ss)
+    got = swap(part, "yl")
     values, c = make_error(probs, u, part, got, targets[None], scored[None])
     c, dot, keep, send = make_rows(c, swap(c, "yl"), rms, x)
-    z = (keep + swap(send, "core")).astype(BF16).reshape(32, HALF, 128)
+    z = (keep + swap(send, "core").astype(F32)).astype(BF16).reshape(32, HALF, 128)
     z = lax.all_to_all(z, PLANE, 0, 0)
     grad_input, log_scale = input_grad(width, c, dot, rms, gvt, x, z)
-    tails = whole(sum_kernel, shape(8, HALF + 16, 128), z, gain, own, own_y, weight, other_weight)
+    tails = whole(sum_kernel, shape(8, HALF + 16, 128), z, gain, v, weight)
     tails = lax.all_to_all(tails, NEAR, 0, 0)
     tails, z = whole(near_kernel, [shape(32, HALF + 8, 128, dtype=BF16), shape(8, 128)], tails)
     grad_weight = whole(weight_kernel, shape(ROWS, 2 * HD), z, read)

time: 99.5 us -> 89.6 us (0.901)
  waiting for transfers between devices: 18.8 us -> 13.6 us
  local copies, waits for them, and re-layouts: 5.22 us -> 1.49 us
  blocking collectives: 49.2 us -> 45.5 us
  starting transfers between devices: 13.4 us -> 15.3 us
    all_to_all x1, blocking collectives: 25.9 us -> 20.2 us  [shards(): v = lax.all_to_all(v.reshape(32, 8, 128), PLANE, 0, 0).reshape(256, 128)]
    ppermute x8 -> x5, waiting for transfers between devices: 11.5 us -> 6.24 us  [swap(): return lax.ppermute(v, axis, [(0, 1), (1, 0)])]
    unnamed x20 -> x16, local copies, waits for them, and re-layouts: 5.21 us -> 1.48 us
    ppermute x1 -> x2, starting transfers between devices: 0.66 us -> 3.93 us  [the longest x1 3.27 us: shards(): first = lax.ppermute(both, ('yh', 'yl'), [(1, 0), (0, 2), (2, 3), (3, 1)])]
    all_to_all x1, blocking collectives: 9.06 us -> 11.2 us  [shards(): tails = lax.all_to_all(tails, NEAR, 0, 0)]
    pallas_call x9 -> x12, Pallas kernels: 5.67 us -> 7.55 us  [whole(): pl.pallas_call(body, in_specs=[VMEM] * len(args), out_specs=[VMEM] * len(...]
    ppermute x8 -> x5, starting transfers between devices: 8.38 us -> 7.06 us  [swap(): return lax.ppermute(v, axis, [(0, 1), (1, 0)])]
    pallas_call x2 -> x1, Pallas kernels: 3.11 us -> 2.1 us  [load(): pl.pallas_call(load_kernel, in_specs=[HBM, ANY], out_specs=[VMEM] * 2, ou...]
  transfers between devices with their start and end apart: 10 -> 8, of which waited for: 6 -> 5; matrix products, arithmetic and copies ran while one was open for 0% -> 0% of each run, Pallas kernels for 7% -> 9%
where the time goes in v4:
time: 89.6 us; the launch traced here: 89.1 us
  blocking collectives  45.5 us (51%)
  starting transfers between devices  15.3 us (17%)
  waiting for transfers between devices  13.6 us (15%)
  Pallas kernels  12.4 us (14%)
  local copies, waits for them, and re-layouts  1.49 us (2%)
    all_to_all x1, blocking collectives, shards(): v = lax.all_to_all(v.reshape(32, 8, 128), PLANE, 0, 0).reshape(256, 128)  20.2 us
    all_to_all x1, blocking collectives, shards(): z = lax.all_to_all(z, PLANE, 0, 0)  14.2 us
    all_to_all x1, blocking collectives, shards(): tails = lax.all_to_all(tails, NEAR, 0, 0)  11.2 us
    pallas_call x12, Pallas kernels, whole(): pl.pallas_call(body, in_specs=[VMEM] * len(args), out_specs=[VMEM] * len(...  7.55 us
    all_to_all x1, waiting for transfers between devices, shards(): tails = lax.all_to_all(tails, PLANE, 0, 0)  7.33 us
    ppermute x5, starting transfers between devices, swap(): return lax.ppermute(v, axis, [(0, 1), (1, 0)])  7.06 us
    ppermute x5, waiting for transfers between devices, swap(): return lax.ppermute(v, axis, [(0, 1), (1, 0)])  6.24 us
    all_to_all x1, starting transfers between devices, shards(): tails = lax.all_to_all(tails, PLANE, 0, 0)  4.35 us
  transfers between devices with their start and end apart: 8, of which 5 were waited for; matrix products, arithmetic and copies ran while one was open for 0% of the time, Pallas kernels for 9%

profile of v4, /device:TPU:32, one launch (start us, length us, event | category | flops | bytes accessed | tf_op | source)
XLA Modules:
  0.0 89.1 jit_solution(4082159197098003839)
XLA Ops:
  0.6 0.0 copy-start.2
  0.6 0.7 copy-done.2
  1.3 0.0 copy-start.4
  1.3 0.8 copy-done.4
  2.1 0.0 copy-start.7
  2.1 0.2 shard_map.127
  2.3 20.2 %all_to_all.20 = bf16[32,8,128]{2,1,0:T(8,128)(2,1)S(1)} all-to-all(bf16[32,8,128]{2,1,0:T(8,128)(2,1)S(1)} %bitcast.12), channel_id=1, replica_groups=mesh['yh'=2,'x'=4,'core'=2,'z'=8,'yl'=2] {'x','z'}, dimensions={0} | all-to-all | bytes 131072 | tf_op jit(solution)/shard_map/all_to_all | solution.py:387
  22.5 0.0 copy-start
  22.5 0.0 copy-start.1
  22.5 3.3 %collective-permute-start = (bf16[384,128]{1,0:T(8,128)(2,1)S(1)}, bf16[384,128]{1,0:T(8,128)(2,1)S(1)}, u32[]{:S(2)}, u32[]{:S(2)}) collective-permute-start(bf16[384,128]{1,0:T(8,128)(2,1)S(1)} %shard_map.128.self_ref), channel_id=1, source_target_pairs={{1,0},{0,128},{128,129},{129,1},{3,2},{2,130},{130,131},{131,3},{5... | collective-permute-start | bytes 294920 | tf_op jit(solution)/shard_map/ppermute | solution.py:391
  25.8 0.7 collective-permute-start.1
  26.4 2.1 %shard_map.129 = (bf16[256,4096]{1,0:T(8,128)(2,1)S(1)}, f32[1,256]{1,0:T(1,128)S(1)}) custom-call(bf16[256,4096]{1,0:T(8,128)(2,1)} %x_ref.1, bf16[256,128]{1,0:T(8,128)(2,1)S(1)} %bitcast.11), custom_call_target="tpu_custom_call" | custom-call | tf_op jit(solution)/shard_map/pallas_call | solution.py:112
  28.5 0.0 collective-permute-done.ring_ref
  28.5 0.0 collective-permute-done.1.swap_ref
  28.6 0.1 collective-permute-start.2
  28.7 0.0 copy-done.7
  28.7 1.3 %collective-permute-done.2.got_ref = bf16[512,128]{1,0:T(8,128)(2,1)S(1)} collective-permute-done((bf16[512,128]{1,0:T(8,128)(2,1)S(1)}, bf16[512,128]{1,0:T(8,128)(2,1)S(1)}, u32[]{:S(2)}, u32[]{:S(2)}) %collective-permute-start.2) | collective-permute-done | bytes 131104 | tf_op jit(solution)/shard_map/ppermute | solution.py:30
  30.0 0.8 shard_map.131
  30.8 3.0 %collective-permute-start.3 = (f32[24,256]{1,0:T(8,128)S(1)}, f32[24,256]{1,0:T(8,128)S(1)}, u32[]{:S(2)}, u32[]{:S(2)}) collective-permute-start(f32[24,256]{1,0:T(8,128)S(1)} %get-tuple-element.48), channel_id=1, source_target_pairs={{0,1},{1,0},{2,3},{3,2},{4,5},{5,4},{6,7},{7,6},{8,9},{9,8},{10,11... | collective-permute-start | bytes 73736 | tf_op jit(solution)/shard_map/ppermute | solution.py:30
  33.8 0.0 copy-done
  33.8 0.0 copy-done.1
  33.8 0.0 copy-start.5
  33.8 0.0 copy-start.6
  33.8 1.9 %shard_map.132.refs_0_.p_ref = bf16[16,256,256]{2,1,0:T(8,128)(2,1)S(1)} custom-call(bf16[256,2048]{1,0:T(8,128)(2,1)S(1)} %copy-done, bf16[256,256]{1,0:T(8,128)(2,1)S(1)} %copy-done.1, f32[16,256]{1,0:T(8,128)S(1)} %get-tuple-element.47.after_ref.refs_1_), custom_call_target="tpu_custom_call" | custom-call | tf_op jit(solution)/shard_map/pallas_call | solution.py:46
  35.7 0.0 collective-permute-done.3.refs_2_
  35.7 0.6 shard_map.133
  36.3 2.0 %collective-permute-start.4 = (f32[1,256]{1,0:T(1,128)S(1)}, f32[1,256]{1,0:T(1,128)S(1)}, u32[]{:S(2)}, u32[]{:S(2)}) collective-permute-start(f32[1,256]{1,0:T(1,128)S(1)} %get-tuple-element.50.own_ref), channel_id=1, source_target_pairs={{0,1},{1,0},{2,3},{3,2},{4,5},{5,4},{6,7},{7,6},{8,9},{9,8},{10,11... | collective-permute-start | bytes 3080 | tf_op jit(solution)/shard_map/ppermute | solution.py:30
  38.3 1.7 %collective-permute-done.4.got_ref = f32[1,256]{1,0:T(1,128)S(1)} collective-permute-done((f32[1,256]{1,0:T(1,128)S(1)}, f32[1,256]{1,0:T(1,128)S(1)}, u32[]{:S(2)}, u32[]{:S(2)}) %collective-permute-start.4) | collective-permute-done | bytes 1056 | tf_op jit(solution)/shard_map/ppermute | solution.py:30
  39.9 0.0 copy-done.5
  39.9 0.0 copy-done.6
  39.9 0.8 shard_map.134
  40.8 1.9 %collective-permute-start.5 = (f32[24,256]{1,0:T(8,128)S(1)}, f32[24,256]{1,0:T(8,128)S(1)}, u32[]{:S(2)}, u32[]{:S(2)}) collective-permute-start(f32[24,256]{1,0:T(8,128)S(1)} %get-tuple-element.54.own_ref), channel_id=1, source_target_pairs={{0,1},{1,0},{2,3},{3,2},{4,5},{5,4},{6,7},{7,6},{8,9},{9,8},{10,11... | collective-permute-start | bytes 73736 | tf_op jit(solution)/shard_map/ppermute | solution.py:30
  42.7 1.9 %collective-permute-done.5.got_ref = f32[24,256]{1,0:T(8,128)S(1)} collective-permute-done((f32[24,256]{1,0:T(8,128)S(1)}, f32[24,256]{1,0:T(8,128)S(1)}, u32[]{:S(2)}, u32[]{:S(2)}) %collective-permute-start.5) | collective-permute-done | bytes 24608 | tf_op jit(solution)/shard_map/ppermute | solution.py:30
  44.6 0.6 shard_map.135
  45.2 0.1 collective-permute-start.6
  45.3 1.3 %collective-permute-done.6 = bf16[512,128]{1,0:T(8,128)(2,1)S(1)} collective-permute-done((bf16[512,128]{1,0:T(8,128)(2,1)S(1)}, bf16[512,128]{1,0:T(8,128)(2,1)S(1)}, u32[]{:S(2)}, u32[]{:S(2)}) %collective-permute-start.6) | collective-permute-done | bytes 131104 | tf_op jit(solution)/shard_map/ppermute | solution.py:30
  46.6 0.0 copy-start.3
  46.6 14.2 %all_to_all.21.refs_5_.parts_ref = bf16[32,16,128]{2,1,0:T(8,128)(2,1)S(1)} all-to-all(bf16[32,16,128]{2,1,0:T(8,128)(2,1)S(1)} %bitcast.17), channel_id=1, replica_groups=mesh['yh'=2,'x'=4,'core'=2,'z'=8,'yl'=2] {'x','z'}, dimensions={0} | all-to-all | bytes 262144 | tf_op jit(solution)/shard_map/all_to_all | solution.py:405
  60.8 0.4 shard_map.137
  61.2 11.2 %all_to_all.22.tails_ref = f32[8,32,128]{2,1,0:T(8,128)S(1)} all-to-all(f32[8,32,128]{2,1,0:T(8,128)S(1)} %shard_map.137), channel_id=1, replica_groups=mesh['yh'=2,'x'=4,'core'=2,'z'=8,'yl'=2] {'yh','core','yl'}, dimensions={0} | all-to-all | bytes 262144 | tf_op jit(solution)/shard_map/all_to_all | solution.py:408
  72.4 0.7 shard_map.138
  73.1 4.4 %all-to-all-start.3 = ((bf16[32,24,128]{2,1,0:T(8,128)(2,1)}), bf16[32,24,128]{2,1,0:T(8,128)(2,1)S(1)}, u32[]{:S(2)}, u32[]{:S(2)}) async-start(bf16[32,24,128]{2,1,0:T(8,128)(2,1)} %get-tuple-element.64), calls=%async_computation.3 | async-start | bytes 393216 | tf_op jit(solution)/shard_map/all_to_all | solution.py:411
  77.4 2.7 %shard_map.136 = (bf16[256,4096]{1,0:T(8,128)(2,1)}, f32[1,256]{1,0:T(1,128)}) custom-call(f32[32,256]{1,0:T(8,128)S(1)} %get-tuple-element.56.refs_0_, f32[1,256]{1,0:T(1,128)S(1)} %get-tuple-element.57.refs_1_, f32[1,256]{1,0:T(1,128)S(1)} %get-tuple-element.55.rms_ref.refs_2_, bf16[32,4096]{1,0:T(8,128)(2,1)S(1)} %get-tuple-element.58.refs_3_, ...), custom_call_target="tpu_custom_call" | custom-call | tf_op jit(solution)/shard_map/pallas_call | solution.py:357
  80.2 0.0 copy-done.3
  80.2 0.9 %shard_map.139 = f32[64,256]{1,0:T(8,128)} custom-call(f32[8,128]{1,0:T(8,128)S(1)} %get-tuple-element.63.z_ref, f32[16,128]{1,0:T(8,128)S(1)} %bitcast.14), custom_call_target="tpu_custom_call" | custom-call | tf_op jit(solution)/shard_map/pallas_call | solution.py:46
  81.1 7.3 %all-to-all-done.3.all_ref = bf16[32,24,128]{2,1,0:T(8,128)(2,1)S(1)} async-done(((bf16[32,24,128]{2,1,0:T(8,128)(2,1)}), bf16[32,24,128]{2,1,0:T(8,128)(2,1)S(1)}, u32[]{:S(2)}, u32[]{:S(2)}) %all-to-all-start.3) | async-done | bytes 196640 | tf_op jit(solution)/shard_map/all_to_all | solution.py:411
  88.4 0.7 shard_map.140
  (4 shorter events, 0.1 us)
Async XLA Ops:
  0.6 0.7 copy-start.2
  1.3 0.8 copy-start.4
  2.1 26.6 %copy-start.7 = (bf16[4096]{0:T(1024)(128)(2,1)S(1)}, bf16[4096]{0:T(1024)(128)(2,1)}, u32[]{:S(2)}) copy-start(bf16[4096]{0:T(1024)(128)(2,1)} %param.9) | copy-start | bytes 24580
  22.5 11.3 %copy-start = (bf16[256,2048]{1,0:T(8,128)(2,1)S(1)}, bf16[256,2048]{1,0:T(8,128)(2,1)}, u32[]{:S(2)}) copy-start(bf16[256,2048]{1,0:T(8,128)(2,1)} %q_ref.1) | copy-start | bytes 3145732
  22.5 11.3 %copy-start.1 = (bf16[256,256]{1,0:T(8,128)(2,1)S(1)}, bf16[256,256]{1,0:T(8,128)(2,1)}, u32[]{:S(2)}) copy-start(bf16[256,256]{1,0:T(8,128)(2,1)} %k_ref.1) | copy-start | bytes 393220
  22.5 6.0 %collective-permute-start = (bf16[384,128]{1,0:T(8,128)(2,1)S(1)}, bf16[384,128]{1,0:T(8,128)(2,1)S(1)}, u32[]{:S(2)}, u32[]{:S(2)}) collective-permute-start(bf16[384,128]{1,0:T(8,128)(2,1)S(1)} %shard_map.128.self_ref), channel_id=1, source_target_pairs={{1,0},{0,128},{128,129},{129,1},{3,2},{2,130},{130,131},{131,3},{5... | collective-permute-start | bytes 294920 | tf_op jit(solution)/shard_map/ppermute | solution.py:391
  25.8 2.8 %collective-permute-start.1 = (bf16[384,128]{1,0:T(8,128)(2,1)S(1)}, bf16[384,128]{1,0:T(8,128)(2,1)S(1)}, u32[]{:S(2)}, u32[]{:S(2)}) collective-permute-start(bf16[384,128]{1,0:T(8,128)(2,1)S(1)} %shard_map.128.self_ref), channel_id=1, source_target_pairs={{1,128},{128,1},{3,130},{130,3},{5,132},{132,5},{7,134},{134,7},{9... | collective-permute-start | bytes 294920 | tf_op jit(solution)/shard_map/ppermute | solution.py:392
  28.6 1.4 %collective-permute-start.2 = (bf16[512,128]{1,0:T(8,128)(2,1)S(1)}, bf16[512,128]{1,0:T(8,128)(2,1)S(1)}, u32[]{:S(2)}, u32[]{:S(2)}) collective-permute-start(bf16[512,128]{1,0:T(8,128)(2,1)S(1)} %get-tuple-element.43.own_ref.v_ref), channel_id=1, source_target_pairs={{0,16},{16,0},{1,17},{17,1},{2,18},{18,2},{3,19},{19,3},{4,20},{20... | collective-permute-start | bytes 393224 | tf_op jit(solution)/shard_map/ppermute | solution.py:30
  30.8 4.9 %collective-permute-start.3 = (f32[24,256]{1,0:T(8,128)S(1)}, f32[24,256]{1,0:T(8,128)S(1)}, u32[]{:S(2)}, u32[]{:S(2)}) collective-permute-start(f32[24,256]{1,0:T(8,128)S(1)} %get-tuple-element.48), channel_id=1, source_target_pairs={{0,1},{1,0},{2,3},{3,2},{4,5},{5,4},{6,7},{7,6},{8,9},{9,8},{10,11... | collective-permute-start | bytes 73736 | tf_op jit(solution)/shard_map/ppermute | solution.py:30
  33.8 6.1 %copy-start.5 = (f32[256]{0:T(256)S(1)}, f32[256]{0:T(256)}, u32[]{:S(2)}) copy-start(f32[256]{0:T(256)} %param.14) | copy-start | bytes 3076
  33.8 6.1 %copy-start.6 = (s32[256]{0:T(256)S(1)}, s32[256]{0:T(256)}, u32[]{:S(2)}) copy-start(s32[256]{0:T(256)} %param.15) | copy-start | bytes 3076
  36.3 3.7 %collective-permute-start.4 = (f32[1,256]{1,0:T(1,128)S(1)}, f32[1,256]{1,0:T(1,128)S(1)}, u32[]{:S(2)}, u32[]{:S(2)}) collective-permute-start(f32[1,256]{1,0:T(1,128)S(1)} %get-tuple-element.50.own_ref), channel_id=1, source_target_pairs={{0,1},{1,0},{2,3},{3,2},{4,5},{5,4},{6,7},{7,6},{8,9},{9,8},{10,11... | collective-permute-start | bytes 3080 | tf_op jit(solution)/shard_map/ppermute | solution.py:30
  40.8 3.8 %collective-permute-start.5 = (f32[24,256]{1,0:T(8,128)S(1)}, f32[24,256]{1,0:T(8,128)S(1)}, u32[]{:S(2)}, u32[]{:S(2)}) collective-permute-start(f32[24,256]{1,0:T(8,128)S(1)} %get-tuple-element.54.own_ref), channel_id=1, source_target_pairs={{0,1},{1,0},{2,3},{3,2},{4,5},{5,4},{6,7},{7,6},{8,9},{9,8},{10,11... | collective-permute-start | bytes 73736 | tf_op jit(solution)/shard_map/ppermute | solution.py:30
  45.2 1.4 %collective-permute-start.6 = (bf16[512,128]{1,0:T(8,128)(2,1)S(1)}, bf16[512,128]{1,0:T(8,128)(2,1)S(1)}, u32[]{:S(2)}, u32[]{:S(2)}) collective-permute-start(bf16[512,128]{1,0:T(8,128)(2,1)S(1)} %get-tuple-element.60), channel_id=1, source_target_pairs={{0,16},{16,0},{1,17},{17,1},{2,18},{18,2},{3,19},{19,3},{4,20},{20... | collective-permute-start | bytes 393224 | tf_op jit(solution)/shard_map/ppermute | solution.py:30
  46.6 33.5 %copy-start.3 = (f32[2048]{0:T(1024)S(1)}, f32[2048]{0:T(1024)}, u32[]{:S(2)}) copy-start(f32[2048]{0:T(1024)} %param.13) | copy-start | bytes 24580
  73.1 15.4 %all-to-all-start.3 = ((bf16[32,24,128]{2,1,0:T(8,128)(2,1)}), bf16[32,24,128]{2,1,0:T(8,128)(2,1)S(1)}, u32[]{:S(2)}, u32[]{:S(2)}) async-start(bf16[32,24,128]{2,1,0:T(8,128)(2,1)} %get-tuple-element.64), calls=%async_computation.3 | async-start | bytes 393216 | tf_op jit(solution)/shard_map/all_to_all | solution.py:411

commit v5 on v4

--- a/solution.py
+++ b/solution.py
@@ -65,21 +65,14 @@
     return lax.broadcasted_iota(jnp.int32, (rows, 128), 1) < 64
 
 
-def read_kernel(w_ref, r_ref, v_ref, w2_ref):
+def read_kernel(w_ref, r_ref, out_ref):
     parts = []
     for g in range(2):
         w = w_ref[:, g * HD : (g + 1) * HD]
-        w2_ref[g * ROWS : (g + 1) * ROWS] = w
+        out_ref[g * ROWS : (g + 1) * ROWS] = w
         parts.append(exact_dot(r_ref[g * GROUP : (g + 1) * GROUP], w.astype(F32), ((1,), (1,))))
     v = jnp.concatenate(parts, axis=1)
-    v = jnp.concatenate([v, v], axis=0).astype(BF16)
-    for i in range(16):
-        v_ref[i * 16 : (i + 1) * 16] = v
-
-
-def stack_kernel(v_ref, w_ref, out_ref):
-    out_ref[:256] = v_ref[...]
-    out_ref[256:] = w_ref[...]
+    out_ref[128:] = jnp.concatenate([v, v], axis=0).astype(BF16)
 
 
 def merge_kernel(self_ref, ring_ref, swap_ref, v_ref, w_ref):
@@ -87,10 +80,12 @@
     ring = ring_ref[...]
     own = jnp.where(straight, self_ref[...], ring)
     other = jnp.where(straight, ring, swap_ref[...])
-    v_ref[:256] = own[:256]
-    v_ref[256:] = other[:256]
-    w_ref[:128] = own[256:]
-    w_ref[128:] = other[256:]
+    w_ref[:128] = own[:128]
+    w_ref[128:] = other[:128]
+    upper = lax.broadcasted_iota(jnp.int32, (16, 128), 0) < 8
+    v = jnp.where(upper, own[128:].astype(F32), other[128:].astype(F32)).astype(BF16)
+    for i in range(32):
+        v_ref[i * 16 : (i + 1) * 16] = v
 
 
 def row_sum_of_transpose(a):
@@ -150,13 +145,13 @@
     for b in range(BLOCKS // 2):
         xi, c, zp = b // 8, b // 4 % 2, b % 4
         at = slice(b * 128, (b + 1) * 128)
+        row = (xi * 8 + 2 * zp) * 16
+        quad = jnp.where(
+            core == c, own_ref[row : row + 32].astype(F32), got_ref[row : row + 32].astype(F32)
+        )
         halves = []
         for h in range(2):
-            row = h * 256 + (xi * 8 + 2 * zp) * 8
-            pair = jnp.where(
-                core == c, own_ref[row : row + 16].astype(F32), got_ref[row : row + 16].astype(F32)
-            )
-            one, two = pair[:8], pair[8:]
+            one, two = quad[h * 8 : h * 8 + 8], quad[h * 8 + 16 : h * 8 + 24]
             halves.append(jnp.where(low, one, pltpu.roll(two, 64, 1)))
             halves.append(jnp.where(low, pltpu.roll(one, 64, 1), two))
         vt = jnp.concatenate(halves, axis=0)
@@ -264,12 +259,7 @@
     side = lax.axis_index("yl")
     xi, zi = lax.axis_index("x"), lax.axis_index("z")
     even = zi % 2 == 0
-    vs = []
-    for h in range(2):
-        at = pl.ds(pl.multiple_of(h * 256 + (xi * 4 + zi // 2) * 16, 16), 16)
-        pair = v_ref[at].astype(F32)
-        vs.append(jnp.where(even, pair[:8], pair[8:]))
-    v = jnp.concatenate(vs, axis=0)
+    v = v_ref[pl.ds(pl.multiple_of((xi * 8 + zi) * 16, 16), 16)].astype(F32)
     spot = (xi * 2 + lax.axis_index("core")) * 4 + zi // 2
     gain = jnp.zeros((1, 128), F32)
     for b in range(BLOCKS // 2):
@@ -290,7 +280,7 @@
             reads.append(exact_dot(rows[:, g * ROWS : (g + 1) * ROWS], ws[2 * h + g], ((1,), (0,))))
         tails.append(jnp.concatenate([*reads, part, rows], axis=0))
     for i in range(8):
-        tails_ref[i] = jnp.where(side == i % 2, tails[0], tails[1])
+        tails_ref[i] = jnp.where(side == i % 2, tails[0], tails[1]).astype(BF16)
 
 
 def weight_kernel(z_ref, r_ref, grad_ref):
@@ -301,14 +291,15 @@
 
 def near_kernel(tails_ref, out_ref, z_ref):
     core, side, far = lax.axis_index("core"), lax.axis_index("yl"), lax.axis_index("yh")
-    read = tails_ref[0][:HALF]
+    read = tails_ref[0].astype(F32)[:HALF]
     for i in range(1, 8):
-        read += tails_ref[i][:HALF]
-    gain = slice(HALF, HALF + 8)
-    zero = tails_ref[side][gain] + tails_ref[4 + side][gain]
-    one = tails_ref[2 + side][gain] + tails_ref[6 + side][gain]
-    at = 2 * core + far
-    z_ref[...] = tails_ref[at][HALF + 8 :] + tails_ref[4 + at][HALF + 8 :]
+        read += tails_ref[i].astype(F32)[:HALF]
+
+    def pair(i):
+        return tails_ref[i].astype(F32) + tails_ref[4 + i].astype(F32)
+
+    zero, one = pair(side)[HALF : HALF + 8], pair(2 + side)[HALF : HALF + 8]
+    z_ref[...] = pair(2 * core + far)[HALF + 8 :]
     tail = jnp.concatenate([read, jnp.where(left_lanes(8), zero, one)], axis=0).astype(BF16)
     for i in range(32):
         out_ref[i] = tail
@@ -381,20 +372,17 @@
 def shards(hidden_states, norm_gain, value_weight, queries, keys, readout, targets, scored):
     width = hidden_states.shape[1] * 2
     read = readout.reshape(HALF, HD)
-    v, w = whole(
-        read_kernel, [shape(256, 128, dtype=BF16), shape(128, 128, dtype=BF16)], value_weight, read
-    )
-    v = lax.all_to_all(v.reshape(32, 8, 128), PLANE, 0, 0).reshape(256, 128)
-    v, norm_gain, targets, scored = together(v, norm_gain, targets, scored)
-    gain = norm_gain[None]
-    both = whole(stack_kernel, shape(384, 128, dtype=BF16), v, w)
+    both = whole(read_kernel, shape(144, 128, dtype=BF16), value_weight, read)
     first = lax.ppermute(both, ("yh", "yl"), [(1, 0), (0, 2), (2, 3), (3, 1)])
     second = lax.ppermute(both, ("yh", "yl"), [(1, 2), (2, 1)])
-    x, ss = load(hidden_states, v)
+    x, ss = load(hidden_states, both)
     first, second, ss = together(first, second, ss)
     v, weight = whole(
         merge_kernel, [shape(512, 128, dtype=BF16), shape(256, 128, dtype=BF16)], both, first, second
     )
+    v = lax.all_to_all(v.reshape(32, HALF, 128), PLANE, 0, 0).reshape(512, 128)
+    v, norm_gain, targets, scored = together(v, norm_gain, targets, scored)
+    gain = norm_gain[None]
     gvt, u, send = project(v, swap(v, "core"), gain, x, ss)
     probs = attention(queries, keys, u)
     part, u, rms = make_values(width, probs, u, swap(send, "yl"), ss)
@@ -404,7 +392,7 @@
     z = (keep + swap(send, "core").astype(F32)).astype(BF16).reshape(32, HALF, 128)
     z = lax.all_to_all(z, PLANE, 0, 0)
     grad_input, log_scale = input_grad(width, c, dot, rms, gvt, x, z)
-    tails = whole(sum_kernel, shape(8, HALF + 16, 128), z, gain, v, weight)
+    tails = whole(sum_kernel, shape(8, HALF + 16, 128, dtype=BF16), z, gain, v, weight)
     tails = lax.all_to_all(tails, NEAR, 0, 0)
     tails, z = whole(near_kernel, [shape(32, HALF + 8, 128, dtype=BF16), shape(8, 128)], tails)
     grad_weight = whole(weight_kernel, shape(ROWS, 2 * HD), z, read)

time: 89.6 us -> 89 us (level)
    pallas_call x12 -> x11, Pallas kernels: 7.55 us -> 7.53 us  [whole(): pl.pallas_call(body, in_specs=[VMEM] * len(args), out_specs=[VMEM] * len(...]
where the time goes in v5:
time: 89 us; the launch traced here: 88.6 us
  blocking collectives  45.2 us (51%)
  starting transfers between devices  14.8 us (17%)
  waiting for transfers between devices  13.9 us (16%)
  Pallas kernels  12.3 us (14%)
  local copies, waits for them, and re-layouts  1.48 us (2%)
    all_to_all x1, blocking collectives, shards(): v = lax.all_to_all(v.reshape(32, HALF, 128), PLANE, 0, 0).reshape(512, 128)  20.7 us
    all_to_all x1, blocking collectives, shards(): z = lax.all_to_all(z, PLANE, 0, 0)  14.1 us
    all_to_all x1, blocking collectives, shards(): tails = lax.all_to_all(tails, NEAR, 0, 0)  10.4 us
    all_to_all x1, waiting for transfers between devices, shards(): tails = lax.all_to_all(tails, PLANE, 0, 0)  7.59 us
    pallas_call x11, Pallas kernels, whole(): pl.pallas_call(body, in_specs=[VMEM] * len(args), out_specs=[VMEM] * len(...  7.53 us
    ppermute x5, starting transfers between devices, swap(): return lax.ppermute(v, axis, [(0, 1), (1, 0)])  6.56 us
    ppermute x5, waiting for transfers between devices, swap(): return lax.ppermute(v, axis, [(0, 1), (1, 0)])  6.29 us
    all_to_all x1, starting transfers between devices, shards(): tails = lax.all_to_all(tails, PLANE, 0, 0)  4.35 us
  transfers between devices with their start and end apart: 8, of which 5 were waited for; matrix products, arithmetic and copies ran while one was open for 0% of the time, Pallas kernels for 9%

profile of v5, /device:TPU:32, one launch (start us, length us, event | category | flops | bytes accessed | tf_op | source)
XLA Modules:
  0.0 88.6 jit_solution(10089030906125396249)
XLA Ops:
  0.6 0.0 copy-start.2
  0.6 0.7 copy-done.2
  1.3 0.0 copy-start.4
  1.3 0.8 copy-done.4
  2.1 0.0 copy-start.7
  2.1 0.2 shard_map.127.after_ref.self_ref
  2.3 0.0 copy-start
  2.3 0.0 copy-start.1
  2.3 3.3 %collective-permute-start = (bf16[144,128]{1,0:T(8,128)(2,1)S(1)}, bf16[144,128]{1,0:T(8,128)(2,1)S(1)}, u32[]{:S(2)}, u32[]{:S(2)}) collective-permute-start(bf16[144,128]{1,0:T(8,128)(2,1)S(1)} %shard_map.127.after_ref.self_ref), channel_id=1, source_target_pairs={{1,0},{0,128},{128,129},{129,1},{3,2},{2,130},{130,131},{131,3},{5... | collective-permute-start | bytes 110600 | tf_op jit(solution)/shard_map/ppermute | solution.py:376
  5.6 0.7 collective-permute-start.1
  6.2 2.1 %shard_map.128 = (bf16[256,4096]{1,0:T(8,128)(2,1)S(1)}, f32[1,256]{1,0:T(1,128)S(1)}) custom-call(bf16[256,4096]{1,0:T(8,128)(2,1)} %x_ref.1, bf16[144,128]{1,0:T(8,128)(2,1)S(1)} %shard_map.127.after_ref.self_ref), custom_call_target="tpu_custom_call" | custom-call | tf_op jit(solution)/shard_map/pallas_call | solution.py:107
  8.3 0.0 collective-permute-done.ring_ref
  8.3 0.0 collective-permute-done.1.swap_ref
  8.4 20.7 %all_to_all.20 = bf16[32,16,128]{2,1,0:T(8,128)(2,1)S(1)} all-to-all(bf16[32,16,128]{2,1,0:T(8,128)(2,1)S(1)} %bitcast.13), channel_id=1, replica_groups=mesh['yh'=2,'x'=4,'core'=2,'z'=8,'yl'=2] {'x','z'}, dimensions={0} | all-to-all | bytes 262144 | tf_op jit(solution)/shard_map/all_to_all | solution.py:383
  29.1 0.0 collective-permute-start.2
  29.1 0.0 copy-done.7
  29.1 1.3 %collective-permute-done.2.got_ref = bf16[512,128]{1,0:T(8,128)(2,1)S(1)} collective-permute-done((bf16[512,128]{1,0:T(8,128)(2,1)S(1)}, bf16[512,128]{1,0:T(8,128)(2,1)S(1)}, u32[]{:S(2)}, u32[]{:S(2)}) %collective-permute-start.2) | collective-permute-done | bytes 131104 | tf_op jit(solution)/shard_map/ppermute | solution.py:30
  30.4 0.8 shard_map.130
  31.2 2.6 %collective-permute-start.3 = (f32[24,256]{1,0:T(8,128)S(1)}, f32[24,256]{1,0:T(8,128)S(1)}, u32[]{:S(2)}, u32[]{:S(2)}) collective-permute-start(f32[24,256]{1,0:T(8,128)S(1)} %get-tuple-element.44), channel_id=1, source_target_pairs={{0,1},{1,0},{2,3},{3,2},{4,5},{5,4},{6,7},{7,6},{8,9},{9,8},{10,11... | collective-permute-start | bytes 73736 | tf_op jit(solution)/shard_map/ppermute | solution.py:30
  33.8 0.0 copy-done
  33.8 0.0 copy-done.1
  33.8 0.0 copy-start.5
  33.8 0.0 copy-start.6
  33.8 1.9 %shard_map.131.refs_0_.p_ref = bf16[16,256,256]{2,1,0:T(8,128)(2,1)S(1)} custom-call(bf16[256,2048]{1,0:T(8,128)(2,1)S(1)} %copy-done, bf16[256,256]{1,0:T(8,128)(2,1)S(1)} %copy-done.1, f32[16,256]{1,0:T(8,128)S(1)} %get-tuple-element.43.after_ref.refs_1_), custom_call_target="tpu_custom_call" | custom-call | tf_op jit(solution)/shard_map/pallas_call | solution.py:46
  35.7 0.0 collective-permute-done.3.refs_2_
  35.7 0.6 shard_map.132
  36.3 2.0 %collective-permute-start.4 = (f32[1,256]{1,0:T(1,128)S(1)}, f32[1,256]{1,0:T(1,128)S(1)}, u32[]{:S(2)}, u32[]{:S(2)}) collective-permute-start(f32[1,256]{1,0:T(1,128)S(1)} %get-tuple-element.46.own_ref), channel_id=1, source_target_pairs={{0,1},{1,0},{2,3},{3,2},{4,5},{5,4},{6,7},{7,6},{8,9},{9,8},{10,11... | collective-permute-start | bytes 3080 | tf_op jit(solution)/shard_map/ppermute | solution.py:30
  38.3 1.7 %collective-permute-done.4.got_ref = f32[1,256]{1,0:T(1,128)S(1)} collective-permute-done((f32[1,256]{1,0:T(1,128)S(1)}, f32[1,256]{1,0:T(1,128)S(1)}, u32[]{:S(2)}, u32[]{:S(2)}) %collective-permute-start.4) | collective-permute-done | bytes 1056 | tf_op jit(solution)/shard_map/ppermute | solution.py:30
  39.9 0.0 copy-done.5
  39.9 0.0 copy-done.6
  39.9 0.8 shard_map.133
  40.8 1.9 %collective-permute-start.5 = (f32[24,256]{1,0:T(8,128)S(1)}, f32[24,256]{1,0:T(8,128)S(1)}, u32[]{:S(2)}, u32[]{:S(2)}) collective-permute-start(f32[24,256]{1,0:T(8,128)S(1)} %get-tuple-element.50.own_ref), channel_id=1, source_target_pairs={{0,1},{1,0},{2,3},{3,2},{4,5},{5,4},{6,7},{7,6},{8,9},{9,8},{10,11... | collective-permute-start | bytes 73736 | tf_op jit(solution)/shard_map/ppermute | solution.py:30
  42.6 1.9 %collective-permute-done.5.got_ref = f32[24,256]{1,0:T(8,128)S(1)} collective-permute-done((f32[24,256]{1,0:T(8,128)S(1)}, f32[24,256]{1,0:T(8,128)S(1)}, u32[]{:S(2)}, u32[]{:S(2)}) %collective-permute-start.5) | collective-permute-done | bytes 24608 | tf_op jit(solution)/shard_map/ppermute | solution.py:30
  44.6 0.6 shard_map.134
  45.2 0.1 collective-permute-start.6
  45.3 1.3 %collective-permute-done.6 = bf16[512,128]{1,0:T(8,128)(2,1)S(1)} collective-permute-done((bf16[512,128]{1,0:T(8,128)(2,1)S(1)}, bf16[512,128]{1,0:T(8,128)(2,1)S(1)}, u32[]{:S(2)}, u32[]{:S(2)}) %collective-permute-start.6) | collective-permute-done | bytes 131104 | tf_op jit(solution)/shard_map/ppermute | solution.py:30
  46.6 0.0 copy-start.3
  46.6 14.1 %all_to_all.21.refs_5_.parts_ref = bf16[32,16,128]{2,1,0:T(8,128)(2,1)S(1)} all-to-all(bf16[32,16,128]{2,1,0:T(8,128)(2,1)S(1)} %bitcast.18), channel_id=1, replica_groups=mesh['yh'=2,'x'=4,'core'=2,'z'=8,'yl'=2] {'x','z'}, dimensions={0} | all-to-all | bytes 262144 | tf_op jit(solution)/shard_map/all_to_all | solution.py:393
  60.7 0.4 shard_map.136
  61.1 10.4 %all_to_all.22.tails_ref = bf16[8,32,128]{2,1,0:T(8,128)(2,1)S(1)} all-to-all(bf16[8,32,128]{2,1,0:T(8,128)(2,1)S(1)} %shard_map.136), channel_id=1, replica_groups=mesh['yh'=2,'x'=4,'core'=2,'z'=8,'yl'=2] {'yh','core','yl'}, dimensions={0} | all-to-all | bytes 131072 | tf_op jit(solution)/shard_map/all_to_all | solution.py:396
  71.5 0.7 shard_map.137
  72.2 4.4 %all-to-all-start.3 = ((bf16[32,24,128]{2,1,0:T(8,128)(2,1)}), bf16[32,24,128]{2,1,0:T(8,128)(2,1)S(1)}, u32[]{:S(2)}, u32[]{:S(2)}) async-start(bf16[32,24,128]{2,1,0:T(8,128)(2,1)} %get-tuple-element.60), calls=%async_computation.3 | async-start | bytes 393216 | tf_op jit(solution)/shard_map/all_to_all | solution.py:399
  76.6 2.7 %shard_map.135 = (bf16[256,4096]{1,0:T(8,128)(2,1)}, f32[1,256]{1,0:T(1,128)}) custom-call(f32[32,256]{1,0:T(8,128)S(1)} %get-tuple-element.52.refs_0_, f32[1,256]{1,0:T(1,128)S(1)} %get-tuple-element.53.refs_1_, f32[1,256]{1,0:T(1,128)S(1)} %get-tuple-element.51.rms_ref.refs_2_, bf16[32,4096]{1,0:T(8,128)(2,1)S(1)} %get-tuple-element.54.refs_3_, ...), custom_call_target="tpu_custom_call" | custom-call | tf_op jit(solution)/shard_map/pallas_call | solution.py:348
  79.3 0.0 copy-done.3
  79.3 0.9 %shard_map.138 = f32[64,256]{1,0:T(8,128)} custom-call(f32[8,128]{1,0:T(8,128)S(1)} %get-tuple-element.59.z_ref, f32[16,128]{1,0:T(8,128)S(1)} %bitcast.15), custom_call_target="tpu_custom_call" | custom-call | tf_op jit(solution)/shard_map/pallas_call | solution.py:46
  80.3 7.6 %all-to-all-done.3.all_ref = bf16[32,24,128]{2,1,0:T(8,128)(2,1)S(1)} async-done(((bf16[32,24,128]{2,1,0:T(8,128)(2,1)}), bf16[32,24,128]{2,1,0:T(8,128)(2,1)S(1)}, u32[]{:S(2)}, u32[]{:S(2)}) %all-to-all-start.3) | async-done | bytes 196640 | tf_op jit(solution)/shard_map/all_to_all | solution.py:399
  87.9 0.7 shard_map.139
  (3 shorter events, 0.1 us)
Async XLA Ops:
  0.6 0.7 copy-start.2
  1.3 0.8 copy-start.4
  2.1 27.0 %copy-start.7 = (bf16[4096]{0:T(1024)(128)(2,1)S(1)}, bf16[4096]{0:T(1024)(128)(2,1)}, u32[]{:S(2)}) copy-start(bf16[4096]{0:T(1024)(128)(2,1)} %param.9) | copy-start | bytes 24580
  2.3 31.5 %copy-start = (bf16[256,2048]{1,0:T(8,128)(2,1)S(1)}, bf16[256,2048]{1,0:T(8,128)(2,1)}, u32[]{:S(2)}) copy-start(bf16[256,2048]{1,0:T(8,128)(2,1)} %q_ref.1) | copy-start | bytes 3145732
  2.3 31.5 %copy-start.1 = (bf16[256,256]{1,0:T(8,128)(2,1)S(1)}, bf16[256,256]{1,0:T(8,128)(2,1)}, u32[]{:S(2)}) copy-start(bf16[256,256]{1,0:T(8,128)(2,1)} %k_ref.1) | copy-start | bytes 393220
  2.3 6.0 %collective-permute-start = (bf16[144,128]{1,0:T(8,128)(2,1)S(1)}, bf16[144,128]{1,0:T(8,128)(2,1)S(1)}, u32[]{:S(2)}, u32[]{:S(2)}) collective-permute-start(bf16[144,128]{1,0:T(8,128)(2,1)S(1)} %shard_map.127.after_ref.self_ref), channel_id=1, source_target_pairs={{1,0},{0,128},{128,129},{129,1},{3,2},{2,130},{130,131},{131,3},{5... | collective-permute-start | bytes 110600 | tf_op jit(solution)/shard_map/ppermute | solution.py:376
  5.6 2.8 %collective-permute-start.1 = (bf16[144,128]{1,0:T(8,128)(2,1)S(1)}, bf16[144,128]{1,0:T(8,128)(2,1)S(1)}, u32[]{:S(2)}, u32[]{:S(2)}) collective-permute-start(bf16[144,128]{1,0:T(8,128)(2,1)S(1)} %shard_map.127.after_ref.self_ref), channel_id=1, source_target_pairs={{1,128},{128,1},{3,130},{130,3},{5,132},{132,5},{7,134},{134,7},{9... | collective-permute-start | bytes 110600 | tf_op jit(solution)/shard_map/ppermute | solution.py:377
  29.1 1.3 %collective-permute-start.2 = (bf16[512,128]{1,0:T(8,128)(2,1)S(1)}, bf16[512,128]{1,0:T(8,128)(2,1)S(1)}, u32[]{:S(2)}, u32[]{:S(2)}) collective-permute-start(bf16[512,128]{1,0:T(8,128)(2,1)S(1)} %bitcast.10), channel_id=1, source_target_pairs={{0,16},{16,0},{1,17},{17,1},{2,18},{18,2},{3,19},{19,3},{4,20},{20... | collective-permute-start | bytes 393224 | tf_op jit(solution)/shard_map/ppermute | solution.py:30
  31.2 4.5 %collective-permute-start.3 = (f32[24,256]{1,0:T(8,128)S(1)}, f32[24,256]{1,0:T(8,128)S(1)}, u32[]{:S(2)}, u32[]{:S(2)}) collective-permute-start(f32[24,256]{1,0:T(8,128)S(1)} %get-tuple-element.44), channel_id=1, source_target_pairs={{0,1},{1,0},{2,3},{3,2},{4,5},{5,4},{6,7},{7,6},{8,9},{9,8},{10,11... | collective-permute-start | bytes 73736 | tf_op jit(solution)/shard_map/ppermute | solution.py:30
  33.8 6.1 %copy-start.5 = (f32[256]{0:T(256)S(1)}, f32[256]{0:T(256)}, u32[]{:S(2)}) copy-start(f32[256]{0:T(256)} %param.14) | copy-start | bytes 3076
  33.8 6.1 %copy-start.6 = (s32[256]{0:T(256)S(1)}, s32[256]{0:T(256)}, u32[]{:S(2)}) copy-start(s32[256]{0:T(256)} %param.15) | copy-start | bytes 3076
  36.3 3.7 %collective-permute-start.4 = (f32[1,256]{1,0:T(1,128)S(1)}, f32[1,256]{1,0:T(1,128)S(1)}, u32[]{:S(2)}, u32[]{:S(2)}) collective-permute-start(f32[1,256]{1,0:T(1,128)S(1)} %get-tuple-element.46.own_ref), channel_id=1, source_target_pairs={{0,1},{1,0},{2,3},{3,2},{4,5},{5,4},{6,7},{7,6},{8,9},{9,8},{10,11... | collective-permute-start | bytes 3080 | tf_op jit(solution)/shard_map/ppermute | solution.py:30
  40.8 3.8 %collective-permute-start.5 = (f32[24,256]{1,0:T(8,128)S(1)}, f32[24,256]{1,0:T(8,128)S(1)}, u32[]{:S(2)}, u32[]{:S(2)}) collective-permute-start(f32[24,256]{1,0:T(8,128)S(1)} %get-tuple-element.50.own_ref), channel_id=1, source_target_pairs={{0,1},{1,0},{2,3},{3,2},{4,5},{5,4},{6,7},{7,6},{8,9},{9,8},{10,11... | collective-permute-start | bytes 73736 | tf_op jit(solution)/shard_map/ppermute | solution.py:30
  45.2 1.4 %collective-permute-start.6 = (bf16[512,128]{1,0:T(8,128)(2,1)S(1)}, bf16[512,128]{1,0:T(8,128)(2,1)S(1)}, u32[]{:S(2)}, u32[]{:S(2)}) collective-permute-start(bf16[512,128]{1,0:T(8,128)(2,1)S(1)} %get-tuple-element.56), channel_id=1, source_target_pairs={{0,16},{16,0},{1,17},{17,1},{2,18},{18,2},{3,19},{19,3},{4,20},{20... | collective-permute-start | bytes 393224 | tf_op jit(solution)/shard_map/ppermute | solution.py:30
  46.6 32.7 %copy-start.3 = (f32[2048]{0:T(1024)S(1)}, f32[2048]{0:T(1024)}, u32[]{:S(2)}) copy-start(f32[2048]{0:T(1024)} %param.13) | copy-start | bytes 24580
  72.2 15.6 %all-to-all-start.3 = ((bf16[32,24,128]{2,1,0:T(8,128)(2,1)}), bf16[32,24,128]{2,1,0:T(8,128)(2,1)S(1)}, u32[]{:S(2)}, u32[]{:S(2)}) async-start(bf16[32,24,128]{2,1,0:T(8,128)(2,1)} %get-tuple-element.60), calls=%async_computation.3 | async-start | bytes 393216 | tf_op jit(solution)/shard_map/all_to_all | solution.py:399

commit v6 on v5

--- a/solution.py
+++ b/solution.py
@@ -65,25 +65,20 @@
     return lax.broadcasted_iota(jnp.int32, (rows, 128), 1) < 64
 
 
-def read_kernel(w_ref, r_ref, out_ref):
+def read_kernel(ring_ref, swap_ref, r_ref, other_r_ref, v_ref, w_both_ref):
+    straight = lax.axis_index("yh") == lax.axis_index("yl")
+    ring, pair = ring_ref[...], swap_ref[...]
+    own = jnp.where(straight, pair, ring)
+    other = jnp.where(straight, ring, pair)
     parts = []
-    for g in range(2):
-        w = w_ref[:, g * HD : (g + 1) * HD]
-        out_ref[g * ROWS : (g + 1) * ROWS] = w
-        parts.append(exact_dot(r_ref[g * GROUP : (g + 1) * GROUP], w.astype(F32), ((1,), (1,))))
-    v = jnp.concatenate(parts, axis=1)
-    out_ref[128:] = jnp.concatenate([v, v], axis=0).astype(BF16)
-
-
-def merge_kernel(self_ref, ring_ref, swap_ref, v_ref, w_ref):
-    straight = lax.axis_index("yh") == lax.axis_index("yl")
-    ring = ring_ref[...]
-    own = jnp.where(straight, self_ref[...], ring)
-    other = jnp.where(straight, ring, swap_ref[...])
-    w_ref[:128] = own[:128]
-    w_ref[128:] = other[:128]
-    upper = lax.broadcasted_iota(jnp.int32, (16, 128), 0) < 8
-    v = jnp.where(upper, own[128:].astype(F32), other[128:].astype(F32)).astype(BF16)
+    for i, (w, r) in enumerate(((own, r_ref), (other, other_r_ref))):
+        halves = []
+        for g in range(2):
+            wg = w[:, g * HD : (g + 1) * HD]
+            w_both_ref[(2 * i + g) * ROWS : (2 * i + g + 1) * ROWS] = wg
+            halves.append(exact_dot(r[g * GROUP : (g + 1) * GROUP], wg.astype(F32), ((1,), (1,))))
+        parts.append(jnp.concatenate(halves, axis=1))
+    v = jnp.concatenate(parts, axis=0).astype(BF16)
     for i in range(32):
         v_ref[i * 16 : (i + 1) * 16] = v
 
@@ -372,13 +367,15 @@
 def shards(hidden_states, norm_gain, value_weight, queries, keys, readout, targets, scored):
     width = hidden_states.shape[1] * 2
     read = readout.reshape(HALF, HD)
-    both = whole(read_kernel, shape(144, 128, dtype=BF16), value_weight, read)
-    first = lax.ppermute(both, ("yh", "yl"), [(1, 0), (0, 2), (2, 3), (3, 1)])
-    second = lax.ppermute(both, ("yh", "yl"), [(1, 2), (2, 1)])
-    x, ss = load(hidden_states, both)
-    first, second, ss = together(first, second, ss)
+    other_read = swap(read, "yl")
+    ring = lax.ppermute(value_weight, ("yh", "yl"), [(1, 0), (0, 2), (2, 3), (3, 1)])
+    pair = cross(value_weight)
+    x, ss = load(hidden_states, norm_gain)
+    ring, pair, other_read, ss = together(ring, pair, other_read, ss)
     v, weight = whole(
-        merge_kernel, [shape(512, 128, dtype=BF16), shape(256, 128, dtype=BF16)], both, first, second
+        read_kernel,
+        [shape(512, 128, dtype=BF16), shape(256, 128, dtype=BF16)],
+        ring, pair, read, other_read,
     )
     v = lax.all_to_all(v.reshape(32, HALF, 128), PLANE, 0, 0).reshape(512, 128)
     v, norm_gain, targets, scored = together(v, norm_gain, targets, scored)

time: 89 us -> 88 us (0.989)
  waiting for transfers between devices: 13.9 us -> 16.5 us
  blocking collectives: 45.2 us -> 42.9 us
    ppermute x5 -> x6, waiting for transfers between devices: 6.29 us -> 8.9 us  [swap(): return lax.ppermute(v, axis, [(0, 1), (1, 0)])]
    all_to_all x1, blocking collectives: 10.4 us -> 8.01 us  [shards(): tails = lax.all_to_all(tails, NEAR, 0, 0)]
    ppermute x5 -> x6, starting transfers between devices: 6.56 us -> 5.12 us  [swap(): return lax.ppermute(v, axis, [(0, 1), (1, 0)])]
    pallas_call x11 -> x10, Pallas kernels: 7.53 us -> 7.7 us  [whole(): pl.pallas_call(body, in_specs=[VMEM] * len(args), out_specs=[VMEM] * len(...]
  transfers between devices with their start and end apart: 8 -> 9, of which waited for: 5 -> 6; matrix products, arithmetic and copies ran while one was open for 0% -> 0% of each run, Pallas kernels for 9% -> 9%
where the time goes in v6:
time: 88 us; the launch traced here: 87.5 us
  blocking collectives  42.9 us (49%)
  waiting for transfers between devices  16.5 us (19%)
  starting transfers between devices  14.1 us (16%)
  Pallas kernels  12.5 us (14%)
    all_to_all x1, blocking collectives, shards(): v = lax.all_to_all(v.reshape(32, HALF, 128), PLANE, 0, 0).reshape(512, 128)  20.7 us
    all_to_all x1, blocking collectives, shards(): z = lax.all_to_all(z, PLANE, 0, 0)  14.2 us
    ppermute x6, waiting for transfers between devices, swap(): return lax.ppermute(v, axis, [(0, 1), (1, 0)])  8.9 us
    all_to_all x1, blocking collectives, shards(): tails = lax.all_to_all(tails, NEAR, 0, 0)  8.01 us
    pallas_call x10, Pallas kernels, whole(): pl.pallas_call(body, in_specs=[VMEM] * len(args), out_specs=[VMEM] * len(...  7.7 us
    all_to_all x1, waiting for transfers between devices, shards(): tails = lax.all_to_all(tails, PLANE, 0, 0)  7.6 us
    ppermute x6, starting transfers between devices, swap(): return lax.ppermute(v, axis, [(0, 1), (1, 0)])  5.12 us
    all_to_all x1, starting transfers between devices, shards(): tails = lax.all_to_all(tails, PLANE, 0, 0)  4.35 us
  transfers between devices with their start and end apart: 9, of which 6 were waited for; matrix products, arithmetic and copies ran while one was open for 0% of the time, Pallas kernels for 9%

profile of v6, /device:TPU:32, one launch (start us, length us, event | category | flops | bytes accessed | tf_op | source)
XLA Modules:
  0.0 87.5 jit_solution(6848604256296687446)
XLA Ops:
  0.6 3.3 %collective-permute-start = (bf16[64,256]{1,0:T(8,128)(2,1)}, bf16[64,256]{1,0:T(8,128)(2,1)S(1)}, u32[]{:S(2)}, u32[]{:S(2)}) collective-permute-start(bf16[64,256]{1,0:T(8,128)(2,1)} %param.10), channel_id=1, source_target_pairs={{1,0},{0,128},{128,129},{129,1},{3,2},{2,130},{130,131},{131,3},{5... | collective-permute-start | bytes 98312 | tf_op jit(solution)/shard_map/ppermute | solution.py:371
  3.9 1.4 %collective-permute-start.1 = (bf16[64,256]{1,0:T(8,128)(2,1)}, bf16[64,256]{1,0:T(8,128)(2,1)S(1)}, u32[]{:S(2)}, u32[]{:S(2)}) collective-permute-start(bf16[64,256]{1,0:T(8,128)(2,1)} %param.10), channel_id=1, source_target_pairs={{0,0},{1,128},{128,1},{129,129},{2,2},{3,130},{130,3},{131,131},{4... | collective-permute-start | bytes 98312 | tf_op jit(solution)/shard_map/ppermute | solution.py:34
  5.3 0.0 copy-start
  5.3 0.0 copy-start.1
  5.3 1.8 %collective-permute-start.2 = (f32[16,128]{1,0:T(8,128)}, f32[16,128]{1,0:T(8,128)S(1)}, u32[]{:S(2)}, u32[]{:S(2)}) collective-permute-start(f32[16,128]{1,0:T(8,128)} %bitcast.14), channel_id=1, source_target_pairs={{0,1},{1,0},{2,3},{3,2},{4,5},{5,4},{6,7},{7,6},{8,9},{9,8},{10,11... | collective-permute-start | bytes 24584 | tf_op jit(solution)/shard_map/ppermute | solution.py:30
  7.2 0.0 copy-start.2
  7.2 0.7 copy-done.2
  7.9 0.0 copy-start.3
  7.9 2.1 %shard_map.127 = (bf16[256,4096]{1,0:T(8,128)(2,1)S(1)}, f32[1,256]{1,0:T(1,128)S(1)}) custom-call(bf16[256,4096]{1,0:T(8,128)(2,1)} %x_ref.1, bf16[4096]{0:T(1024)(128)(2,1)S(1)} %copy-done.2), custom_call_target="tpu_custom_call" | custom-call | tf_op jit(solution)/shard_map/pallas_call | solution.py:102
  10.0 0.0 collective-permute-done.2.other_r_ref
  10.0 0.0 collective-permute-done.ring_ref
  10.0 0.0 collective-permute-done.1.swap_ref
  10.0 0.0 copy-done.3
  10.0 0.4 shard_map.128
  10.4 20.7 %all_to_all.20 = bf16[32,16,128]{2,1,0:T(8,128)(2,1)S(1)} all-to-all(bf16[32,16,128]{2,1,0:T(8,128)(2,1)S(1)} %bitcast.13), channel_id=1, replica_groups=mesh['yh'=2,'x'=4,'core'=2,'z'=8,'yl'=2] {'x','z'}, dimensions={0} | all-to-all | bytes 262144 | tf_op jit(solution)/shard_map/all_to_all | solution.py:380
  31.1 0.0 collective-permute-start.3
  31.1 1.3 %collective-permute-done.3.got_ref = bf16[512,128]{1,0:T(8,128)(2,1)S(1)} collective-permute-done((bf16[512,128]{1,0:T(8,128)(2,1)S(1)}, bf16[512,128]{1,0:T(8,128)(2,1)S(1)}, u32[]{:S(2)}, u32[]{:S(2)}) %collective-permute-start.3) | collective-permute-done | bytes 131104 | tf_op jit(solution)/shard_map/ppermute | solution.py:30
  32.4 0.8 shard_map.129
  33.2 1.1 %collective-permute-start.4 = (f32[24,256]{1,0:T(8,128)S(1)}, f32[24,256]{1,0:T(8,128)S(1)}, u32[]{:S(2)}, u32[]{:S(2)}) collective-permute-start(f32[24,256]{1,0:T(8,128)S(1)} %get-tuple-element.46), channel_id=1, source_target_pairs={{0,1},{1,0},{2,3},{3,2},{4,5},{5,4},{6,7},{7,6},{8,9},{9,8},{10,11... | collective-permute-start | bytes 73736 | tf_op jit(solution)/shard_map/ppermute | solution.py:30
  34.2 0.0 copy-done
  34.2 0.0 copy-done.1
  34.2 0.0 copy-start.4
  34.3 0.0 copy-start.5
  34.3 1.9 %shard_map.130.refs_0_.p_ref = bf16[16,256,256]{2,1,0:T(8,128)(2,1)S(1)} custom-call(bf16[256,2048]{1,0:T(8,128)(2,1)S(1)} %copy-done, bf16[256,256]{1,0:T(8,128)(2,1)S(1)} %copy-done.1, f32[16,256]{1,0:T(8,128)S(1)} %get-tuple-element.45.after_ref.refs_1_), custom_call_target="tpu_custom_call" | custom-call | tf_op jit(solution)/shard_map/pallas_call | solution.py:46
  36.2 0.9 collective-permute-done.4.refs_2_
  37.1 0.6 shard_map.131
  37.6 1.1 %collective-permute-start.5 = (f32[1,256]{1,0:T(1,128)S(1)}, f32[1,256]{1,0:T(1,128)S(1)}, u32[]{:S(2)}, u32[]{:S(2)}) collective-permute-start(f32[1,256]{1,0:T(1,128)S(1)} %get-tuple-element.48.own_ref), channel_id=1, source_target_pairs={{0,1},{1,0},{2,3},{3,2},{4,5},{5,4},{6,7},{7,6},{8,9},{9,8},{10,11... | collective-permute-start | bytes 3080 | tf_op jit(solution)/shard_map/ppermute | solution.py:30
  38.7 2.5 %collective-permute-done.5.got_ref = f32[1,256]{1,0:T(1,128)S(1)} collective-permute-done((f32[1,256]{1,0:T(1,128)S(1)}, f32[1,256]{1,0:T(1,128)S(1)}, u32[]{:S(2)}, u32[]{:S(2)}) %collective-permute-start.5) | collective-permute-done | bytes 1056 | tf_op jit(solution)/shard_map/ppermute | solution.py:30
  41.3 0.0 copy-done.4
  41.3 0.0 copy-done.5
  41.3 0.8 shard_map.132
  42.1 1.0 %collective-permute-start.6 = (f32[24,256]{1,0:T(8,128)S(1)}, f32[24,256]{1,0:T(8,128)S(1)}, u32[]{:S(2)}, u32[]{:S(2)}) collective-permute-start(f32[24,256]{1,0:T(8,128)S(1)} %get-tuple-element.52.own_ref), channel_id=1, source_target_pairs={{0,1},{1,0},{2,3},{3,2},{4,5},{5,4},{6,7},{7,6},{8,9},{9,8},{10,11... | collective-permute-start | bytes 73736 | tf_op jit(solution)/shard_map/ppermute | solution.py:30
  43.1 2.8 %collective-permute-done.6.got_ref = f32[24,256]{1,0:T(8,128)S(1)} collective-permute-done((f32[24,256]{1,0:T(8,128)S(1)}, f32[24,256]{1,0:T(8,128)S(1)}, u32[]{:S(2)}, u32[]{:S(2)}) %collective-permute-start.6) | collective-permute-done | bytes 24608 | tf_op jit(solution)/shard_map/ppermute | solution.py:30
  45.9 0.6 shard_map.133
  46.5 0.1 collective-permute-start.7
  46.6 1.3 %collective-permute-done.7 = bf16[512,128]{1,0:T(8,128)(2,1)S(1)} collective-permute-done((bf16[512,128]{1,0:T(8,128)(2,1)S(1)}, bf16[512,128]{1,0:T(8,128)(2,1)S(1)}, u32[]{:S(2)}, u32[]{:S(2)}) %collective-permute-start.7) | collective-permute-done | bytes 131104 | tf_op jit(solution)/shard_map/ppermute | solution.py:30
  48.0 14.2 %all_to_all.21.refs_5_.parts_ref = bf16[32,16,128]{2,1,0:T(8,128)(2,1)S(1)} all-to-all(bf16[32,16,128]{2,1,0:T(8,128)(2,1)S(1)} %bitcast.19), channel_id=1, replica_groups=mesh['yh'=2,'x'=4,'core'=2,'z'=8,'yl'=2] {'x','z'}, dimensions={0} | all-to-all | bytes 262144 | tf_op jit(solution)/shard_map/all_to_all | solution.py:390
  62.2 0.4 shard_map.135
  62.5 8.0 %all_to_all.22.tails_ref = bf16[8,32,128]{2,1,0:T(8,128)(2,1)S(1)} all-to-all(bf16[8,32,128]{2,1,0:T(8,128)(2,1)S(1)} %shard_map.135), channel_id=1, replica_groups=mesh['yh'=2,'x'=4,'core'=2,'z'=8,'yl'=2] {'yh','core','yl'}, dimensions={0} | all-to-all | bytes 131072 | tf_op jit(solution)/shard_map/all_to_all | solution.py:393
  70.5 0.7 shard_map.136
  71.2 4.4 %all-to-all-start.3 = ((bf16[32,24,128]{2,1,0:T(8,128)(2,1)}), bf16[32,24,128]{2,1,0:T(8,128)(2,1)S(1)}, u32[]{:S(2)}, u32[]{:S(2)}) async-start(bf16[32,24,128]{2,1,0:T(8,128)(2,1)} %get-tuple-element.62), calls=%async_computation.3 | async-start | bytes 393216 | tf_op jit(solution)/shard_map/all_to_all | solution.py:396
  75.6 2.7 %shard_map.134 = (bf16[256,4096]{1,0:T(8,128)(2,1)}, f32[1,256]{1,0:T(1,128)}) custom-call(f32[32,256]{1,0:T(8,128)S(1)} %get-tuple-element.54.refs_0_, f32[1,256]{1,0:T(1,128)S(1)} %get-tuple-element.55.refs_1_, f32[1,256]{1,0:T(1,128)S(1)} %get-tuple-element.53.rms_ref.refs_2_, bf16[32,4096]{1,0:T(8,128)(2,1)S(1)} %get-tuple-element.56.refs_3_, ...), custom_call_target="tpu_custom_call" | custom-call | tf_op jit(solution)/shard_map/pallas_call | solution.py:343
  78.3 0.9 %shard_map.137 = f32[64,256]{1,0:T(8,128)} custom-call(f32[8,128]{1,0:T(8,128)S(1)} %get-tuple-element.61.z_ref, f32[16,128]{1,0:T(8,128)S(1)} %bitcast.16), custom_call_target="tpu_custom_call" | custom-call | tf_op jit(solution)/shard_map/pallas_call | solution.py:46
  79.3 7.6 %all-to-all-done.3.all_ref = bf16[32,24,128]{2,1,0:T(8,128)(2,1)S(1)} async-done(((bf16[32,24,128]{2,1,0:T(8,128)(2,1)}), bf16[32,24,128]{2,1,0:T(8,128)(2,1)S(1)}, u32[]{:S(2)}, u32[]{:S(2)}) %all-to-all-start.3) | async-done | bytes 196640 | tf_op jit(solution)/shard_map/all_to_all | solution.py:396
  86.9 0.7 shard_map.138
  (2 shorter events, 0.0 us)
Async XLA Ops:
  0.6 9.3 %collective-permute-start = (bf16[64,256]{1,0:T(8,128)(2,1)}, bf16[64,256]{1,0:T(8,128)(2,1)S(1)}, u32[]{:S(2)}, u32[]{:S(2)}) collective-permute-start(bf16[64,256]{1,0:T(8,128)(2,1)} %param.10), channel_id=1, source_target_pairs={{1,0},{0,128},{128,129},{129,1},{3,2},{2,130},{130,131},{131,3},{5... | collective-permute-start | bytes 98312 | tf_op jit(solution)/shard_map/ppermute | solution.py:371
  3.9 6.1 %collective-permute-start.1 = (bf16[64,256]{1,0:T(8,128)(2,1)}, bf16[64,256]{1,0:T(8,128)(2,1)S(1)}, u32[]{:S(2)}, u32[]{:S(2)}) collective-permute-start(bf16[64,256]{1,0:T(8,128)(2,1)} %param.10), channel_id=1, source_target_pairs={{0,0},{1,128},{128,1},{129,129},{2,2},{3,130},{130,3},{131,131},{4... | collective-permute-start | bytes 98312 | tf_op jit(solution)/shard_map/ppermute | solution.py:34
  5.3 28.9 %copy-start = (bf16[256,2048]{1,0:T(8,128)(2,1)S(1)}, bf16[256,2048]{1,0:T(8,128)(2,1)}, u32[]{:S(2)}) copy-start(bf16[256,2048]{1,0:T(8,128)(2,1)} %q_ref.1) | copy-start | bytes 3145732
  5.3 28.9 %copy-start.1 = (bf16[256,256]{1,0:T(8,128)(2,1)S(1)}, bf16[256,256]{1,0:T(8,128)(2,1)}, u32[]{:S(2)}) copy-start(bf16[256,256]{1,0:T(8,128)(2,1)} %k_ref.1) | copy-start | bytes 393220
  5.3 4.7 %collective-permute-start.2 = (f32[16,128]{1,0:T(8,128)}, f32[16,128]{1,0:T(8,128)S(1)}, u32[]{:S(2)}, u32[]{:S(2)}) collective-permute-start(f32[16,128]{1,0:T(8,128)} %bitcast.14), channel_id=1, source_target_pairs={{0,1},{1,0},{2,3},{3,2},{4,5},{5,4},{6,7},{7,6},{8,9},{9,8},{10,11... | collective-permute-start | bytes 24584 | tf_op jit(solution)/shard_map/ppermute | solution.py:30
  7.2 0.7 copy-start.2
  7.9 2.1 %copy-start.3 = (f32[2048]{0:T(1024)S(1)}, f32[2048]{0:T(1024)}, u32[]{:S(2)}) copy-start(f32[2048]{0:T(1024)} %param.13) | copy-start | bytes 24580
  31.1 1.3 %collective-permute-start.3 = (bf16[512,128]{1,0:T(8,128)(2,1)S(1)}, bf16[512,128]{1,0:T(8,128)(2,1)S(1)}, u32[]{:S(2)}, u32[]{:S(2)}) collective-permute-start(bf16[512,128]{1,0:T(8,128)(2,1)S(1)} %bitcast.10), channel_id=1, source_target_pairs={{0,16},{16,0},{1,17},{17,1},{2,18},{18,2},{3,19},{19,3},{4,20},{20... | collective-permute-start | bytes 393224 | tf_op jit(solution)/shard_map/ppermute | solution.py:30
  33.2 3.9 %collective-permute-start.4 = (f32[24,256]{1,0:T(8,128)S(1)}, f32[24,256]{1,0:T(8,128)S(1)}, u32[]{:S(2)}, u32[]{:S(2)}) collective-permute-start(f32[24,256]{1,0:T(8,128)S(1)} %get-tuple-element.46), channel_id=1, source_target_pairs={{0,1},{1,0},{2,3},{3,2},{4,5},{5,4},{6,7},{7,6},{8,9},{9,8},{10,11... | collective-permute-start | bytes 73736 | tf_op jit(solution)/shard_map/ppermute | solution.py:30
  34.2 7.0 %copy-start.4 = (f32[256]{0:T(256)S(1)}, f32[256]{0:T(256)}, u32[]{:S(2)}) copy-start(f32[256]{0:T(256)} %param.14) | copy-start | bytes 3076
  34.3 7.0 %copy-start.5 = (s32[256]{0:T(256)S(1)}, s32[256]{0:T(256)}, u32[]{:S(2)}) copy-start(s32[256]{0:T(256)} %param.15) | copy-start | bytes 3076
  37.6 3.7 %collective-permute-start.5 = (f32[1,256]{1,0:T(1,128)S(1)}, f32[1,256]{1,0:T(1,128)S(1)}, u32[]{:S(2)}, u32[]{:S(2)}) collective-permute-start(f32[1,256]{1,0:T(1,128)S(1)} %get-tuple-element.48.own_ref), channel_id=1, source_target_pairs={{0,1},{1,0},{2,3},{3,2},{4,5},{5,4},{6,7},{7,6},{8,9},{9,8},{10,11... | collective-permute-start | bytes 3080 | tf_op jit(solution)/shard_map/ppermute | solution.py:30
  42.1 3.8 %collective-permute-start.6 = (f32[24,256]{1,0:T(8,128)S(1)}, f32[24,256]{1,0:T(8,128)S(1)}, u32[]{:S(2)}, u32[]{:S(2)}) collective-permute-start(f32[24,256]{1,0:T(8,128)S(1)} %get-tuple-element.52.own_ref), channel_id=1, source_target_pairs={{0,1},{1,0},{2,3},{3,2},{4,5},{5,4},{6,7},{7,6},{8,9},{9,8},{10,11... | collective-permute-start | bytes 73736 | tf_op jit(solution)/shard_map/ppermute | solution.py:30
  46.5 1.4 %collective-permute-start.7 = (bf16[512,128]{1,0:T(8,128)(2,1)S(1)}, bf16[512,128]{1,0:T(8,128)(2,1)S(1)}, u32[]{:S(2)}, u32[]{:S(2)}) collective-permute-start(bf16[512,128]{1,0:T(8,128)(2,1)S(1)} %get-tuple-element.58), channel_id=1, source_target_pairs={{0,16},{16,0},{1,17},{17,1},{2,18},{18,2},{3,19},{19,3},{4,20},{20... | collective-permute-start | bytes 393224 | tf_op jit(solution)/shard_map/ppermute | solution.py:30
  71.2 15.6 %all-to-all-start.3 = ((bf16[32,24,128]{2,1,0:T(8,128)(2,1)}), bf16[32,24,128]{2,1,0:T(8,128)(2,1)S(1)}, u32[]{:S(2)}, u32[]{:S(2)}) async-start(bf16[32,24,128]{2,1,0:T(8,128)(2,1)} %get-tuple-element.62), calls=%async_computation.3 | async-start | bytes 393216 | tf_op jit(solution)/shard_map/all_to_all | solution.py:396

commit v7 on v6

--- a/solution.py
+++ b/solution.py
@@ -65,20 +65,25 @@
     return lax.broadcasted_iota(jnp.int32, (rows, 128), 1) < 64
 
 
-def read_kernel(ring_ref, swap_ref, r_ref, other_r_ref, v_ref, w_both_ref):
+def rows_on(r, w):
+    parts = [
+        exact_dot(r[g * GROUP : (g + 1) * GROUP], w[g * ROWS : (g + 1) * ROWS].astype(F32), ((1,), (1,)))
+        for g in range(2)
+    ]
+    return jnp.concatenate(parts, axis=1)
+
+
+def choose_kernel(ring_ref, swap_ref, r_ref, w_both_ref, v_ref):
     straight = lax.axis_index("yh") == lax.axis_index("yl")
     ring, pair = ring_ref[...], swap_ref[...]
-    own = jnp.where(straight, pair, ring)
-    other = jnp.where(straight, ring, pair)
-    parts = []
-    for i, (w, r) in enumerate(((own, r_ref), (other, other_r_ref))):
-        halves = []
+    for i, w in enumerate((jnp.where(straight, pair, ring), jnp.where(straight, ring, pair))):
         for g in range(2):
-            wg = w[:, g * HD : (g + 1) * HD]
-            w_both_ref[(2 * i + g) * ROWS : (2 * i + g + 1) * ROWS] = wg
-            halves.append(exact_dot(r[g * GROUP : (g + 1) * GROUP], wg.astype(F32), ((1,), (1,))))
-        parts.append(jnp.concatenate(halves, axis=1))
-    v = jnp.concatenate(parts, axis=0).astype(BF16)
+            w_both_ref[(2 * i + g) * ROWS : (2 * i + g + 1) * ROWS] = w[:, g * HD : (g + 1) * HD]
+    v_ref[...] = rows_on(r_ref, w_both_ref[: 2 * ROWS])
+
+
+def read_kernel(w_both_ref, own_ref, r_ref, v_ref):
+    v = jnp.concatenate([own_ref[...], rows_on(r_ref, w_both_ref[2 * ROWS :])], axis=0).astype(BF16)
     for i in range(32):
         v_ref[i * 16 : (i + 1) * 16] = v
 
@@ -132,28 +137,42 @@
     return whole(attention_kernel, shape(HALF, length, length, dtype=BF16), queries, keys, after)
 
 
-def project_kernel(
-    own_ref, got_ref, gain_ref, x_ref, ss_ref, gvt_ref, u_ref, send_ref
-):
-    core = lax.axis_index("core")
+def project_half(v_ref, gain_ref, x_ref, gvt_ref, core):
     low = left_lanes(8)
-    for b in range(BLOCKS // 2):
-        xi, c, zp = b // 8, b // 4 % 2, b % 4
-        at = slice(b * 128, (b + 1) * 128)
-        row = (xi * 8 + 2 * zp) * 16
-        quad = jnp.where(
-            core == c, own_ref[row : row + 32].astype(F32), got_ref[row : row + 32].astype(F32)
+    total = jnp.zeros((32, x_ref.shape[0]), F32)
+    for xi in range(4):
+        for zp in range(4):
+            row = (xi * 8 + 2 * zp) * 16
+            quad = v_ref[row : row + 32].astype(F32)
+            halves = []
+            for h in range(2):
+                one, two = quad[h * 8 : h * 8 + 8], quad[h * 8 + 16 : h * 8 + 24]
+                halves.append(jnp.where(low, one, pltpu.roll(two, 64, 1)))
+                halves.append(jnp.where(low, pltpu.roll(one, 64, 1), two))
+            zero = (xi * 8 + zp) * 128
+            gain = jnp.where(
+                core == 0,
+                gain_ref[:, zero : zero + 128].astype(F32),
+                gain_ref[:, zero + 512 : zero + 640].astype(F32),
+            )
+            at = (xi * 4 + zp) * 128
+            gvt_ref[:, at : at + 128] = (jnp.concatenate(halves, axis=0) * gain).astype(BF16)
+        spot = pl.ds(pl.multiple_of(xi * 1024 + core * 512, 512), 512)
+        total += lax.dot_general(
+            gvt_ref[:, xi * 512 : (xi + 1) * 512],
+            x_ref[:, spot],
+            (((1,), (1,)), ((), ())),
+            preferred_element_type=F32,
         )
-        halves = []
-        for h in range(2):
-            one, two = quad[h * 8 : h * 8 + 8], quad[h * 8 + 16 : h * 8 + 24]
-            halves.append(jnp.where(low, one, pltpu.roll(two, 64, 1)))
-            halves.append(jnp.where(low, pltpu.roll(one, 64, 1), two))
-        vt = jnp.concatenate(halves, axis=0)
-        gvt_ref[:, at] = (vt * gain_ref[:, at].astype(F32)).astype(BF16)
-    u = lax.dot_general(
-        gvt_ref[...], x_ref[...], (((1,), (1,)), ((), ())), preferred_element_type=F32
-    )
+    return total
+
+
+def project_own_kernel(v_ref, gain_ref, x_ref, gvt_ref, u_ref):
+    u_ref[...] = project_half(v_ref, gain_ref, x_ref, gvt_ref, lax.axis_index("core"))
+
+
+def project_got_kernel(v_ref, gain_ref, x_ref, part_ref, ss_ref, gvt_ref, u_ref, send_ref):
+    u = part_ref[...] + project_half(v_ref, gain_ref, x_ref, gvt_ref, 1 - lax.axis_index("core"))
     u_ref[...] = u[:HALF]
     send_ref[:HALF] = u[HALF:]
     send_ref[HALF:] = jnp.broadcast_to(ss_ref[...], (8, u.shape[1]))
@@ -161,11 +180,14 @@
 
 def project(own, got, gain, x, ss):
     length, wide = x.shape
-    return whole(
-        project_kernel,
-        [shape(32, wide, dtype=BF16), shape(HALF, length), shape(HALF + 8, length)],
-        own, got, gain, x, ss,
-    )
+    half = shape(32, wide // 2, dtype=BF16)
+    mine, part = whole(project_own_kernel, [half, shape(32, length)], own, gain, x)
+    other, u, send = whole(
+        project_got_kernel,
+        [half, shape(HALF, length), shape(HALF + 8, length)],
+        got, gain, x, part, ss,
+    )
+    return (mine, other), u, send
 
 
 def values_kernel(width, p_ref, own_ref, got_ref, ss_ref, v_ref, u_ref, rms_ref):
@@ -316,7 +338,7 @@
             gain_ref[row + 4 : row + 5] = jnp.where(left, pltpu.roll(one, 64, 1), two)
 
 
-def input_kernel(width, c_ref, dot_ref, rms_ref, gvt_ref, x_ref, after_ref, out_ref, log_ref):
+def input_kernel(width, c_ref, dot_ref, rms_ref, mine_ref, other_ref, x_ref, after_ref, out_ref, log_ref):
     rms = rms_ref[...]
     length = rms.shape[1]
     c = c_ref[...]
@@ -325,7 +347,9 @@
     log_scale = rms * dot_ref[...]
     log_ref[...] = log_scale
     back = jnp.broadcast_to(rms * rms * log_scale / width, (128, length)).T
-    gvt = gvt_ref[...]
+    first = lax.axis_index("core") == 0
+    mine, other = mine_ref[...], other_ref[...]
+    gvt = jnp.concatenate([jnp.where(first, mine, other), jnp.where(first, other, mine)], axis=1)
     grad = lax.dot_general(
         jnp.concatenate([high, low], axis=0),
         jnp.concatenate([gvt, gvt], axis=0),
@@ -347,7 +371,8 @@
             pl.BlockSpec((32, length), lambda i: (0, 0)),
             pl.BlockSpec((1, length), lambda i: (0, 0)),
             pl.BlockSpec((1, length), lambda i: (0, 0)),
-            pl.BlockSpec((32, wide // steps), lambda i: (0, i)),
+            pl.BlockSpec((32, wide // steps // 2), lambda i: (0, i)),
+            pl.BlockSpec((32, wide // steps // 2), lambda i: (0, i)),
             pl.BlockSpec((length, wide // steps), lambda i: (0, i)),
             ANY,
         ],
@@ -357,7 +382,7 @@
         ],
         out_shape=[shape(length, wide, dtype=BF16), shape(1, length)],
         compiler_params=PARAMS,
-    )(c, dot, rms, gvt, x, after)
+    )(c, dot, rms, *gvt, x, after)
 
 
 def together(*values):
@@ -371,12 +396,12 @@
     ring = lax.ppermute(value_weight, ("yh", "yl"), [(1, 0), (0, 2), (2, 3), (3, 1)])
     pair = cross(value_weight)
     x, ss = load(hidden_states, norm_gain)
-    ring, pair, other_read, ss = together(ring, pair, other_read, ss)
-    v, weight = whole(
-        read_kernel,
-        [shape(512, 128, dtype=BF16), shape(256, 128, dtype=BF16)],
-        ring, pair, read, other_read,
-    )
+    ring, pair, ss = together(ring, pair, ss)
+    weight, v = whole(
+        choose_kernel, [shape(256, 128, dtype=BF16), shape(8, 128)], ring, pair, read
+    )
+    v, other_read = together(v, other_read)
+    v = whole(read_kernel, shape(512, 128, dtype=BF16), weight, v, other_read)
     v = lax.all_to_all(v.reshape(32, HALF, 128), PLANE, 0, 0).reshape(512, 128)
     v, norm_gain, targets, scored = together(v, norm_gain, targets, scored)
     gain = norm_gain[None]

time: 88 us -> 87.9 us (level)
  starting transfers between devices: 14.1 us -> 13.2 us
    ppermute x6, starting transfers between devices: 5.12 us -> 4.22 us  [swap(): return lax.ppermute(v, axis, [(0, 1), (1, 0)])]
    pallas_call x10 -> x12, Pallas kernels: 7.7 us -> 7.97 us  [whole(): pl.pallas_call(body, in_specs=[VMEM] * len(args), out_specs=[VMEM] * len(...]
  transfers between devices with their start and end apart: 9 -> 9, of which waited for: 6 -> 6; matrix products, arithmetic and copies ran while one was open for 0% -> 0% of each run, Pallas kernels for 9% -> 10%
where the time goes in v7:
time: 87.9 us; the launch traced here: 87.5 us
  blocking collectives  42.9 us (49%)
  waiting for transfers between devices  17 us (19%)
  starting transfers between devices  13.2 us (15%)
  Pallas kernels  12.8 us (15%)
    all_to_all x1, blocking collectives, shards(): v = lax.all_to_all(v.reshape(32, HALF, 128), PLANE, 0, 0).reshape(512, 128)  20.7 us
    all_to_all x1, blocking collectives, shards(): z = lax.all_to_all(z, PLANE, 0, 0)  14.2 us
    ppermute x6, waiting for transfers between devices, swap(): return lax.ppermute(v, axis, [(0, 1), (1, 0)])  9.4 us
    all_to_all x1, blocking collectives, shards(): tails = lax.all_to_all(tails, NEAR, 0, 0)  8.01 us
    pallas_call x12, Pallas kernels, whole(): pl.pallas_call(body, in_specs=[VMEM] * len(args), out_specs=[VMEM] * len(...  7.97 us
    all_to_all x1, waiting for transfers between devices, shards(): tails = lax.all_to_all(tails, PLANE, 0, 0)  7.6 us
    all_to_all x1, starting transfers between devices, shards(): tails = lax.all_to_all(tails, PLANE, 0, 0)  4.35 us
    ppermute x6, starting transfers between devices, swap(): return lax.ppermute(v, axis, [(0, 1), (1, 0)])  4.22 us
  transfers between devices with their start and end apart: 9, of which 6 were waited for; matrix products, arithmetic and copies ran while one was open for 0% of the time, Pallas kernels for 10%

profile of v7, /device:TPU:32, one launch (start us, length us, event | category | flops | bytes accessed | tf_op | source)
XLA Modules:
  0.0 87.5 jit_solution(3142028119924186011)
XLA Ops:
  0.6 3.3 %collective-permute-start = (bf16[64,256]{1,0:T(8,128)(2,1)}, bf16[64,256]{1,0:T(8,128)(2,1)S(1)}, u32[]{:S(2)}, u32[]{:S(2)}) collective-permute-start(bf16[64,256]{1,0:T(8,128)(2,1)} %param.10), channel_id=1, source_target_pairs={{1,0},{0,128},{128,129},{129,1},{3,2},{2,130},{130,131},{131,3},{5... | collective-permute-start | bytes 98312 | tf_op jit(solution)/shard_map/ppermute | solution.py:396
  3.9 1.4 %collective-permute-start.1 = (bf16[64,256]{1,0:T(8,128)(2,1)}, bf16[64,256]{1,0:T(8,128)(2,1)S(1)}, u32[]{:S(2)}, u32[]{:S(2)}) collective-permute-start(bf16[64,256]{1,0:T(8,128)(2,1)} %param.10), channel_id=1, source_target_pairs={{0,0},{1,128},{128,1},{129,129},{2,2},{3,130},{130,3},{131,131},{4... | collective-permute-start | bytes 98312 | tf_op jit(solution)/shard_map/ppermute | solution.py:34
  5.3 1.8 %collective-permute-start.2 = (f32[16,128]{1,0:T(8,128)}, f32[16,128]{1,0:T(8,128)S(1)}, u32[]{:S(2)}, u32[]{:S(2)}) collective-permute-start(f32[16,128]{1,0:T(8,128)} %bitcast.14), channel_id=1, source_target_pairs={{0,1},{1,0},{2,3},{3,2},{4,5},{5,4},{6,7},{7,6},{8,9},{9,8},{10,11... | collective-permute-start | bytes 24584 | tf_op jit(solution)/shard_map/ppermute | solution.py:30
  7.1 0.0 copy-start.2
  7.1 0.7 copy-done.2
  7.8 0.0 copy-start.3
  7.8 2.1 %shard_map.127 = (bf16[256,4096]{1,0:T(8,128)(2,1)S(1)}, f32[1,256]{1,0:T(1,128)S(1)}) custom-call(bf16[256,4096]{1,0:T(8,128)(2,1)} %x_ref.1, bf16[4096]{0:T(1024)(128)(2,1)S(1)} %copy-done.2), custom_call_target="tpu_custom_call" | custom-call | tf_op jit(solution)/shard_map/pallas_call | solution.py:107
  9.9 0.0 collective-permute-done.ring_ref
  10.0 0.0 collective-permute-done.1.swap_ref
  10.0 0.0 copy-done.3
  10.0 0.2 shard_map.128
  10.2 0.0 collective-permute-done.2.r_ref
  10.2 0.4 shard_map.129
  10.6 20.7 %all_to_all.20 = bf16[32,16,128]{2,1,0:T(8,128)(2,1)S(1)} all-to-all(bf16[32,16,128]{2,1,0:T(8,128)(2,1)S(1)} %bitcast.13), channel_id=1, replica_groups=mesh['yh'=2,'x'=4,'core'=2,'z'=8,'yl'=2] {'x','z'}, dimensions={0} | all-to-all | bytes 262144 | tf_op jit(solution)/shard_map/all_to_all | solution.py:405
  31.2 0.0 collective-permute-start.3
  31.3 0.0 copy-start
  31.3 0.0 copy-start.1
  31.3 0.4 shard_map.130
  31.7 0.9 %collective-permute-done.3.v_ref = bf16[512,128]{1,0:T(8,128)(2,1)S(1)} collective-permute-done((bf16[512,128]{1,0:T(8,128)(2,1)S(1)}, bf16[512,128]{1,0:T(8,128)(2,1)S(1)}, u32[]{:S(2)}, u32[]{:S(2)}) %collective-permute-start.3) | collective-permute-done | bytes 131104 | tf_op jit(solution)/shard_map/ppermute | solution.py:30
  32.6 0.4 shard_map.131
  33.0 0.8 collective-permute-start.4
  33.8 0.0 copy-done
  33.8 0.0 copy-done.1
  33.8 0.0 copy-start.4
  33.8 0.0 copy-start.5
  33.9 1.9 %shard_map.132.refs_0_.p_ref = bf16[16,256,256]{2,1,0:T(8,128)(2,1)S(1)} custom-call(bf16[256,2048]{1,0:T(8,128)(2,1)S(1)} %copy-done, bf16[256,256]{1,0:T(8,128)(2,1)S(1)} %copy-done.1, f32[16,256]{1,0:T(8,128)S(1)} %get-tuple-element.51.after_ref.refs_1_), custom_call_target="tpu_custom_call" | custom-call | tf_op jit(solution)/shard_map/pallas_call | solution.py:46
  35.8 1.2 %collective-permute-done.4.refs_2_ = f32[24,256]{1,0:T(8,128)S(1)} collective-permute-done((f32[24,256]{1,0:T(8,128)S(1)}, f32[24,256]{1,0:T(8,128)S(1)}, u32[]{:S(2)}, u32[]{:S(2)}) %collective-permute-start.4) | collective-permute-done | bytes 24608 | tf_op jit(solution)/shard_map/ppermute | solution.py:30
  37.0 0.6 shard_map.133
  37.5 0.8 collective-permute-start.5
  38.3 2.9 %collective-permute-done.5.got_ref = f32[1,256]{1,0:T(1,128)S(1)} collective-permute-done((f32[1,256]{1,0:T(1,128)S(1)}, f32[1,256]{1,0:T(1,128)S(1)}, u32[]{:S(2)}, u32[]{:S(2)}) %collective-permute-start.5) | collective-permute-done | bytes 1056 | tf_op jit(solution)/shard_map/ppermute | solution.py:30
  41.2 0.0 copy-done.4
  41.2 0.0 copy-done.5
  41.2 0.8 shard_map.134
  42.0 0.7 collective-permute-start.6
  42.7 3.1 %collective-permute-done.6.got_ref = f32[24,256]{1,0:T(8,128)S(1)} collective-permute-done((f32[24,256]{1,0:T(8,128)S(1)}, f32[24,256]{1,0:T(8,128)S(1)}, u32[]{:S(2)}, u32[]{:S(2)}) %collective-permute-start.6) | collective-permute-done | bytes 24608 | tf_op jit(solution)/shard_map/ppermute | solution.py:30
  45.8 0.6 shard_map.135
  46.4 0.1 collective-permute-start.7
  46.5 1.3 %collective-permute-done.7 = bf16[512,128]{1,0:T(8,128)(2,1)S(1)} collective-permute-done((bf16[512,128]{1,0:T(8,128)(2,1)S(1)}, bf16[512,128]{1,0:T(8,128)(2,1)S(1)}, u32[]{:S(2)}, u32[]{:S(2)}) %collective-permute-start.7) | collective-permute-done | bytes 131104 | tf_op jit(solution)/shard_map/ppermute | solution.py:30
  47.9 14.2 %all_to_all.21.refs_6_.parts_ref = bf16[32,16,128]{2,1,0:T(8,128)(2,1)S(1)} all-to-all(bf16[32,16,128]{2,1,0:T(8,128)(2,1)S(1)} %bitcast.19), channel_id=1, replica_groups=mesh['yh'=2,'x'=4,'core'=2,'z'=8,'yl'=2] {'x','z'}, dimensions={0} | all-to-all | bytes 262144 | tf_op jit(solution)/shard_map/all_to_all | solution.py:415
  62.1 0.4 shard_map.137
  62.4 8.0 %all_to_all.22.tails_ref = bf16[8,32,128]{2,1,0:T(8,128)(2,1)S(1)} all-to-all(bf16[8,32,128]{2,1,0:T(8,128)(2,1)S(1)} %shard_map.137), channel_id=1, replica_groups=mesh['yh'=2,'x'=4,'core'=2,'z'=8,'yl'=2] {'yh','core','yl'}, dimensions={0} | all-to-all | bytes 131072 | tf_op jit(solution)/shard_map/all_to_all | solution.py:418
  70.4 0.7 shard_map.138
  71.1 4.4 %all-to-all-start.3 = ((bf16[32,24,128]{2,1,0:T(8,128)(2,1)}), bf16[32,24,128]{2,1,0:T(8,128)(2,1)S(1)}, u32[]{:S(2)}, u32[]{:S(2)}) async-start(bf16[32,24,128]{2,1,0:T(8,128)(2,1)} %get-tuple-element.68), calls=%async_computation.3 | async-start | bytes 393216 | tf_op jit(solution)/shard_map/all_to_all | solution.py:421
  75.5 2.7 %shard_map.136 = (bf16[256,4096]{1,0:T(8,128)(2,1)}, f32[1,256]{1,0:T(1,128)}) custom-call(f32[32,256]{1,0:T(8,128)S(1)} %get-tuple-element.60.refs_0_, f32[1,256]{1,0:T(1,128)S(1)} %get-tuple-element.61.refs_1_, f32[1,256]{1,0:T(1,128)S(1)} %get-tuple-element.59.rms_ref.refs_2_, bf16[32,2048]{1,0:T(8,128)(2,1)S(1)} %get-tuple-element.62.refs_3_, ...), custom_call_target="tpu_custom_call" | custom-call | tf_op jit(solution)/shard_map/pallas_call | solution.py:367
  78.2 0.9 %shard_map.139 = f32[64,256]{1,0:T(8,128)} custom-call(f32[8,128]{1,0:T(8,128)S(1)} %get-tuple-element.67.z_ref, f32[16,128]{1,0:T(8,128)S(1)} %bitcast.16), custom_call_target="tpu_custom_call" | custom-call | tf_op jit(solution)/shard_map/pallas_call | solution.py:46
  79.2 7.6 %all-to-all-done.3.all_ref = bf16[32,24,128]{2,1,0:T(8,128)(2,1)S(1)} async-done(((bf16[32,24,128]{2,1,0:T(8,128)(2,1)}), bf16[32,24,128]{2,1,0:T(8,128)(2,1)S(1)}, u32[]{:S(2)}, u32[]{:S(2)}) %all-to-all-start.3) | async-done | bytes 196640 | tf_op jit(solution)/shard_map/all_to_all | solution.py:421
  86.8 0.7 shard_map.140
  (2 shorter events, 0.0 us)
Async XLA Ops:
  0.6 9.3 %collective-permute-start = (bf16[64,256]{1,0:T(8,128)(2,1)}, bf16[64,256]{1,0:T(8,128)(2,1)S(1)}, u32[]{:S(2)}, u32[]{:S(2)}) collective-permute-start(bf16[64,256]{1,0:T(8,128)(2,1)} %param.10), channel_id=1, source_target_pairs={{1,0},{0,128},{128,129},{129,1},{3,2},{2,130},{130,131},{131,3},{5... | collective-permute-start | bytes 98312 | tf_op jit(solution)/shard_map/ppermute | solution.py:396
  3.9 6.1 %collective-permute-start.1 = (bf16[64,256]{1,0:T(8,128)(2,1)}, bf16[64,256]{1,0:T(8,128)(2,1)S(1)}, u32[]{:S(2)}, u32[]{:S(2)}) collective-permute-start(bf16[64,256]{1,0:T(8,128)(2,1)} %param.10), channel_id=1, source_target_pairs={{0,0},{1,128},{128,1},{129,129},{2,2},{3,130},{130,3},{131,131},{4... | collective-permute-start | bytes 98312 | tf_op jit(solution)/shard_map/ppermute | solution.py:34
  5.3 4.9 %collective-permute-start.2 = (f32[16,128]{1,0:T(8,128)}, f32[16,128]{1,0:T(8,128)S(1)}, u32[]{:S(2)}, u32[]{:S(2)}) collective-permute-start(f32[16,128]{1,0:T(8,128)} %bitcast.14), channel_id=1, source_target_pairs={{0,1},{1,0},{2,3},{3,2},{4,5},{5,4},{6,7},{7,6},{8,9},{9,8},{10,11... | collective-permute-start | bytes 24584 | tf_op jit(solution)/shard_map/ppermute | solution.py:30
  7.1 0.7 copy-start.2
  7.8 2.1 %copy-start.3 = (f32[2048]{0:T(1024)S(1)}, f32[2048]{0:T(1024)}, u32[]{:S(2)}) copy-start(f32[2048]{0:T(1024)} %param.13) | copy-start | bytes 24580
  31.2 1.3 %collective-permute-start.3 = (bf16[512,128]{1,0:T(8,128)(2,1)S(1)}, bf16[512,128]{1,0:T(8,128)(2,1)S(1)}, u32[]{:S(2)}, u32[]{:S(2)}) collective-permute-start(bf16[512,128]{1,0:T(8,128)(2,1)S(1)} %bitcast.10), channel_id=1, source_target_pairs={{0,16},{16,0},{1,17},{17,1},{2,18},{18,2},{3,19},{19,3},{4,20},{20... | collective-permute-start | bytes 393224 | tf_op jit(solution)/shard_map/ppermute | solution.py:30
  31.3 2.6 %copy-start = (bf16[256,2048]{1,0:T(8,128)(2,1)S(1)}, bf16[256,2048]{1,0:T(8,128)(2,1)}, u32[]{:S(2)}) copy-start(bf16[256,2048]{1,0:T(8,128)(2,1)} %q_ref.1) | copy-start | bytes 3145732
  31.3 2.6 %copy-start.1 = (bf16[256,256]{1,0:T(8,128)(2,1)S(1)}, bf16[256,256]{1,0:T(8,128)(2,1)}, u32[]{:S(2)}) copy-start(bf16[256,256]{1,0:T(8,128)(2,1)} %k_ref.1) | copy-start | bytes 393220
  33.0 3.9 %collective-permute-start.4 = (f32[24,256]{1,0:T(8,128)S(1)}, f32[24,256]{1,0:T(8,128)S(1)}, u32[]{:S(2)}, u32[]{:S(2)}) collective-permute-start(f32[24,256]{1,0:T(8,128)S(1)} %get-tuple-element.52), channel_id=1, source_target_pairs={{0,1},{1,0},{2,3},{3,2},{4,5},{5,4},{6,7},{7,6},{8,9},{9,8},{10,11... | collective-permute-start | bytes 73736 | tf_op jit(solution)/shard_map/ppermute | solution.py:30
  33.8 7.3 %copy-start.4 = (f32[256]{0:T(256)S(1)}, f32[256]{0:T(256)}, u32[]{:S(2)}) copy-start(f32[256]{0:T(256)} %param.14) | copy-start | bytes 3076
  33.8 7.3 %copy-start.5 = (s32[256]{0:T(256)S(1)}, s32[256]{0:T(256)}, u32[]{:S(2)}) copy-start(s32[256]{0:T(256)} %param.15) | copy-start | bytes 3076
  37.5 3.7 %collective-permute-start.5 = (f32[1,256]{1,0:T(1,128)S(1)}, f32[1,256]{1,0:T(1,128)S(1)}, u32[]{:S(2)}, u32[]{:S(2)}) collective-permute-start(f32[1,256]{1,0:T(1,128)S(1)} %get-tuple-element.54.own_ref), channel_id=1, source_target_pairs={{0,1},{1,0},{2,3},{3,2},{4,5},{5,4},{6,7},{7,6},{8,9},{9,8},{10,11... | collective-permute-start | bytes 3080 | tf_op jit(solution)/shard_map/ppermute | solution.py:30
  42.0 3.8 %collective-permute-start.6 = (f32[24,256]{1,0:T(8,128)S(1)}, f32[24,256]{1,0:T(8,128)S(1)}, u32[]{:S(2)}, u32[]{:S(2)}) collective-permute-start(f32[24,256]{1,0:T(8,128)S(1)} %get-tuple-element.58.own_ref), channel_id=1, source_target_pairs={{0,1},{1,0},{2,3},{3,2},{4,5},{5,4},{6,7},{7,6},{8,9},{9,8},{10,11... | collective-permute-start | bytes 73736 | tf_op jit(solution)/shard_map/ppermute | solution.py:30
  46.4 1.4 %collective-permute-start.7 = (bf16[512,128]{1,0:T(8,128)(2,1)S(1)}, bf16[512,128]{1,0:T(8,128)(2,1)S(1)}, u32[]{:S(2)}, u32[]{:S(2)}) collective-permute-start(bf16[512,128]{1,0:T(8,128)(2,1)S(1)} %get-tuple-element.65), channel_id=1, source_target_pairs={{0,16},{16,0},{1,17},{17,1},{2,18},{18,2},{3,19},{19,3},{4,20},{20... | collective-permute-start | bytes 393224 | tf_op jit(solution)/shard_map/ppermute | solution.py:30
  71.1 15.6 %all-to-all-start.3 = ((bf16[32,24,128]{2,1,0:T(8,128)(2,1)}), bf16[32,24,128]{2,1,0:T(8,128)(2,1)S(1)}, u32[]{:S(2)}, u32[]{:S(2)}) async-start(bf16[32,24,128]{2,1,0:T(8,128)(2,1)} %get-tuple-element.68), calls=%async_computation.3 | async-start | bytes 393216 | tf_op jit(solution)/shard_map/all_to_all | solution.py:421

commit v8 on v7

--- a/solution.py
+++ b/solution.py
@@ -61,13 +61,21 @@
     return lax.dot_general(a, b, (dims, ((), ())), precision=HIGHEST, preferred_element_type=F32)
 
 
+def split_dot(a, w, dims):
+    high = a.astype(BF16)
+    low = (a - high.astype(F32)).astype(BF16)
+    both = jnp.concatenate([high.astype(F32), low.astype(F32)], axis=0).astype(BF16)
+    out = lax.dot_general(both, w, (dims, ((), ())), preferred_element_type=F32)
+    return out[: a.shape[0]] + out[a.shape[0] :]
+
+
 def left_lanes(rows):
     return lax.broadcasted_iota(jnp.int32, (rows, 128), 1) < 64
 
 
 def rows_on(r, w):
     parts = [
-        exact_dot(r[g * GROUP : (g + 1) * GROUP], w[g * ROWS : (g + 1) * ROWS].astype(F32), ((1,), (1,)))
+        split_dot(r[g * GROUP : (g + 1) * GROUP], w[g * ROWS : (g + 1) * ROWS], ((1,), (1,)))
         for g in range(2)
     ]
     return jnp.concatenate(parts, axis=1)
@@ -92,14 +100,18 @@
     return jnp.sum(a.T, axis=0, keepdims=True)
 
 
-def load_kernel(x_ref, after_ref, xv_ref, ss_ref, sem):
-    copy = pltpu.make_async_copy(x_ref, xv_ref, sem)
-    copy.start()
-    copy.wait()
+def load_kernel(x_ref, after_ref, xv_ref, ss_ref, sems):
+    wide = xv_ref.shape[1]
+    spots = [slice(i * wide // 4, (i + 1) * wide // 4) for i in range(4)]
+    copies = [pltpu.make_async_copy(x_ref.at[:, s], xv_ref.at[:, s], sems.at[i]) for i, s in enumerate(spots)]
+    for copy in copies:
+        copy.start()
     total = jnp.zeros((xv_ref.shape[0], 128), F32)
-    for b in range(xv_ref.shape[1] // 128):
-        xb = xv_ref[:, b * 128 : (b + 1) * 128].astype(F32)
-        total += xb * xb
+    for copy, spot in zip(copies, spots):
+        copy.wait()
+        for at in range(spot.start, spot.stop, 128):
+            xb = xv_ref[:, at : at + 128].astype(F32)
+            total += xb * xb
     ss_ref[...] = row_sum_of_transpose(total)
 
 
@@ -109,7 +121,7 @@
         in_specs=[HBM, ANY],
         out_specs=[VMEM] * 2,
         out_shape=[shape(*x.shape, dtype=BF16), shape(1, x.shape[0])],
-        scratch_shapes=[pltpu.SemaphoreType.DMA],
+        scratch_shapes=[pltpu.SemaphoreType.DMA((4,))],
         compiler_params=LOADS,
     )(x, after)
 
@@ -288,13 +300,13 @@
     z = total * gain
     part = jnp.sum(total * v, axis=0, keepdims=True)
     part = jnp.broadcast_to(part + pltpu.roll(part, 64, 1), (8, 128))
-    ws = [w_ref[i * ROWS : (i + 1) * ROWS].astype(F32) for i in range(4)]
+    ws = [w_ref[i * ROWS : (i + 1) * ROWS] for i in range(4)]
     tails = []
     for h in range(2):
         rows = z[h * 8 : (h + 1) * 8]
         reads = []
         for g in range(2):
-            reads.append(exact_dot(rows[:, g * ROWS : (g + 1) * ROWS], ws[2 * h + g], ((1,), (0,))))
+            reads.append(split_dot(rows[:, g * ROWS : (g + 1) * ROWS], ws[2 * h + g], ((1,), (0,))))
         tails.append(jnp.concatenate([*reads, part, rows], axis=0))
     for i in range(8):
         tails_ref[i] = jnp.where(side == i % 2, tails[0], tails[1]).astype(BF16)

time: 87.9 us -> 87.5 us (level)
  starting transfers between devices: 13.2 us -> 14.6 us
  waiting for transfers between devices: 17 us -> 15.7 us
    ppermute x6, starting transfers between devices: 4.22 us -> 5.52 us  [swap(): return lax.ppermute(v, axis, [(0, 1), (1, 0)])]
    ppermute x6, waiting for transfers between devices: 9.4 us -> 8.1 us  [swap(): return lax.ppermute(v, axis, [(0, 1), (1, 0)])]
  transfers between devices with their start and end apart: 9 -> 9, of which waited for: 6 -> 6; matrix products, arithmetic and copies ran while one was open for 0% -> 0% of each run, Pallas kernels for 10% -> 9%
where the time goes in v8:
time: 87.5 us; the launch traced here: 87.1 us
  blocking collectives  43.1 us (49%)
  waiting for transfers between devices  15.7 us (18%)
  starting transfers between devices  14.6 us (17%)
  Pallas kernels  12.2 us (14%)
    all_to_all x1, blocking collectives, shards(): v = lax.all_to_all(v.reshape(32, HALF, 128), PLANE, 0, 0).reshape(512, 128)  20.7 us
    all_to_all x1, blocking collectives, shards(): z = lax.all_to_all(z, PLANE, 0, 0)  14.2 us
    all_to_all x1, blocking collectives, shards(): tails = lax.all_to_all(tails, NEAR, 0, 0)  8.26 us
    ppermute x6, waiting for transfers between devices, swap(): return lax.ppermute(v, axis, [(0, 1), (1, 0)])  8.1 us
    pallas_call x12, Pallas kernels, whole(): pl.pallas_call(body, in_specs=[VMEM] * len(args), out_specs=[VMEM] * len(...  7.73 us
    all_to_all x1, waiting for transfers between devices, shards(): tails = lax.all_to_all(tails, PLANE, 0, 0)  7.59 us
    ppermute x6, starting transfers between devices, swap(): return lax.ppermute(v, axis, [(0, 1), (1, 0)])  5.52 us
    all_to_all x1, starting transfers between devices, shards(): tails = lax.all_to_all(tails, PLANE, 0, 0)  4.35 us
  transfers between devices with their start and end apart: 9, of which 6 were waited for; matrix products, arithmetic and copies ran while one was open for 0% of the time, Pallas kernels for 9%

profile of v8, /device:TPU:32, one launch (start us, length us, event | category | flops | bytes accessed | tf_op | source)
XLA Modules:
  0.0 87.1 jit_solution(6268313524879915084)
XLA Ops:
  0.6 3.3 %collective-permute-start = (bf16[64,256]{1,0:T(8,128)(2,1)}, bf16[64,256]{1,0:T(8,128)(2,1)S(1)}, u32[]{:S(2)}, u32[]{:S(2)}) collective-permute-start(bf16[64,256]{1,0:T(8,128)(2,1)} %param.10), channel_id=1, source_target_pairs={{1,0},{0,128},{128,129},{129,1},{3,2},{2,130},{130,131},{131,3},{5... | collective-permute-start | bytes 98312 | tf_op jit(solution)/shard_map/ppermute | solution.py:408
  3.9 1.4 %collective-permute-start.1 = (bf16[64,256]{1,0:T(8,128)(2,1)}, bf16[64,256]{1,0:T(8,128)(2,1)S(1)}, u32[]{:S(2)}, u32[]{:S(2)}) collective-permute-start(bf16[64,256]{1,0:T(8,128)(2,1)} %param.10), channel_id=1, source_target_pairs={{0,0},{1,128},{128,1},{129,129},{2,2},{3,130},{130,3},{131,131},{4... | collective-permute-start | bytes 98312 | tf_op jit(solution)/shard_map/ppermute | solution.py:34
  5.3 1.8 %collective-permute-start.2 = (f32[16,128]{1,0:T(8,128)}, f32[16,128]{1,0:T(8,128)S(1)}, u32[]{:S(2)}, u32[]{:S(2)}) collective-permute-start(f32[16,128]{1,0:T(8,128)} %bitcast.14), channel_id=1, source_target_pairs={{0,1},{1,0},{2,3},{3,2},{4,5},{5,4},{6,7},{7,6},{8,9},{9,8},{10,11... | collective-permute-start | bytes 24584 | tf_op jit(solution)/shard_map/ppermute | solution.py:30
  7.1 0.0 copy-start.2
  7.1 0.7 copy-done.2
  7.8 0.0 copy-start.3
  7.8 1.8 %shard_map.127 = (bf16[256,4096]{1,0:T(8,128)(2,1)S(1)}, f32[1,256]{1,0:T(1,128)S(1)}) custom-call(bf16[256,4096]{1,0:T(8,128)(2,1)} %x_ref.1, bf16[4096]{0:T(1024)(128)(2,1)S(1)} %copy-done.2), custom_call_target="tpu_custom_call" | custom-call | tf_op jit(solution)/shard_map/pallas_call | solution.py:119
  9.6 0.0 collective-permute-done.ring_ref
  9.6 0.0 collective-permute-done.1.swap_ref
  9.6 0.0 copy-done.3
  9.6 0.2 shard_map.128
  9.8 0.0 collective-permute-done.2.r_ref
  9.8 0.2 shard_map.129
  10.1 20.7 %all_to_all.20 = bf16[32,16,128]{2,1,0:T(8,128)(2,1)S(1)} all-to-all(bf16[32,16,128]{2,1,0:T(8,128)(2,1)S(1)} %bitcast.13), channel_id=1, replica_groups=mesh['yh'=2,'x'=4,'core'=2,'z'=8,'yl'=2] {'x','z'}, dimensions={0} | all-to-all | bytes 262144 | tf_op jit(solution)/shard_map/all_to_all | solution.py:417
  30.7 0.0 collective-permute-start.3
  30.7 0.0 copy-start
  30.8 0.0 copy-start.1
  30.8 0.4 shard_map.130
  31.2 0.9 %collective-permute-done.3.v_ref = bf16[512,128]{1,0:T(8,128)(2,1)S(1)} collective-permute-done((bf16[512,128]{1,0:T(8,128)(2,1)S(1)}, bf16[512,128]{1,0:T(8,128)(2,1)S(1)}, u32[]{:S(2)}, u32[]{:S(2)}) %collective-permute-start.3) | collective-permute-done | bytes 131104 | tf_op jit(solution)/shard_map/ppermute | solution.py:30
  32.1 0.4 shard_map.131
  32.5 1.2 %collective-permute-start.4 = (f32[24,256]{1,0:T(8,128)S(1)}, f32[24,256]{1,0:T(8,128)S(1)}, u32[]{:S(2)}, u32[]{:S(2)}) collective-permute-start(f32[24,256]{1,0:T(8,128)S(1)} %get-tuple-element.52), channel_id=1, source_target_pairs={{0,1},{1,0},{2,3},{3,2},{4,5},{5,4},{6,7},{7,6},{8,9},{9,8},{10,11... | collective-permute-start | bytes 73736 | tf_op jit(solution)/shard_map/ppermute | solution.py:30
  33.8 0.0 copy-done
  33.8 0.0 copy-done.1
  33.8 0.0 copy-start.4
  33.8 0.0 copy-start.5
  33.8 1.9 %shard_map.132.refs_0_.p_ref = bf16[16,256,256]{2,1,0:T(8,128)(2,1)S(1)} custom-call(bf16[256,2048]{1,0:T(8,128)(2,1)S(1)} %copy-done, bf16[256,256]{1,0:T(8,128)(2,1)S(1)} %copy-done.1, f32[16,256]{1,0:T(8,128)S(1)} %get-tuple-element.51.after_ref.refs_1_), custom_call_target="tpu_custom_call" | custom-call | tf_op jit(solution)/shard_map/pallas_call | solution.py:46
  35.7 0.8 collective-permute-done.4.refs_2_
  36.4 0.6 shard_map.133
  37.0 1.2 %collective-permute-start.5 = (f32[1,256]{1,0:T(1,128)S(1)}, f32[1,256]{1,0:T(1,128)S(1)}, u32[]{:S(2)}, u32[]{:S(2)}) collective-permute-start(f32[1,256]{1,0:T(1,128)S(1)} %get-tuple-element.54.own_ref), channel_id=1, source_target_pairs={{0,1},{1,0},{2,3},{3,2},{4,5},{5,4},{6,7},{7,6},{8,9},{9,8},{10,11... | collective-permute-start | bytes 3080 | tf_op jit(solution)/shard_map/ppermute | solution.py:30
  38.2 2.4 %collective-permute-done.5.got_ref = f32[1,256]{1,0:T(1,128)S(1)} collective-permute-done((f32[1,256]{1,0:T(1,128)S(1)}, f32[1,256]{1,0:T(1,128)S(1)}, u32[]{:S(2)}, u32[]{:S(2)}) %collective-permute-start.5) | collective-permute-done | bytes 1056 | tf_op jit(solution)/shard_map/ppermute | solution.py:30
  40.7 0.0 copy-done.4
  40.7 0.0 copy-done.5
  40.7 0.8 shard_map.134
  41.5 1.1 %collective-permute-start.6 = (f32[24,256]{1,0:T(8,128)S(1)}, f32[24,256]{1,0:T(8,128)S(1)}, u32[]{:S(2)}, u32[]{:S(2)}) collective-permute-start(f32[24,256]{1,0:T(8,128)S(1)} %get-tuple-element.58.own_ref), channel_id=1, source_target_pairs={{0,1},{1,0},{2,3},{3,2},{4,5},{5,4},{6,7},{7,6},{8,9},{9,8},{10,11... | collective-permute-start | bytes 73736 | tf_op jit(solution)/shard_map/ppermute | solution.py:30
  42.6 2.7 %collective-permute-done.6.got_ref = f32[24,256]{1,0:T(8,128)S(1)} collective-permute-done((f32[24,256]{1,0:T(8,128)S(1)}, f32[24,256]{1,0:T(8,128)S(1)}, u32[]{:S(2)}, u32[]{:S(2)}) %collective-permute-start.6) | collective-permute-done | bytes 24608 | tf_op jit(solution)/shard_map/ppermute | solution.py:30
  45.3 0.6 shard_map.135
  45.9 0.1 collective-permute-start.7
  46.0 1.3 %collective-permute-done.7 = bf16[512,128]{1,0:T(8,128)(2,1)S(1)} collective-permute-done((bf16[512,128]{1,0:T(8,128)(2,1)S(1)}, bf16[512,128]{1,0:T(8,128)(2,1)S(1)}, u32[]{:S(2)}, u32[]{:S(2)}) %collective-permute-start.7) | collective-permute-done | bytes 131104 | tf_op jit(solution)/shard_map/ppermute | solution.py:30
  47.3 14.2 %all_to_all.21.refs_6_.parts_ref = bf16[32,16,128]{2,1,0:T(8,128)(2,1)S(1)} all-to-all(bf16[32,16,128]{2,1,0:T(8,128)(2,1)S(1)} %bitcast.19), channel_id=1, replica_groups=mesh['yh'=2,'x'=4,'core'=2,'z'=8,'yl'=2] {'x','z'}, dimensions={0} | all-to-all | bytes 262144 | tf_op jit(solution)/shard_map/all_to_all | solution.py:427
  61.5 0.3 shard_map.137
  61.8 8.3 %all_to_all.22.tails_ref = bf16[8,32,128]{2,1,0:T(8,128)(2,1)S(1)} all-to-all(bf16[8,32,128]{2,1,0:T(8,128)(2,1)S(1)} %shard_map.137), channel_id=1, replica_groups=mesh['yh'=2,'x'=4,'core'=2,'z'=8,'yl'=2] {'yh','core','yl'}, dimensions={0} | all-to-all | bytes 131072 | tf_op jit(solution)/shard_map/all_to_all | solution.py:430
  70.1 0.7 shard_map.138
  70.8 4.4 %all-to-all-start.3 = ((bf16[32,24,128]{2,1,0:T(8,128)(2,1)}), bf16[32,24,128]{2,1,0:T(8,128)(2,1)S(1)}, u32[]{:S(2)}, u32[]{:S(2)}) async-start(bf16[32,24,128]{2,1,0:T(8,128)(2,1)} %get-tuple-element.68), calls=%async_computation.3 | async-start | bytes 393216 | tf_op jit(solution)/shard_map/all_to_all | solution.py:433
  75.2 2.7 %shard_map.136 = (bf16[256,4096]{1,0:T(8,128)(2,1)}, f32[1,256]{1,0:T(1,128)}) custom-call(f32[32,256]{1,0:T(8,128)S(1)} %get-tuple-element.60.refs_0_, f32[1,256]{1,0:T(1,128)S(1)} %get-tuple-element.61.refs_1_, f32[1,256]{1,0:T(1,128)S(1)} %get-tuple-element.59.rms_ref.refs_2_, bf16[32,2048]{1,0:T(8,128)(2,1)S(1)} %get-tuple-element.62.refs_3_, ...), custom_call_target="tpu_custom_call" | custom-call | tf_op jit(solution)/shard_map/pallas_call | solution.py:379
  77.9 0.9 %shard_map.139 = f32[64,256]{1,0:T(8,128)} custom-call(f32[8,128]{1,0:T(8,128)S(1)} %get-tuple-element.67.z_ref, f32[16,128]{1,0:T(8,128)S(1)} %bitcast.16), custom_call_target="tpu_custom_call" | custom-call | tf_op jit(solution)/shard_map/pallas_call | solution.py:46
  78.8 7.6 %all-to-all-done.3.all_ref = bf16[32,24,128]{2,1,0:T(8,128)(2,1)S(1)} async-done(((bf16[32,24,128]{2,1,0:T(8,128)(2,1)}), bf16[32,24,128]{2,1,0:T(8,128)(2,1)S(1)}, u32[]{:S(2)}, u32[]{:S(2)}) %all-to-all-start.3) | async-done | bytes 196640 | tf_op jit(solution)/shard_map/all_to_all | solution.py:433
  86.4 0.7 shard_map.140
  (2 shorter events, 0.0 us)
Async XLA Ops:
  0.6 9.0 %collective-permute-start = (bf16[64,256]{1,0:T(8,128)(2,1)}, bf16[64,256]{1,0:T(8,128)(2,1)S(1)}, u32[]{:S(2)}, u32[]{:S(2)}) collective-permute-start(bf16[64,256]{1,0:T(8,128)(2,1)} %param.10), channel_id=1, source_target_pairs={{1,0},{0,128},{128,129},{129,1},{3,2},{2,130},{130,131},{131,3},{5... | collective-permute-start | bytes 98312 | tf_op jit(solution)/shard_map/ppermute | solution.py:408
  3.9 5.7 %collective-permute-start.1 = (bf16[64,256]{1,0:T(8,128)(2,1)}, bf16[64,256]{1,0:T(8,128)(2,1)S(1)}, u32[]{:S(2)}, u32[]{:S(2)}) collective-permute-start(bf16[64,256]{1,0:T(8,128)(2,1)} %param.10), channel_id=1, source_target_pairs={{0,0},{1,128},{128,1},{129,129},{2,2},{3,130},{130,3},{131,131},{4... | collective-permute-start | bytes 98312 | tf_op jit(solution)/shard_map/ppermute | solution.py:34
  5.3 4.5 %collective-permute-start.2 = (f32[16,128]{1,0:T(8,128)}, f32[16,128]{1,0:T(8,128)S(1)}, u32[]{:S(2)}, u32[]{:S(2)}) collective-permute-start(f32[16,128]{1,0:T(8,128)} %bitcast.14), channel_id=1, source_target_pairs={{0,1},{1,0},{2,3},{3,2},{4,5},{5,4},{6,7},{7,6},{8,9},{9,8},{10,11... | collective-permute-start | bytes 24584 | tf_op jit(solution)/shard_map/ppermute | solution.py:30
  7.1 0.7 copy-start.2
  7.8 1.8 %copy-start.3 = (f32[2048]{0:T(1024)S(1)}, f32[2048]{0:T(1024)}, u32[]{:S(2)}) copy-start(f32[2048]{0:T(1024)} %param.13) | copy-start | bytes 24580
  30.7 1.3 %collective-permute-start.3 = (bf16[512,128]{1,0:T(8,128)(2,1)S(1)}, bf16[512,128]{1,0:T(8,128)(2,1)S(1)}, u32[]{:S(2)}, u32[]{:S(2)}) collective-permute-start(bf16[512,128]{1,0:T(8,128)(2,1)S(1)} %bitcast.10), channel_id=1, source_target_pairs={{0,16},{16,0},{1,17},{17,1},{2,18},{18,2},{3,19},{19,3},{4,20},{20... | collective-permute-start | bytes 393224 | tf_op jit(solution)/shard_map/ppermute | solution.py:30
  30.7 3.0 %copy-start = (bf16[256,2048]{1,0:T(8,128)(2,1)S(1)}, bf16[256,2048]{1,0:T(8,128)(2,1)}, u32[]{:S(2)}) copy-start(bf16[256,2048]{1,0:T(8,128)(2,1)} %q_ref.1) | copy-start | bytes 3145732
  30.8 3.0 %copy-start.1 = (bf16[256,256]{1,0:T(8,128)(2,1)S(1)}, bf16[256,256]{1,0:T(8,128)(2,1)}, u32[]{:S(2)}) copy-start(bf16[256,256]{1,0:T(8,128)(2,1)} %k_ref.1) | copy-start | bytes 393220
  32.5 3.9 %collective-permute-start.4 = (f32[24,256]{1,0:T(8,128)S(1)}, f32[24,256]{1,0:T(8,128)S(1)}, u32[]{:S(2)}, u32[]{:S(2)}) collective-permute-start(f32[24,256]{1,0:T(8,128)S(1)} %get-tuple-element.52), channel_id=1, source_target_pairs={{0,1},{1,0},{2,3},{3,2},{4,5},{5,4},{6,7},{7,6},{8,9},{9,8},{10,11... | collective-permute-start | bytes 73736 | tf_op jit(solution)/shard_map/ppermute | solution.py:30
  33.8 6.9 %copy-start.4 = (f32[256]{0:T(256)S(1)}, f32[256]{0:T(256)}, u32[]{:S(2)}) copy-start(f32[256]{0:T(256)} %param.14) | copy-start | bytes 3076
  33.8 6.9 %copy-start.5 = (s32[256]{0:T(256)S(1)}, s32[256]{0:T(256)}, u32[]{:S(2)}) copy-start(s32[256]{0:T(256)} %param.15) | copy-start | bytes 3076
  37.0 3.7 %collective-permute-start.5 = (f32[1,256]{1,0:T(1,128)S(1)}, f32[1,256]{1,0:T(1,128)S(1)}, u32[]{:S(2)}, u32[]{:S(2)}) collective-permute-start(f32[1,256]{1,0:T(1,128)S(1)} %get-tuple-element.54.own_ref), channel_id=1, source_target_pairs={{0,1},{1,0},{2,3},{3,2},{4,5},{5,4},{6,7},{7,6},{8,9},{9,8},{10,11... | collective-permute-start | bytes 3080 | tf_op jit(solution)/shard_map/ppermute | solution.py:30
  41.5 3.8 %collective-permute-start.6 = (f32[24,256]{1,0:T(8,128)S(1)}, f32[24,256]{1,0:T(8,128)S(1)}, u32[]{:S(2)}, u32[]{:S(2)}) collective-permute-start(f32[24,256]{1,0:T(8,128)S(1)} %get-tuple-element.58.own_ref), channel_id=1, source_target_pairs={{0,1},{1,0},{2,3},{3,2},{4,5},{5,4},{6,7},{7,6},{8,9},{9,8},{10,11... | collective-permute-start | bytes 73736 | tf_op jit(solution)/shard_map/ppermute | solution.py:30
  45.9 1.4 %collective-permute-start.7 = (bf16[512,128]{1,0:T(8,128)(2,1)S(1)}, bf16[512,128]{1,0:T(8,128)(2,1)S(1)}, u32[]{:S(2)}, u32[]{:S(2)}) collective-permute-start(bf16[512,128]{1,0:T(8,128)(2,1)S(1)} %get-tuple-element.65), channel_id=1, source_target_pairs={{0,16},{16,0},{1,17},{17,1},{2,18},{18,2},{3,19},{19,3},{4,20},{20... | collective-permute-start | bytes 393224 | tf_op jit(solution)/shard_map/ppermute | solution.py:30
  70.8 15.6 %all-to-all-start.3 = ((bf16[32,24,128]{2,1,0:T(8,128)(2,1)}), bf16[32,24,128]{2,1,0:T(8,128)(2,1)S(1)}, u32[]{:S(2)}, u32[]{:S(2)}) async-start(bf16[32,24,128]{2,1,0:T(8,128)(2,1)} %get-tuple-element.68), calls=%async_computation.3 | async-start | bytes 393216 | tf_op jit(solution)/shard_map/all_to_all | solution.py:433

commit v9 on v8

--- a/solution.py
+++ b/solution.py
@@ -209,10 +209,13 @@
     u = own_ref[...] + got[:HALF]
     u_ref[...] = u
     u = u * rms
-    total = jnp.zeros(p_ref.shape[1:], F32)
-    for j in range(HALF):
-        total += p_ref[j].astype(F32) * u[j : j + 1]
-    v_ref[...] = row_sum_of_transpose(total)
+    strips = []
+    for row in range(0, p_ref.shape[1], 64):
+        total = p_ref[0, row : row + 64].astype(F32) * u[:1]
+        for j in range(1, HALF):
+            total += p_ref[j, row : row + 64].astype(F32) * u[j : j + 1]
+        strips.append(total)
+    v_ref[...] = row_sum_of_transpose(jnp.concatenate(strips, axis=0))
 
 
 def make_values(width, probs, own, got, ss):

time: 87.5 us -> 87.5 us (level)
  no operation moved by 1% of the time
where the time goes in v9:
time: 87.5 us; the launch traced here: 87.1 us
  blocking collectives  43.1 us (49%)
  waiting for transfers between devices  15.7 us (18%)
  starting transfers between devices  14.5 us (17%)
  Pallas kernels  12.2 us (14%)
    all_to_all x1, blocking collectives, shards(): v = lax.all_to_all(v.reshape(32, HALF, 128), PLANE, 0, 0).reshape(512, 128)  20.7 us
    all_to_all x1, blocking collectives, shards(): z = lax.all_to_all(z, PLANE, 0, 0)  14.2 us
    all_to_all x1, blocking collectives, shards(): tails = lax.all_to_all(tails, NEAR, 0, 0)  8.26 us
    ppermute x6, waiting for transfers between devices, swap(): return lax.ppermute(v, axis, [(0, 1), (1, 0)])  8.1 us
    pallas_call x12, Pallas kernels, whole(): pl.pallas_call(body, in_specs=[VMEM] * len(args), out_specs=[VMEM] * len(...  7.73 us
    all_to_all x1, waiting for transfers between devices, shards(): tails = lax.all_to_all(tails, PLANE, 0, 0)  7.59 us
    ppermute x6, starting transfers between devices, swap(): return lax.ppermute(v, axis, [(0, 1), (1, 0)])  5.52 us
    all_to_all x1, starting transfers between devices, shards(): tails = lax.all_to_all(tails, PLANE, 0, 0)  4.35 us
  transfers between devices with their start and end apart: 9, of which 6 were waited for; matrix products, arithmetic and copies ran while one was open for 0% of the time, Pallas kernels for 9%

profile of v9, /device:TPU:32, one launch (start us, length us, event | category | flops | bytes accessed | tf_op | source)
XLA Modules:
  0.0 87.1 jit_solution(11289077029642863987)
XLA Ops:
  0.6 3.3 %collective-permute-start = (bf16[64,256]{1,0:T(8,128)(2,1)}, bf16[64,256]{1,0:T(8,128)(2,1)S(1)}, u32[]{:S(2)}, u32[]{:S(2)}) collective-permute-start(bf16[64,256]{1,0:T(8,128)(2,1)} %param.10), channel_id=1, source_target_pairs={{1,0},{0,128},{128,129},{129,1},{3,2},{2,130},{130,131},{131,3},{5... | collective-permute-start | bytes 98312 | tf_op jit(solution)/shard_map/ppermute | solution.py:411
  3.9 1.4 %collective-permute-start.1 = (bf16[64,256]{1,0:T(8,128)(2,1)}, bf16[64,256]{1,0:T(8,128)(2,1)S(1)}, u32[]{:S(2)}, u32[]{:S(2)}) collective-permute-start(bf16[64,256]{1,0:T(8,128)(2,1)} %param.10), channel_id=1, source_target_pairs={{0,0},{1,128},{128,1},{129,129},{2,2},{3,130},{130,3},{131,131},{4... | collective-permute-start | bytes 98312 | tf_op jit(solution)/shard_map/ppermute | solution.py:34
  5.3 1.8 %collective-permute-start.2 = (f32[16,128]{1,0:T(8,128)}, f32[16,128]{1,0:T(8,128)S(1)}, u32[]{:S(2)}, u32[]{:S(2)}) collective-permute-start(f32[16,128]{1,0:T(8,128)} %bitcast.14), channel_id=1, source_target_pairs={{0,1},{1,0},{2,3},{3,2},{4,5},{5,4},{6,7},{7,6},{8,9},{9,8},{10,11... | collective-permute-start | bytes 24584 | tf_op jit(solution)/shard_map/ppermute | solution.py:30
  7.1 0.0 copy-start.2
  7.1 0.7 copy-done.2
  7.8 0.0 copy-start.3
  7.8 1.8 %shard_map.127 = (bf16[256,4096]{1,0:T(8,128)(2,1)S(1)}, f32[1,256]{1,0:T(1,128)S(1)}) custom-call(bf16[256,4096]{1,0:T(8,128)(2,1)} %x_ref.1, bf16[4096]{0:T(1024)(128)(2,1)S(1)} %copy-done.2), custom_call_target="tpu_custom_call" | custom-call | tf_op jit(solution)/shard_map/pallas_call | solution.py:119
  9.6 0.0 collective-permute-done.ring_ref
  9.6 0.0 collective-permute-done.1.swap_ref
  9.6 0.0 copy-done.3
  9.6 0.2 shard_map.128
  9.8 0.0 collective-permute-done.2.r_ref
  9.8 0.2 shard_map.129
  10.1 20.7 %all_to_all.20 = bf16[32,16,128]{2,1,0:T(8,128)(2,1)S(1)} all-to-all(bf16[32,16,128]{2,1,0:T(8,128)(2,1)S(1)} %bitcast.13), channel_id=1, replica_groups=mesh['yh'=2,'x'=4,'core'=2,'z'=8,'yl'=2] {'x','z'}, dimensions={0} | all-to-all | bytes 262144 | tf_op jit(solution)/shard_map/all_to_all | solution.py:420
  30.7 0.0 collective-permute-start.3
  30.7 0.0 copy-start
  30.8 0.0 copy-start.1
  30.8 0.4 shard_map.130
  31.2 0.9 %collective-permute-done.3.v_ref = bf16[512,128]{1,0:T(8,128)(2,1)S(1)} collective-permute-done((bf16[512,128]{1,0:T(8,128)(2,1)S(1)}, bf16[512,128]{1,0:T(8,128)(2,1)S(1)}, u32[]{:S(2)}, u32[]{:S(2)}) %collective-permute-start.3) | collective-permute-done | bytes 131104 | tf_op jit(solution)/shard_map/ppermute | solution.py:30
  32.1 0.4 shard_map.131
  32.5 1.2 %collective-permute-start.4 = (f32[24,256]{1,0:T(8,128)S(1)}, f32[24,256]{1,0:T(8,128)S(1)}, u32[]{:S(2)}, u32[]{:S(2)}) collective-permute-start(f32[24,256]{1,0:T(8,128)S(1)} %get-tuple-element.52), channel_id=1, source_target_pairs={{0,1},{1,0},{2,3},{3,2},{4,5},{5,4},{6,7},{7,6},{8,9},{9,8},{10,11... | collective-permute-start | bytes 73736 | tf_op jit(solution)/shard_map/ppermute | solution.py:30
  33.8 0.0 copy-done
  33.8 0.0 copy-done.1
  33.8 0.0 copy-start.4
  33.8 0.0 copy-start.5
  33.8 1.9 %shard_map.132.refs_0_.p_ref = bf16[16,256,256]{2,1,0:T(8,128)(2,1)S(1)} custom-call(bf16[256,2048]{1,0:T(8,128)(2,1)S(1)} %copy-done, bf16[256,256]{1,0:T(8,128)(2,1)S(1)} %copy-done.1, f32[16,256]{1,0:T(8,128)S(1)} %get-tuple-element.51.after_ref.refs_1_), custom_call_target="tpu_custom_call" | custom-call | tf_op jit(solution)/shard_map/pallas_call | solution.py:46
  35.7 0.8 collective-permute-done.4.refs_2_
  36.4 0.6 shard_map.133
  37.0 1.2 %collective-permute-start.5 = (f32[1,256]{1,0:T(1,128)S(1)}, f32[1,256]{1,0:T(1,128)S(1)}, u32[]{:S(2)}, u32[]{:S(2)}) collective-permute-start(f32[1,256]{1,0:T(1,128)S(1)} %get-tuple-element.54.own_ref), channel_id=1, source_target_pairs={{0,1},{1,0},{2,3},{3,2},{4,5},{5,4},{6,7},{7,6},{8,9},{9,8},{10,11... | collective-permute-start | bytes 3080 | tf_op jit(solution)/shard_map/ppermute | solution.py:30
  38.2 2.4 %collective-permute-done.5.got_ref = f32[1,256]{1,0:T(1,128)S(1)} collective-permute-done((f32[1,256]{1,0:T(1,128)S(1)}, f32[1,256]{1,0:T(1,128)S(1)}, u32[]{:S(2)}, u32[]{:S(2)}) %collective-permute-start.5) | collective-permute-done | bytes 1056 | tf_op jit(solution)/shard_map/ppermute | solution.py:30
  40.6 0.0 copy-done.4
  40.7 0.0 copy-done.5
  40.7 0.8 shard_map.134
  41.5 1.1 %collective-permute-start.6 = (f32[24,256]{1,0:T(8,128)S(1)}, f32[24,256]{1,0:T(8,128)S(1)}, u32[]{:S(2)}, u32[]{:S(2)}) collective-permute-start(f32[24,256]{1,0:T(8,128)S(1)} %get-tuple-element.58.own_ref), channel_id=1, source_target_pairs={{0,1},{1,0},{2,3},{3,2},{4,5},{5,4},{6,7},{7,6},{8,9},{9,8},{10,11... | collective-permute-start | bytes 73736 | tf_op jit(solution)/shard_map/ppermute | solution.py:30
  42.6 2.7 %collective-permute-done.6.got_ref = f32[24,256]{1,0:T(8,128)S(1)} collective-permute-done((f32[24,256]{1,0:T(8,128)S(1)}, f32[24,256]{1,0:T(8,128)S(1)}, u32[]{:S(2)}, u32[]{:S(2)}) %collective-permute-start.6) | collective-permute-done | bytes 24608 | tf_op jit(solution)/shard_map/ppermute | solution.py:30
  45.3 0.6 shard_map.135
  45.9 0.1 collective-permute-start.7
  46.0 1.3 %collective-permute-done.7 = bf16[512,128]{1,0:T(8,128)(2,1)S(1)} collective-permute-done((bf16[512,128]{1,0:T(8,128)(2,1)S(1)}, bf16[512,128]{1,0:T(8,128)(2,1)S(1)}, u32[]{:S(2)}, u32[]{:S(2)}) %collective-permute-start.7) | collective-permute-done | bytes 131104 | tf_op jit(solution)/shard_map/ppermute | solution.py:30
  47.3 14.2 %all_to_all.21.refs_6_.parts_ref = bf16[32,16,128]{2,1,0:T(8,128)(2,1)S(1)} all-to-all(bf16[32,16,128]{2,1,0:T(8,128)(2,1)S(1)} %bitcast.19), channel_id=1, replica_groups=mesh['yh'=2,'x'=4,'core'=2,'z'=8,'yl'=2] {'x','z'}, dimensions={0} | all-to-all | bytes 262144 | tf_op jit(solution)/shard_map/all_to_all | solution.py:430
  61.5 0.3 shard_map.137
  61.8 8.3 %all_to_all.22.tails_ref = bf16[8,32,128]{2,1,0:T(8,128)(2,1)S(1)} all-to-all(bf16[8,32,128]{2,1,0:T(8,128)(2,1)S(1)} %shard_map.137), channel_id=1, replica_groups=mesh['yh'=2,'x'=4,'core'=2,'z'=8,'yl'=2] {'yh','core','yl'}, dimensions={0} | all-to-all | bytes 131072 | tf_op jit(solution)/shard_map/all_to_all | solution.py:433
  70.1 0.7 shard_map.138
  70.8 4.4 %all-to-all-start.3 = ((bf16[32,24,128]{2,1,0:T(8,128)(2,1)}), bf16[32,24,128]{2,1,0:T(8,128)(2,1)S(1)}, u32[]{:S(2)}, u32[]{:S(2)}) async-start(bf16[32,24,128]{2,1,0:T(8,128)(2,1)} %get-tuple-element.68), calls=%async_computation.3 | async-start | bytes 393216 | tf_op jit(solution)/shard_map/all_to_all | solution.py:436
  75.1 2.7 %shard_map.136 = (bf16[256,4096]{1,0:T(8,128)(2,1)}, f32[1,256]{1,0:T(1,128)}) custom-call(f32[32,256]{1,0:T(8,128)S(1)} %get-tuple-element.60.refs_0_, f32[1,256]{1,0:T(1,128)S(1)} %get-tuple-element.61.refs_1_, f32[1,256]{1,0:T(1,128)S(1)} %get-tuple-element.59.rms_ref.refs_2_, bf16[32,2048]{1,0:T(8,128)(2,1)S(1)} %get-tuple-element.62.refs_3_, ...), custom_call_target="tpu_custom_call" | custom-call | tf_op jit(solution)/shard_map/pallas_call | solution.py:382
  77.9 0.9 %shard_map.139 = f32[64,256]{1,0:T(8,128)} custom-call(f32[8,128]{1,0:T(8,128)S(1)} %get-tuple-element.67.z_ref, f32[16,128]{1,0:T(8,128)S(1)} %bitcast.16), custom_call_target="tpu_custom_call" | custom-call | tf_op jit(solution)/shard_map/pallas_call | solution.py:46
  78.8 7.6 %all-to-all-done.3.all_ref = bf16[32,24,128]{2,1,0:T(8,128)(2,1)S(1)} async-done(((bf16[32,24,128]{2,1,0:T(8,128)(2,1)}), bf16[32,24,128]{2,1,0:T(8,128)(2,1)S(1)}, u32[]{:S(2)}, u32[]{:S(2)}) %all-to-all-start.3) | async-done | bytes 196640 | tf_op jit(solution)/shard_map/all_to_all | solution.py:436
  86.4 0.7 shard_map.140
  (2 shorter events, 0.0 us)
Async XLA Ops:
  0.6 9.0 %collective-permute-start = (bf16[64,256]{1,0:T(8,128)(2,1)}, bf16[64,256]{1,0:T(8,128)(2,1)S(1)}, u32[]{:S(2)}, u32[]{:S(2)}) collective-permute-start(bf16[64,256]{1,0:T(8,128)(2,1)} %param.10), channel_id=1, source_target_pairs={{1,0},{0,128},{128,129},{129,1},{3,2},{2,130},{130,131},{131,3},{5... | collective-permute-start | bytes 98312 | tf_op jit(solution)/shard_map/ppermute | solution.py:411
  3.9 5.7 %collective-permute-start.1 = (bf16[64,256]{1,0:T(8,128)(2,1)}, bf16[64,256]{1,0:T(8,128)(2,1)S(1)}, u32[]{:S(2)}, u32[]{:S(2)}) collective-permute-start(bf16[64,256]{1,0:T(8,128)(2,1)} %param.10), channel_id=1, source_target_pairs={{0,0},{1,128},{128,1},{129,129},{2,2},{3,130},{130,3},{131,131},{4... | collective-permute-start | bytes 98312 | tf_op jit(solution)/shard_map/ppermute | solution.py:34
  5.3 4.5 %collective-permute-start.2 = (f32[16,128]{1,0:T(8,128)}, f32[16,128]{1,0:T(8,128)S(1)}, u32[]{:S(2)}, u32[]{:S(2)}) collective-permute-start(f32[16,128]{1,0:T(8,128)} %bitcast.14), channel_id=1, source_target_pairs={{0,1},{1,0},{2,3},{3,2},{4,5},{5,4},{6,7},{7,6},{8,9},{9,8},{10,11... | collective-permute-start | bytes 24584 | tf_op jit(solution)/shard_map/ppermute | solution.py:30
  7.1 0.7 copy-start.2
  7.8 1.8 %copy-start.3 = (f32[2048]{0:T(1024)S(1)}, f32[2048]{0:T(1024)}, u32[]{:S(2)}) copy-start(f32[2048]{0:T(1024)} %param.13) | copy-start | bytes 24580
  30.7 1.3 %collective-permute-start.3 = (bf16[512,128]{1,0:T(8,128)(2,1)S(1)}, bf16[512,128]{1,0:T(8,128)(2,1)S(1)}, u32[]{:S(2)}, u32[]{:S(2)}) collective-permute-start(bf16[512,128]{1,0:T(8,128)(2,1)S(1)} %bitcast.10), channel_id=1, source_target_pairs={{0,16},{16,0},{1,17},{17,1},{2,18},{18,2},{3,19},{19,3},{4,20},{20... | collective-permute-start | bytes 393224 | tf_op jit(solution)/shard_map/ppermute | solution.py:30
  30.7 3.0 %copy-start = (bf16[256,2048]{1,0:T(8,128)(2,1)S(1)}, bf16[256,2048]{1,0:T(8,128)(2,1)}, u32[]{:S(2)}) copy-start(bf16[256,2048]{1,0:T(8,128)(2,1)} %q_ref.1) | copy-start | bytes 3145732
  30.8 3.0 %copy-start.1 = (bf16[256,256]{1,0:T(8,128)(2,1)S(1)}, bf16[256,256]{1,0:T(8,128)(2,1)}, u32[]{:S(2)}) copy-start(bf16[256,256]{1,0:T(8,128)(2,1)} %k_ref.1) | copy-start | bytes 393220
  32.5 3.9 %collective-permute-start.4 = (f32[24,256]{1,0:T(8,128)S(1)}, f32[24,256]{1,0:T(8,128)S(1)}, u32[]{:S(2)}, u32[]{:S(2)}) collective-permute-start(f32[24,256]{1,0:T(8,128)S(1)} %get-tuple-element.52), channel_id=1, source_target_pairs={{0,1},{1,0},{2,3},{3,2},{4,5},{5,4},{6,7},{7,6},{8,9},{9,8},{10,11... | collective-permute-start | bytes 73736 | tf_op jit(solution)/shard_map/ppermute | solution.py:30
  33.8 6.9 %copy-start.4 = (f32[256]{0:T(256)S(1)}, f32[256]{0:T(256)}, u32[]{:S(2)}) copy-start(f32[256]{0:T(256)} %param.14) | copy-start | bytes 3076
  33.8 6.9 %copy-start.5 = (s32[256]{0:T(256)S(1)}, s32[256]{0:T(256)}, u32[]{:S(2)}) copy-start(s32[256]{0:T(256)} %param.15) | copy-start | bytes 3076
  37.0 3.7 %collective-permute-start.5 = (f32[1,256]{1,0:T(1,128)S(1)}, f32[1,256]{1,0:T(1,128)S(1)}, u32[]{:S(2)}, u32[]{:S(2)}) collective-permute-start(f32[1,256]{1,0:T(1,128)S(1)} %get-tuple-element.54.own_ref), channel_id=1, source_target_pairs={{0,1},{1,0},{2,3},{3,2},{4,5},{5,4},{6,7},{7,6},{8,9},{9,8},{10,11... | collective-permute-start | bytes 3080 | tf_op jit(solution)/shard_map/ppermute | solution.py:30
  41.5 3.8 %collective-permute-start.6 = (f32[24,256]{1,0:T(8,128)S(1)}, f32[24,256]{1,0:T(8,128)S(1)}, u32[]{:S(2)}, u32[]{:S(2)}) collective-permute-start(f32[24,256]{1,0:T(8,128)S(1)} %get-tuple-element.58.own_ref), channel_id=1, source_target_pairs={{0,1},{1,0},{2,3},{3,2},{4,5},{5,4},{6,7},{7,6},{8,9},{9,8},{10,11... | collective-permute-start | bytes 73736 | tf_op jit(solution)/shard_map/ppermute | solution.py:30
  45.9 1.4 %collective-permute-start.7 = (bf16[512,128]{1,0:T(8,128)(2,1)S(1)}, bf16[512,128]{1,0:T(8,128)(2,1)S(1)}, u32[]{:S(2)}, u32[]{:S(2)}) collective-permute-start(bf16[512,128]{1,0:T(8,128)(2,1)S(1)} %get-tuple-element.65), channel_id=1, source_target_pairs={{0,16},{16,0},{1,17},{17,1},{2,18},{18,2},{3,19},{19,3},{4,20},{20... | collective-permute-start | bytes 393224 | tf_op jit(solution)/shard_map/ppermute | solution.py:30
  70.8 15.6 %all-to-all-start.3 = ((bf16[32,24,128]{2,1,0:T(8,128)(2,1)}), bf16[32,24,128]{2,1,0:T(8,128)(2,1)S(1)}, u32[]{:S(2)}, u32[]{:S(2)}) async-start(bf16[32,24,128]{2,1,0:T(8,128)(2,1)} %get-tuple-element.68), calls=%async_computation.3 | async-start | bytes 393216 | tf_op jit(solution)/shard_map/all_to_all | solution.py:436
